TPU v7x, 512 devices: a whole 4x4x16 slice. The times are simulated.
512 devices in a mesh: dp: 64 (over y, z), tensor: 8 (over x, core).
Axes of the slice: x: 4, y: 4, z: 16, core: 2. Of those that a mesh axis runs over, the one named last changes fastest.
Arguments:
- inputs: bfloat16 [65536, 5120], P(('dp', 'tensor')), may hold values from -6 to 6
- out_grad: bfloat16 [65536, 5120], P(('dp', 'tensor')), may hold values from -6 to 6
- hidden: bfloat16 [65536, 256], P('dp', 'tensor'), may hold values from -0.1875 to 0.1875
- up_grad: bfloat16 [65536, 256], P('dp', 'tensor'), may hold values from -0.1875 to 0.1875
- gate_grad: bfloat16 [65536, 256], P('dp', 'tensor'), may hold values from -0.1875 to 0.1875
- error_memory: bfloat16 [64, 3, 256, 5120], P('dp', None, 'tensor'), may hold values from -3 to 3
- q_start: bfloat16 [3, 32, 5120], replicated, may hold values from -0.078125 to 0.078125
Outputs:
- error_next: bfloat16 [64, 3, 256, 5120], P('dp', None, 'tensor')
- p_factor: float32 [3, 256, 32], P(None, 'tensor')
- q_factor: bfloat16 [3, 32, 5120], replicated
All inputs are finite; a program needn't handle non-finite values.
Results may differ from a plain program's by a relative error of at most 0.0016.
Values may be sent and summed in bfloat16 or wider, within the bound.
No kernel may reach another device: no remote copies, remote signals or barrier semaphores. Data moves between devices by JAX's collectives and lax.ppermute only.
A program may use at most 128 MiB of HBM per device.

v0:
```python
import jax
import jax.numpy as jnp
from jax import lax
from jax.sharding import PartitionSpec as P

PRECISE = lax.Precision.HIGHEST


def orthonormal(p_rows, gram_matrix):
    factor = jnp.linalg.cholesky(gram_matrix)
    solved = jax.scipy.linalg.solve_triangular(factor, p_rows.T, lower=True)
    return solved.T


def per_device(inputs, out_grad, hidden, up_grad, gate_grad, error_memory, q_start):
    row_count = hidden.shape[1]
    model_width = inputs.shape[1]
    branch_grads = jnp.concatenate([up_grad, gate_grad], axis=1)
    branch_term = jnp.dot(
        branch_grads.T,
        lax.all_gather(inputs, "tensor", axis=0, tiled=True),
        preferred_element_type=jnp.float32,
    )
    down_term = jnp.dot(
        hidden.T,
        lax.all_gather(out_grad, "tensor", axis=0, tiled=True),
        preferred_element_type=jnp.float32,
    )
    matrices = jnp.concatenate([branch_term, down_term], axis=0).reshape(3, row_count, model_width)
    matrices = matrices + error_memory[0].astype(jnp.float32)
    q_float = q_start.astype(jnp.float32)
    p_part = jnp.einsum("mfd,mrd->mfr", matrices, q_float, precision=PRECISE)
    p_local = lax.psum(p_part, "dp")
    gram_part = jnp.einsum("mfr,mfs->mrs", p_local, p_local, precision=PRECISE)
    gram_matrix = lax.psum(gram_part, "tensor")
    p_factor = jax.vmap(orthonormal)(p_local, gram_matrix)
    q_part = jnp.einsum("mfr,mfd->mrd", p_factor, matrices, precision=PRECISE)
    q_sum = lax.psum(q_part, ("dp", "tensor"))
    q_factor = (q_sum / lax.axis_size("dp")).astype(jnp.bfloat16)
    q_used = lax.optimization_barrier(q_factor).astype(jnp.float32)
    rebuilt = jnp.einsum("mfr,mrd->mfd", p_factor, q_used, precision=PRECISE)
    error_next = (matrices - rebuilt).astype(jnp.bfloat16)[None]
    return (error_next, p_factor, q_factor)


def solution(mesh):
    in_specs = (
        P(("dp", "tensor"), None),
        P(("dp", "tensor"), None),
        P("dp", "tensor"),
        P("dp", "tensor"),
        P("dp", "tensor"),
        P("dp", None, "tensor", None),
        P(),
    )
    out_specs = (P("dp", None, "tensor", None), P(None, "tensor", None), P())
    return jax.shard_map(
        per_device, mesh=mesh, in_specs=in_specs, out_specs=out_specs, check_vma=False
    )
```

profile of v0, /device:TPU:1, one launch (start us, length us, event | category | flops | bytes accessed | tf_op | source)
XLA Modules:
  0.0 956.0 jit_solution(10964999595906917111)
XLA Ops:
  7.2 0.0 copy-start
  7.2 0.0 copy-start.5
  7.2 0.0 all-gather.5.cloned.1.call-start
  7.2 0.7 all-gather.5.cloned.1.call-update
  7.9 0.0 all-gather.3.cloned.1.call-start
  8.0 0.7 all-gather.3.cloned.1.call-update
  8.7 0.0 all-reduce.2.cloned.1.call-start
  8.7 0.0 copy-start.6
  8.8 0.0 copy-start.7
  8.8 73.3 %all-gather.5.cloned.1.call-done = bf16[1024,5120]{1,0:T(8,128)(2,1)} async-done(((bf16[128,5120]{1,0:T(8,128)(2,1)}), bf16[1024,5120]{1,0:T(8,128)(2,1)}) %all-gather.5.cloned.1.call-update) | async-done | bytes 10485776 | tf_op jit(solution)/shard_map/all_gather | solution.py:26
  82.1 0.0 copy-done.5
  82.1 6.7 fusion.12
  88.8 62.0 %all-gather.3.cloned.1.call-done = bf16[1024,5120]{1,0:T(8,128)(2,1)} async-done(((bf16[128,5120]{1,0:T(8,128)(2,1)}), bf16[1024,5120]{1,0:T(8,128)(2,1)}) %all-gather.3.cloned.1.call-update) | async-done | bytes 10485776 | tf_op jit(solution)/shard_map/all_gather | solution.py:21
  150.8 0.0 copy-done.6
  150.8 0.0 copy-done.7
  150.8 0.0 copy-start.4
  150.8 6.0 fusion.4
  156.8 0.0 copy-done.4
  156.8 0.0 copy-start.1
  156.8 0.1 pad_maximum_fusion
  156.9 0.0 copy-done
  156.9 1.0 copy-done.1
  158.0 1.2 fusion.3
  159.2 225.5 %psum.21 = f32[3,32,32]{2,1,0:T(8,128)S(1)} all-reduce(f32[3,32,32]{2,1,0:T(8,128)S(1)} %fusion.3), channel_id=1, replica_groups=mesh['dp'=64,'tensor'=8] {'dp'}, use_global_device_ids=true, to_apply=%region_0.0 | all-reduce | flops 3072 | bytes 24576 | tf_op jit(solution)/shard_map/psum | solution.py:33
  384.6 0.3 fusion.13
  384.9 75.7 %psum.22 = f32[3,32,32]{1,2,0:T(8,128)S(1)} all-reduce(f32[3,32,32]{1,2,0:T(8,128)S(1)} %fusion.13), channel_id=1, replica_groups=mesh['dp'=64,'tensor'=8] {'tensor'}, use_global_device_ids=true, to_apply=%region_1.0 | all-reduce | flops 3072 | bytes 24576 | tf_op jit(solution)/shard_map/psum | solution.py:35
  460.6 0.1 copy.18
  460.7 8.8 custom-call.8
  469.6 0.1 compare_reduce_fusion
  469.7 0.1 select_bitcast_fusion
  469.8 7.4 custom-call.9
  477.1 0.3 fusion.8
  477.4 4.2 fusion.2
  481.6 0.0 all-reduce.2.cloned.1.call-update
  481.7 0.7 copy.21
  482.4 463.3 %all-reduce.2.cloned.1.call-done = f32[3,32,5120]{2,1,0:T(8,128)} async-done(((f32[3,32,5120]{2,1,0:T(8,128)}), f32[3,32,5120]{2,1,0:T(8,128)}) %all-reduce.2.cloned.1.call-update) | async-done | bytes 1966096 | tf_op jit(solution)/shard_map/psum | solution.py:38
  945.7 0.0 copy-start.2
  945.7 1.7 multiply_convert_fusion
  947.4 0.0 copy-done.2
  947.4 0.0 copy-start.3
  947.4 2.0 fusion.1
  949.5 0.0 copy-done.3
  (4 shorter events, 0.1 us)
Async XLA Ops:
  7.2 149.8 %copy-start = (bf16[3,32,5120]{2,1,0:T(8,128)(2,1)S(1)}, bf16[3,32,5120]{2,1,0:T(8,128)(2,1)}, u32[]{:S(2)}) copy-start(bf16[3,32,5120]{2,1,0:T(8,128)(2,1)} %param.13) | copy-start | bytes 2949124
  7.2 74.9 %copy-start.5 = (bf16[1024,32]{0,1:T(8,128)(2,1)S(1)}, bf16[1024,32]{0,1:T(8,128)(2,1)}, u32[]{:S(2)}) copy-start(bf16[1024,32]{0,1:T(8,128)(2,1)} %param.9) | copy-start | bytes 196612
  7.2 74.9 %all-gather.5.cloned.1.call-start = ((), (), s32[]{:S(2)}) async-start(), calls=%async_computation.1 | async-start | bytes 11796480 | tf_op jit(solution)/shard_map/all_gather | solution.py:26
  7.9 142.9 %all-gather.3.cloned.1.call-start = ((), (), s32[]{:S(2)}) async-start(), calls=%async_computation | async-start | bytes 11796480 | tf_op jit(solution)/shard_map/all_gather | solution.py:21
  8.7 937.0 %all-reduce.2.cloned.1.call-start = ((), (), s32[]{:S(2)}) async-start(), calls=%async_computation.2 | async-start | bytes 3932160 | tf_op jit(solution)/shard_map/psum | solution.py:38
  8.7 142.0 %copy-start.6 = (bf16[1024,32]{0,1:T(8,128)(2,1)S(1)}, bf16[1024,32]{0,1:T(8,128)(2,1)}, u32[]{:S(2)}) copy-start(bf16[1024,32]{0,1:T(8,128)(2,1)} %param.11) | copy-start | bytes 196612
  8.8 142.0 %copy-start.7 = (bf16[1024,32]{0,1:T(8,128)(2,1)S(1)}, bf16[1024,32]{0,1:T(8,128)(2,1)}, u32[]{:S(2)}) copy-start(bf16[1024,32]{0,1:T(8,128)(2,1)} %param.10) | copy-start | bytes 196612
  150.8 6.0 copy-start.4
  156.8 1.2 copy-start.1
  945.7 1.8 copy-start.2
  947.4 2.0 copy-start.3
Sparse Core Ops, SparseCore 0:
  10.1 71.8 all-gather.4
  84.2 66.5 all-gather.2
  481.8 463.8 all-reduce.1
where the time goes:
time: 957 us; the launch traced here: 956 us
  waiting for transfers between devices  600 us (63%)
  blocking collectives  301 us (31%)
  matrix products  20.6 us (2%)
  other arithmetic  18.3 us (2%)
  between operations  13.9 us (1%)
    psum x1, waiting for transfers between devices, per_device(): q_sum = lax.psum(q_part, ('dp', 'tensor'))  463 us
    psum x1, blocking collectives, per_device(): p_local = lax.psum(p_part, 'dp')  225 us
    psum x1, blocking collectives, per_device(): gram_matrix = lax.psum(gram_part, 'tensor')  75.7 us
    all_gather x1, waiting for transfers between devices, per_device(): lax.all_gather(out_grad, 'tensor', axis=0, tiled=True)  73.3 us
    all_gather x1, waiting for transfers between devices, per_device(): lax.all_gather(inputs, 'tensor', axis=0, tiled=True)  62 us
  transfers between devices with their start and end apart: 3, of which 3 were waited for; matrix products, arithmetic and copies ran while one was open for 1% of the time, Pallas kernels for 0%

commit v1 on v0

v1 whole, which is shorter than its diff:
```python
import jax
import jax.numpy as jnp
from jax import lax
from jax.sharding import Mesh, PartitionSpec as P

PRECISE = lax.Precision.HIGHEST
NY, NZ, NX, NC = 4, 16, 4, 2


def spread(value, axis, count):
    copies = jnp.broadcast_to(value[None], (count,) + value.shape)
    return lax.all_to_all(copies, axis, 0, 0)


def swap_core(value):
    return lax.ppermute(value, "c", [(0, 1), (1, 0)])


def sum_tensor(value):
    value = value + swap_core(value)
    value = value + lax.ppermute(value, "x", [(i, i ^ 1) for i in range(NX)])
    return value + lax.ppermute(value, "x", [(i, i ^ 2) for i in range(NX)])


def inverse_factor(gram_matrix):
    factor = jnp.linalg.cholesky(gram_matrix)
    unit = jnp.eye(gram_matrix.shape[0], dtype=jnp.float32)
    return jax.scipy.linalg.solve_triangular(factor, unit, lower=True)


def per_device(inputs, out_grad, hidden, up_grad, gate_grad, error_memory, q_start):
    row_count = hidden.shape[1]
    width = inputs.shape[1]
    rank = q_start.shape[1]
    core = lax.axis_index("c")
    branch_grads = jnp.concatenate([up_grad, gate_grad], axis=1)
    branch_term = jnp.dot(
        branch_grads.T,
        lax.all_gather(inputs, ("x", "c"), axis=0, tiled=True),
        preferred_element_type=jnp.float32,
    )
    down_term = jnp.dot(
        hidden.T,
        lax.all_gather(out_grad, ("x", "c"), axis=0, tiled=True),
        preferred_element_type=jnp.float32,
    )
    matrices = jnp.concatenate([branch_term, down_term], axis=0).reshape(3, row_count, width)
    matrices = matrices + error_memory[0].astype(jnp.float32)
    q_float = q_start.astype(jnp.float32)
    p_part = jnp.einsum("mfd,mrd->mfr", matrices, q_float, precision=PRECISE)
    p_flat = p_part.reshape(24, 128)
    p_flat = spread(p_flat, "z", NZ).sum(0)
    p_flat = spread(p_flat, "y", NY).sum(0)
    p_local = p_flat.reshape(3, row_count, rank)

    gram_part = jnp.einsum("mfr,mfs->mrs", p_local, p_local, precision=PRECISE)
    inverse = jax.vmap(inverse_factor)(sum_tensor(gram_part))

    half = width // NC
    blocks = half // NX // 128
    w_part = jnp.einsum("mfr,mfd->mrd", p_local, matrices, precision=PRECISE)
    mine = lax.dynamic_slice_in_dim(w_part, core * half, half, axis=2)
    theirs = lax.dynamic_slice_in_dim(w_part, (1 - core) * half, half, axis=2)
    w_core = mine + swap_core(theirs)
    w_core = w_core.reshape(3, rank, NX, blocks, 128).transpose(2, 0, 3, 1, 4)
    w_x = lax.all_to_all(w_core.reshape(NX, 3 * blocks * rank, 128), "x", 0, 0).sum(0)
    w_x = jnp.pad(w_x, ((0, rank), (0, 0))).reshape(NY, 4 * rank, 128)
    w_y = lax.all_to_all(w_x, "y", 0, 0).sum(0).reshape(4, rank, 128)
    unit_of = jnp.minimum((lax.axis_index("y") * 4 + jnp.arange(4)) // blocks, 2)
    q_y = jnp.einsum("urs,usd->urd", inverse[unit_of], w_y, precision=PRECISE)
    q_z = lax.all_to_all(q_y.reshape(NZ, 8, 128), "z", 0, 0).sum(0)
    q_part = (q_z / (NY * NZ)).astype(jnp.bfloat16)

    q_dp = spread(q_part, ("y", "z"), NY * NZ).reshape(NY * NZ * 8, 128)
    q_x = spread(q_dp[: 3 * blocks * rank], "x", NX)
    q_other = swap_core(q_x)
    first = core == 0
    q_all = jnp.stack([jnp.where(first, q_x, q_other), jnp.where(first, q_other, q_x)])
    q_all = q_all.reshape(NC, NX, 3, blocks, rank, 128).transpose(2, 4, 0, 1, 3, 5)
    q_factor = q_all.reshape(3, rank, width)

    p_factor = jnp.einsum("mfr,msr->mfs", p_local, inverse, precision=PRECISE)
    q_used = lax.optimization_barrier(q_factor).astype(jnp.float32)
    rebuilt = jnp.einsum("mfr,mrd->mfd", p_factor, q_used, precision=PRECISE)
    error_next = (matrices - rebuilt).astype(jnp.bfloat16)[None]
    return (error_next, p_factor, q_factor)


def solution(mesh):
    fine = Mesh(mesh.devices.reshape(NY, NZ, NX, NC), ("y", "z", "x", "c"))
    dp, tensor = ("y", "z"), ("x", "c")
    in_specs = (
        P(dp + tensor, None),
        P(dp + tensor, None),
        P(dp, tensor),
        P(dp, tensor),
        P(dp, tensor),
        P(dp, None, tensor, None),
        P(),
    )
    out_specs = (P(dp, None, tensor, None), P(None, tensor, None), P())
    return jax.shard_map(
        per_device, mesh=fine, in_specs=in_specs, out_specs=out_specs, check_vma=False
    )
```

time: 957 us -> 332 us (0.35)
  waiting for transfers between devices: 600 us -> 150 us
  blocking collectives: 301 us -> 71.1 us
  starting transfers between devices: 0.11 us -> 35.3 us
  local copies, waits for them, and re-layouts: 1.9 us -> 16.5 us
    psum x1 -> x0, waiting for transfers between devices: 463 us -> none  [per_device(): q_sum = lax.psum(q_part, ('dp', 'tensor'))]
    psum x2 -> x0, blocking collectives: 301 us -> none  [the longest x1 225 us: per_device(): p_local = lax.psum(p_part, 'dp')]
    all_to_all x0 -> x4, blocking collectives: none -> 71.1 us  [the longest x3 53.9 us: spread(): return lax.all_to_all(copies, axis, 0, 0)]
    ppermute x0 -> x5, starting transfers between devices: none -> 23.6 us  [the longest x3 17.5 us: swap_core(): return lax.ppermute(value, 'c', [(0, 1), (1, 0)])]
    all_to_all x0 -> x3, starting transfers between devices: none -> 11.6 us  [the longest x1 4.22 us: per_device(): lax.all_to_all(w_core.reshape(NX, 3 * blocks * rank, 128), 'x', 0, 0).sum(0)]
  transfers between devices with their start and end apart: 3 -> 10, of which waited for: 3 -> 7; matrix products, arithmetic and copies ran while one was open for 1% -> 10% of each run, Pallas kernels for 0% -> 0%
where the time goes in v1:
time: 332 us; the launch traced here: 331 us
  waiting for transfers between devices  150 us (45%)
  blocking collectives  71.1 us (21%)
  starting transfers between devices  35.3 us (11%)
  matrix products  21.8 us (7%)
  other arithmetic  21.7 us (7%)
  local copies, waits for them, and re-layouts  16.5 us (5%)
  between operations  14.4 us (4%)
    all_gather x1, waiting for transfers between devices, per_device(): lax.all_gather(out_grad, ('x', 'c'), axis=0, tiled=True)  73.4 us
    all_gather x1, waiting for transfers between devices, per_device(): lax.all_gather(inputs, ('x', 'c'), axis=0, tiled=True)  62 us
    all_to_all x3, blocking collectives, spread(): return lax.all_to_all(copies, axis, 0, 0)  53.9 us
    ppermute x3, starting transfers between devices, swap_core(): return lax.ppermute(value, 'c', [(0, 1), (1, 0)])  17.5 us
    all_to_all x1, blocking collectives, per_device(): q_z = lax.all_to_all(q_y.reshape(NZ, 8, 128), 'z', 0, 0).sum(0)  17.1 us
    another operation x4, other arithmetic, inverse_factor(): factor = jnp.linalg.cholesky(gram_matrix)  8.96 us
    another operation x3, other arithmetic, inverse_factor(): return jax.scipy.linalg.solve_triangular(factor, unit, lower=True)  7.46 us
    dot_general x1, matrix products, per_device(): jnp.dot(hidden.T, lax.all_gather(out_grad, ('x', 'c'), axis=0, tiled=True...  6.72 us
  transfers between devices with their start and end apart: 10, of which 7 were waited for; matrix products, arithmetic and copies ran while one was open for 10% of the time, Pallas kernels for 0%

profile of v1, /device:TPU:1, one launch (start us, length us, event | category | flops | bytes accessed | tf_op | source)
XLA Modules:
  0.0 330.7 jit_solution(8749247432261391317)
XLA Ops:
  7.2 0.0 copy-start
  7.2 0.0 copy-start.5
  7.2 0.0 all-gather.5.cloned.1.call-start
  7.2 0.7 all-gather.5.cloned.1.call-update
  7.9 0.0 all-gather.3.cloned.1.call-start
  8.0 0.7 all-gather.3.cloned.1.call-update
  8.7 73.4 %all-gather.5.cloned.1.call-done = bf16[1024,5120]{1,0:T(8,128)(2,1)} async-done(((bf16[128,5120]{1,0:T(8,128)(2,1)}), bf16[1024,5120]{1,0:T(8,128)(2,1)}) %all-gather.5.cloned.1.call-update) | async-done | bytes 10485776 | tf_op jit(solution)/shard_map/all_gather | solution.py:44
  82.1 6.7 %fusion.15 = f32[32,5120]{1,0:T(8,128)} fusion(bf16[1024,32]{0,1:T(8,128)(2,1)S(1)} %copy-done.5, bf16[1024,5120]{1,0:T(8,128)(2,1)} %all-gather.5.cloned.1.call-done), kind=kOutput, calls=%fused_computation.35 | convolution fusion | flops 335544320 | bytes 11206656 | tf_op jit(solution)/shard_map/dot_general | solution.py:42
  88.8 62.0 %all-gather.3.cloned.1.call-done = bf16[1024,5120]{1,0:T(8,128)(2,1)} async-done(((bf16[128,5120]{1,0:T(8,128)(2,1)}), bf16[1024,5120]{1,0:T(8,128)(2,1)}) %all-gather.3.cloned.1.call-update) | async-done | bytes 10485776 | tf_op jit(solution)/shard_map/all_gather | solution.py:39
  150.8 6.0 %fusion.4 = f32[64,5120]{1,0:T(8,128)S(1)} fusion(bf16[1024,5120]{1,0:T(8,128)(2,1)} %all-gather.3.cloned.1.call-done, bf16[1024,32]{0,1:T(8,128)(2,1)S(1)} %copy-done.6, bf16[1024,32]{0,1:T(8,128)(2,1)S(1)} %copy-done.7), kind=kOutput, calls=%fused_computation.12 | convolution fusion | flops 671350784 | bytes 11927552 | tf_op jit(solution)/shard_map/dot_general | solution.py:37
  156.8 0.0 copy-done.3
  156.8 0.0 copy-start.1
  156.8 0.1 pad_maximum_fusion
  156.9 1.0 copy-done.1
  158.0 1.2 fusion.3
  159.2 0.1 broadcast_in_dim.22
  159.3 24.9 %all_to_all.35 = f32[16,24,128]{2,1,0:T(8,128)S(1)} all-to-all(f32[16,24,128]{2,1,0:T(8,128)S(1)} %broadcast_in_dim.40), channel_id=1, replica_groups=mesh['y'=4,'z'=16,'x'=4,'c'=2] {'z'}, dimensions={0} | all-to-all | bytes 393216 | tf_op jit(solution)/shard_map/all_to_all | solution.py:12
  184.2 0.6 broadcast_in_dim.41
  184.8 4.0 %all-to-all-start.1 = ((f32[4,24,128]{2,1,0:T(8,128)}), f32[4,24,128]{2,1,0:T(8,128)S(1)}, u32[]{:S(2)}, u32[]{:S(2)}) async-start(f32[4,24,128]{2,1,0:T(8,128)} %broadcast_in_dim.41), calls=%async_computation.1 | async-start | bytes 98304 | tf_op jit(solution)/shard_map/all_to_all | solution.py:12
  188.8 4.4 %all-to-all-done.1 = f32[4,24,128]{2,1,0:T(8,128)S(1)} async-done(((f32[4,24,128]{2,1,0:T(8,128)}), f32[4,24,128]{2,1,0:T(8,128)S(1)}, u32[]{:S(2)}, u32[]{:S(2)}) %all-to-all-start.1) | async-done | bytes 49184 | tf_op jit(solution)/shard_map/all_to_all | solution.py:12
  193.2 0.1 reshape.102
  193.3 3.0 fusion.2
  196.3 0.0 copy-start.2
  196.3 1.3 copy-done.2
  197.6 1.0 constant_dynamic-slice_fusion
  198.6 6.5 %collective-permute-start.3 = (f32[3,32,2560]{2,1,0:T(8,128)}, f32[3,32,2560]{2,1,0:T(8,128)}, u32[]{:S(2)}, u32[]{:S(2)}) collective-permute-start(f32[3,32,2560]{2,1,0:T(8,128)} %constant_dynamic-slice_fusion), channel_id=1, source_target_pairs={{0,1},{1,0},{2,3},{3,2},{4,5},{5,4},{6,7},{7,6},{8,9},{9,8},{10,11... | collective-permute-start | bytes 2949128 | tf_op jit(solution)/shard_map/ppermute | solution.py:16
  205.2 0.3 fusion.16
  205.4 1.9 collective-permute-start
  207.4 1.2 collective-permute-done
  208.6 2.4 collective-permute-start.1
  211.0 2.4 collective-permute-done.1
  213.4 3.6 %collective-permute-start.2 = (f32[3,32,32]{1,2,0:T(8,128)S(1)}, f32[3,32,32]{1,2,0:T(8,128)S(1)}, u32[]{:S(2)}, u32[]{:S(2)}) collective-permute-start(f32[3,32,32]{1,2,0:T(8,128)S(1)} %add.68), channel_id=1, source_target_pairs={{0,4},{2,6},{4,0},{6,2},{1,5},{3,7},{5,1},{7,3},{8,12},{10,14},{12... | collective-permute-start | bytes 36872 | tf_op jit(solution)/shard_map/ppermute | solution.py:22
  217.1 0.0 collective-permute-done.3
  217.1 2.6 dynamic-slice_add_fusion
  219.6 2.7 reshape.103
  222.4 2.9 copy.30
  225.3 4.2 %all-to-all-start.2 = ((f32[4,480,128]{2,1,0:T(8,128)}), f32[4,480,128]{2,1,0:T(8,128)}, u32[]{:S(2)}, u32[]{:S(2)}) async-start(f32[4,480,128]{2,1,0:T(8,128)} %bitcast.49), calls=%async_computation.2 | async-start | bytes 1966080 | tf_op jit(solution)/shard_map/all_to_all | solution.py:66
  229.5 0.0 collective-permute-done.2
  229.6 0.1 copy.27
  229.7 8.8 %custom-call.8 = f32[3,32,32]{2,1,0:T(8,128)S(1)} custom-call(f32[3,32,32]{2,1,0:T(8,128)S(1)} %fusion.10), custom_call_target="Cholesky" | custom-call | tf_op jit(solution)/shard_map/vmap(jit(cholesky))/cholesky | solution.py:26
  238.5 0.1 compare_reduce_fusion
  238.6 0.1 select_bitcast_fusion
  238.7 7.4 %custom-call.9 = f32[3,1,32,32]{2,3,1,0:T(8,128)S(1)} custom-call(f32[3,1,32,32]{3,2,1,0:T(8,128)S(1)} %select_bitcast_fusion), custom_call_target="InvertDiagBlocksLowerTriangular" | custom-call | tf_op jit(solution)/shard_map/vmap(jit(_solve_triangular))/triangular_solve | solution.py:28
  246.1 0.0 all-to-all-done.2
  246.1 1.3 reduce_sum.47
  247.4 0.7 pad.4
  248.1 3.4 %all-to-all-start.3 = ((f32[4,128,128]{2,1,0:T(8,128)}), f32[4,128,128]{2,1,0:T(8,128)S(1)}, u32[]{:S(2)}, u32[]{:S(2)}) async-start(f32[4,128,128]{2,1,0:T(8,128)} %bitcast.52), calls=%async_computation.3 | async-start | bytes 524288 | tf_op jit(solution)/shard_map/all_to_all | solution.py:68
  251.5 0.3 fusion.8
  251.8 0.6 gather_fusion
  252.3 4.7 %all-to-all-done.3 = f32[4,128,128]{2,1,0:T(8,128)S(1)} async-done(((f32[4,128,128]{2,1,0:T(8,128)}), f32[4,128,128]{2,1,0:T(8,128)S(1)}, u32[]{:S(2)}, u32[]{:S(2)}) %all-to-all-start.3) | async-done | bytes 262176 | tf_op jit(solution)/shard_map/all_to_all | solution.py:68
  257.0 0.2 fusion.18
  257.2 17.1 %all_to_all.36 = f32[16,8,128]{2,1,0:T(8,128)S(1)} all-to-all(f32[16,8,128]{2,1,0:T(8,128)S(1)} %bitcast.54), channel_id=1, replica_groups=mesh['y'=4,'z'=16,'x'=4,'c'=2] {'z'}, dimensions={0} | all-to-all | bytes 131072 | tf_op jit(solution)/shard_map/all_to_all | solution.py:71
  274.4 18.4 %all_to_all.37 = bf16[64,8,128]{2,1,0:T(8,128)(2,1)S(1)} all-to-all(bf16[64,8,128]{2,1,0:T(8,128)(2,1)S(1)} %broadcast_in_dim.43), channel_id=1, replica_groups=mesh['y'=4,'z'=16,'x'=4,'c'=2] {'y','z'}, dimensions={0} | all-to-all | bytes 262144 | tf_op jit(solution)/shard_map/all_to_all | solution.py:12
  292.8 0.1 broadcast_in_dim.45
  292.9 10.7 %all_to_all.38 = bf16[4,480,128]{2,1,0:T(8,128)(2,1)S(1)} all-to-all(bf16[4,480,128]{2,1,0:T(8,128)(2,1)S(1)} %broadcast_in_dim.45), channel_id=1, replica_groups=mesh['y'=4,'z'=16,'x'=4,'c'=2] {'x'}, dimensions={0} | all-to-all | bytes 983040 | tf_op jit(solution)/shard_map/all_to_all | solution.py:12
  303.6 9.0 %collective-permute-start.4 = (bf16[4,480,128]{2,1,0:T(8,128)(2,1)S(1)}, bf16[4,480,128]{2,1,0:T(8,128)(2,1)}, u32[]{:S(2)}, u32[]{:S(2)}) collective-permute-start(bf16[4,480,128]{2,1,0:T(8,128)(2,1)S(1)} %all_to_all.38), channel_id=1, source_target_pairs={{0,1},{1,0},{2,3},{3,2},{4,5},{5,4},{6,7},{7,6},{8,9},{9,8},{10,11... | collective-permute-start | bytes 1474568 | tf_op jit(solution)/shard_map/ppermute | solution.py:16
  312.6 0.8 fusion.17
  313.4 0.6 collective-permute-done.4
  314.0 1.1 broadcast_select_fusion.1
  315.1 0.1 maximum_bitcast_fusion
  315.2 0.0 copy-start.4
  315.2 1.7 copy.31
  316.9 3.5 %reshape.108 = bf16[3,32,5120]{2,1,0:T(8,128)(2,1)} reshape(bf16[3,32,2,4,5,128]{5,4,3,2,1,0:T(8,128)(2,1)} %copy.31) | data formatting | bytes 1966080 | tf_op jit(solution)/shard_map/reshape | solution.py:80
  320.4 3.4 %fusion.1 = bf16[1,3,32,5120]{3,2,1,0:T(8,128)(2,1)} fusion(f32[3,32,32]{2,1,0:T(8,128)S(1)} %copy-done.4, bf16[3,32,5120]{2,1,0:T(8,128)(2,1)} %reshape.108, f32[3,32,5120]{2,1,0:T(8,128)S(1)} %bitcast.47, bf16[1,3,32,5120]{3,2,1,0:T(8,128)(2,1)} %param.12), kind=kOutput, calls=%fused_computation.3 | convolution fusion | flops 190709760 | bytes 4927488 | tf_op jit(solution)/shard_map/mfr,mrd->mfd/dot_general | solution.py:84
  (26 shorter events, 0.3 us)
Async XLA Ops:
  7.2 149.8 %copy-start = (bf16[3,32,5120]{2,1,0:T(8,128)(2,1)S(1)}, bf16[3,32,5120]{2,1,0:T(8,128)(2,1)}, u32[]{:S(2)}) copy-start(bf16[3,32,5120]{2,1,0:T(8,128)(2,1)} %param.13) | copy-start | bytes 2949124
  7.2 74.9 %copy-start.5 = (bf16[1024,32]{0,1:T(8,128)(2,1)S(1)}, bf16[1024,32]{0,1:T(8,128)(2,1)}, u32[]{:S(2)}) copy-start(bf16[1024,32]{0,1:T(8,128)(2,1)} %param.9) | copy-start | bytes 196612
  7.2 74.9 %all-gather.5.cloned.1.call-start = ((), (), s32[]{:S(2)}) async-start(), calls=%async_computation.8 | async-start | bytes 11796480 | tf_op jit(solution)/shard_map/all_gather | solution.py:44
  7.9 142.9 %all-gather.3.cloned.1.call-start = ((), (), s32[]{:S(2)}) async-start(), calls=%async_computation.7 | async-start | bytes 11796480 | tf_op jit(solution)/shard_map/all_gather | solution.py:39
  8.7 142.1 %copy-start.6 = (bf16[1024,32]{0,1:T(8,128)(2,1)S(1)}, bf16[1024,32]{0,1:T(8,128)(2,1)}, u32[]{:S(2)}) copy-start(bf16[1024,32]{0,1:T(8,128)(2,1)} %param.11) | copy-start | bytes 196612
  8.7 142.1 %copy-start.7 = (bf16[1024,32]{0,1:T(8,128)(2,1)S(1)}, bf16[1024,32]{0,1:T(8,128)(2,1)}, u32[]{:S(2)}) copy-start(bf16[1024,32]{0,1:T(8,128)(2,1)} %param.10) | copy-start | bytes 196612
  150.8 6.0 %copy-start.3 = (f32[32,5120]{1,0:T(8,128)S(1)}, f32[32,5120]{1,0:T(8,128)}, u32[]{:S(2)}) copy-start(f32[32,5120]{1,0:T(8,128)} %fusion.15) | copy-start | bytes 1966084
  156.8 1.2 copy-start.1
  184.8 8.4 %all-to-all-start.1 = ((f32[4,24,128]{2,1,0:T(8,128)}), f32[4,24,128]{2,1,0:T(8,128)S(1)}, u32[]{:S(2)}, u32[]{:S(2)}) async-start(f32[4,24,128]{2,1,0:T(8,128)} %broadcast_in_dim.41), calls=%async_computation.1 | async-start | bytes 98304 | tf_op jit(solution)/shard_map/all_to_all | solution.py:12
  196.3 1.3 copy-start.2
  198.6 18.5 %collective-permute-start.3 = (f32[3,32,2560]{2,1,0:T(8,128)}, f32[3,32,2560]{2,1,0:T(8,128)}, u32[]{:S(2)}, u32[]{:S(2)}) collective-permute-start(f32[3,32,2560]{2,1,0:T(8,128)} %constant_dynamic-slice_fusion), channel_id=1, source_target_pairs={{0,1},{1,0},{2,3},{3,2},{4,5},{5,4},{6,7},{7,6},{8,9},{9,8},{10,11... | collective-permute-start | bytes 2949128 | tf_op jit(solution)/shard_map/ppermute | solution.py:16
  205.4 3.1 collective-permute-start
  208.6 4.8 %collective-permute-start.1 = (f32[3,32,32]{1,2,0:T(8,128)S(1)}, f32[3,32,32]{1,2,0:T(8,128)S(1)}, u32[]{:S(2)}, u32[]{:S(2)}) collective-permute-start(f32[3,32,32]{1,2,0:T(8,128)S(1)} %add.67), channel_id=1, source_target_pairs={{0,2},{2,0},{4,6},{6,4},{1,3},{3,1},{5,7},{7,5},{8,10},{10,8},{12,... | collective-permute-start | bytes 36872 | tf_op jit(solution)/shard_map/ppermute | solution.py:21
  213.4 16.1 %collective-permute-start.2 = (f32[3,32,32]{1,2,0:T(8,128)S(1)}, f32[3,32,32]{1,2,0:T(8,128)S(1)}, u32[]{:S(2)}, u32[]{:S(2)}) collective-permute-start(f32[3,32,32]{1,2,0:T(8,128)S(1)} %add.68), channel_id=1, source_target_pairs={{0,4},{2,6},{4,0},{6,2},{1,5},{3,7},{5,1},{7,3},{8,12},{10,14},{12... | collective-permute-start | bytes 36872 | tf_op jit(solution)/shard_map/ppermute | solution.py:22
  225.3 20.8 %all-to-all-start.2 = ((f32[4,480,128]{2,1,0:T(8,128)}), f32[4,480,128]{2,1,0:T(8,128)}, u32[]{:S(2)}, u32[]{:S(2)}) async-start(f32[4,480,128]{2,1,0:T(8,128)} %bitcast.49), calls=%async_computation.2 | async-start | bytes 1966080 | tf_op jit(solution)/shard_map/all_to_all | solution.py:66
  248.1 8.9 %all-to-all-start.3 = ((f32[4,128,128]{2,1,0:T(8,128)}), f32[4,128,128]{2,1,0:T(8,128)S(1)}, u32[]{:S(2)}, u32[]{:S(2)}) async-start(f32[4,128,128]{2,1,0:T(8,128)} %bitcast.52), calls=%async_computation.3 | async-start | bytes 524288 | tf_op jit(solution)/shard_map/all_to_all | solution.py:68
  303.6 10.5 %collective-permute-start.4 = (bf16[4,480,128]{2,1,0:T(8,128)(2,1)S(1)}, bf16[4,480,128]{2,1,0:T(8,128)(2,1)}, u32[]{:S(2)}, u32[]{:S(2)}) collective-permute-start(bf16[4,480,128]{2,1,0:T(8,128)(2,1)S(1)} %all_to_all.38), channel_id=1, source_target_pairs={{0,1},{1,0},{2,3},{3,2},{4,5},{5,4},{6,7},{7,6},{8,9},{9,8},{10,11... | collective-permute-start | bytes 1474568 | tf_op jit(solution)/shard_map/ppermute | solution.py:16
  315.2 5.2 %copy-start.4 = (f32[3,32,32]{2,1,0:T(8,128)S(1)}, f32[3,32,32]{2,1,0:T(8,128)}, u32[]{:S(2)}) copy-start(f32[3,32,32]{2,1,0:T(8,128)} %fusion.17) | copy-start | bytes 36868
Sparse Core Ops, SparseCore 0:
  10.1 71.8 all-gather.4
  84.2 66.5 all-gather.2

commit v2 on v1

v2 whole, which is shorter than its diff:
```python
import jax
import jax.numpy as jnp
from jax import lax
from jax.experimental import pallas as pl
from jax.experimental.pallas import tpu as pltpu
from jax.sharding import Mesh, PartitionSpec as P

NY, NZ, NX, NC = 4, 16, 4, 2
D = 5120
RANK = 32
ROWS = 32
CHUNKS = 4
WIDE = D // CHUNKS
HALF = D // NC
PIECE = HALF // NX
BLOCKS = PIECE // 128
UNITS = 3 * BLOCKS
F32, BF16 = jnp.float32, jnp.bfloat16
VMEM_BYTES = 48 * 1024 * 1024
PRECISE = lax.Precision.HIGHEST


def params():
    return pltpu.CompilerParams(vmem_limit_bytes=VMEM_BYTES)


def split3(value):
    high = value.astype(BF16)
    rest = value - high.astype(F32)
    middle = rest.astype(BF16)
    low = (rest - middle.astype(F32)).astype(BF16)
    return high, middle, low


def pack_rows(p_rows):
    packed = p_rows[0:8]
    for group in range(1, 4):
        packed = packed + pltpu.roll(p_rows[8 * group : 8 * group + 8], 32 * group, 1)
    return packed


def unpack_rows(packed):
    parts = [packed] + [pltpu.roll(packed, 128 - 32 * group, 1) for group in range(1, 4)]
    return jnp.concatenate(parts, axis=0)[:, :RANK]


def partial_kernel(u_self, u_far, own, sibling, pair, pair_sibling, error, mine, far):
    for at, first, last in ((0, 0, 2), (1, 2, 3)):
        tokens = jnp.concatenate([own[at], sibling[at], pair[at], pair_sibling[at]], axis=0)
        rows = slice(first * ROWS, last * ROWS)
        columns = jnp.concatenate([u_self[rows, :], u_far[rows, :]], axis=0)
        sums = jnp.dot(columns, tokens, preferred_element_type=F32)
        count = last - first
        for k in range(count):
            mine[first + k] = sums[k * ROWS : (k + 1) * ROWS] + error[0, first + k].astype(F32)
            far[first + k] = sums[(count + k) * ROWS : (count + k + 1) * ROWS]


def partials(u_self, u_far, own, sibling, pair, pair_sibling, error, chunk):
    steps = 2
    width = WIDE // steps
    u_spec = pl.BlockSpec((3 * ROWS, 512), lambda i: (0, 0))
    x_spec = pl.BlockSpec((2, 128, width), lambda i: (0, 0, i))
    e_spec = pl.BlockSpec((1, 3, ROWS, width), lambda i: (0, 0, 0, chunk * steps + i))
    o_spec = pl.BlockSpec((3, ROWS, width), lambda i: (0, 0, i))
    shape = jax.ShapeDtypeStruct((3, ROWS, WIDE), F32)
    return pl.pallas_call(
        partial_kernel,
        grid=(steps,),
        in_specs=[u_spec, u_spec, x_spec, x_spec, x_spec, x_spec, e_spec],
        out_specs=[o_spec, o_spec],
        out_shape=[shape, shape],
        compiler_params=params(),
        name="partial_gradients",
    )(u_self, u_far, own, sibling, pair, pair_sibling, error)


def left_kernel(*refs):
    mine, far, q_ref = refs[:CHUNKS], refs[CHUNKS : 2 * CHUNKS], refs[2 * CHUNKS]
    matrices, packed = refs[2 * CHUNKS + 1 :]
    total = jnp.zeros((3 * ROWS, 128), F32)
    for chunk in range(CHUNKS):
        columns = slice(chunk * WIDE, (chunk + 1) * WIDE)
        value = mine[chunk][0] + far[chunk][0]
        matrices[0, :, columns] = value
        stacked = jnp.concatenate(split3(value), axis=0)
        right = jnp.concatenate([q_ref[0, :, columns], jnp.zeros((128 - RANK, WIDE), BF16)], axis=0)
        total = total + lax.dot_general(
            stacked, right, (((1,), (1,)), ((), ())), preferred_element_type=F32
        )
    p_rows = total[:ROWS] + (total[ROWS : 2 * ROWS] + total[2 * ROWS :])
    packed[0] = pack_rows(p_rows)


def left_product(mine, far, q_start):
    chunk_spec = pl.BlockSpec((1, ROWS, WIDE), lambda m: (m, 0, 0))
    wide_spec = pl.BlockSpec((1, ROWS, D), lambda m: (m, 0, 0))
    return pl.pallas_call(
        left_kernel,
        grid=(3,),
        in_specs=[chunk_spec] * (2 * CHUNKS) + [wide_spec],
        out_specs=[wide_spec, pl.BlockSpec((1, 8, 128), lambda m: (m, 0, 0))],
        out_shape=[
            jax.ShapeDtypeStruct((3, ROWS, D), F32),
            jax.ShapeDtypeStruct((3, 8, 128), F32),
        ],
        compiler_params=params(),
        name="left_product",
    )(*mine, *far, q_start)


def right_kernel(core_ref, packed, matrices, mine, theirs, gram):
    core = core_ref[0]
    p_rows = unpack_rows(packed[0])
    gram[0] = lax.dot_general(
        p_rows, p_rows, (((0,), (0,)), ((), ())), preferred_element_type=F32, precision=PRECISE
    )
    high, middle, low = split3(p_rows)
    left = jnp.concatenate([high, high, middle, high, low, middle], axis=0)
    for out, half in ((mine, core), (theirs, 1 - core)):
        for at in range(NX):
            start = pl.multiple_of(half * HALF + at * PIECE, 128)
            high, middle, low = split3(matrices[0, :, pl.ds(start, PIECE)])
            right = jnp.concatenate([high, middle, high, low, high, middle], axis=0)
            product = lax.dot_general(
                left, right, (((0,), (0,)), ((), ())), preferred_element_type=F32
            )
            for block in range(BLOCKS):
                out[at, block] = product[:, block * 128 : (block + 1) * 128]


def right_product(core, packed, matrices):
    out_spec = pl.BlockSpec((NX, BLOCKS, RANK, 128), lambda m: (0, m, 0, 0))
    out_shape = jax.ShapeDtypeStruct((NX, UNITS, RANK, 128), F32)
    return pl.pallas_call(
        right_kernel,
        grid=(3,),
        in_specs=[
            pl.BlockSpec(memory_space=pltpu.SMEM),
            pl.BlockSpec((1, 8, 128), lambda m: (m, 0, 0)),
            pl.BlockSpec((1, ROWS, D), lambda m: (m, 0, 0)),
        ],
        out_specs=[out_spec, out_spec, pl.BlockSpec((1, RANK, RANK), lambda m: (m, 0, 0))],
        out_shape=[out_shape, out_shape, jax.ShapeDtypeStruct((3, RANK, RANK), F32)],
        compiler_params=params(),
        name="right_product",
    )(core, packed, matrices)


def factor_kernel(gram, packed, inverse, p_factor):
    lane = lax.broadcasted_iota(jnp.int32, (3, RANK, RANK), 2)
    row = lax.broadcasted_iota(jnp.int32, (3, RANK, RANK), 1)
    left = gram[...]
    right = jnp.where(lane == row, 1.0, 0.0).astype(F32)
    for step in range(RANK):
        pivot = left[:, step : step + 1, :]
        column = left[:, :, step : step + 1] / pivot[:, :, step : step + 1]
        scale = jnp.where(row[:, :, :1] > step, column, 0.0)
        right = right - scale * right[:, step : step + 1, :]
        left = left - scale * pivot
    diagonal = jnp.sum(jnp.where(lane == row, left, 0.0), axis=2, keepdims=True)
    result = right / jnp.sqrt(diagonal)
    inverse[...] = result
    for m in range(3):
        p_factor[m] = lax.dot_general(
            unpack_rows(packed[m]),
            result[m],
            (((1,), (1,)), ((), ())),
            preferred_element_type=F32,
            precision=PRECISE,
        )


def factors(gram, packed):
    shape = jax.ShapeDtypeStruct((3, RANK, RANK), F32)
    return pl.pallas_call(
        factor_kernel,
        out_shape=[shape, shape],
        compiler_params=params(),
        name="factors",
    )(gram, packed)


def error_kernel(core_ref, q_near, q_far, p_factor, matrices, q_factor, error_next):
    core = core_ref[0]
    left = jnp.concatenate(split3(p_factor[0]), axis=1)
    for part, half in ((q_near, core), (q_far, 1 - core)):
        for at in range(NX):
            start = pl.multiple_of(half * HALF + at * PIECE, 128)
            columns = pl.ds(start, PIECE)
            right = jnp.concatenate([part[at, block] for block in range(BLOCKS)], axis=1)
            q_factor[0, :, columns] = right
            rebuilt = jnp.dot(
                left, jnp.concatenate([right] * 3, axis=0), preferred_element_type=F32
            )
            error_next[0, 0, :, columns] = (matrices[0, :, columns] - rebuilt).astype(BF16)


def new_error(core, q_near, q_far, p_factor, matrices):
    q_spec = pl.BlockSpec((NX, BLOCKS, RANK, 128), lambda m: (0, m, 0, 0))
    wide_spec = pl.BlockSpec((1, ROWS, D), lambda m: (m, 0, 0))
    return pl.pallas_call(
        error_kernel,
        grid=(3,),
        in_specs=[
            pl.BlockSpec(memory_space=pltpu.SMEM),
            q_spec,
            q_spec,
            pl.BlockSpec((1, ROWS, RANK), lambda m: (m, 0, 0)),
            wide_spec,
        ],
        out_specs=[wide_spec, pl.BlockSpec((1, 1, ROWS, D), lambda m: (0, m, 0, 0))],
        out_shape=[
            jax.ShapeDtypeStruct((3, RANK, D), BF16),
            jax.ShapeDtypeStruct((1, 3, ROWS, D), BF16),
        ],
        compiler_params=params(),
        name="new_error",
    )(core, q_near, q_far, p_factor, matrices)


def spread(value, axis, count):
    copies = jnp.broadcast_to(value[None], (count,) + value.shape)
    return lax.all_to_all(copies, axis, 0, 0)


def swap_core(value):
    return lax.ppermute(value, "c", [(0, 1), (1, 0)])


def neighbour(at, way):
    return 3 - at if way else at ^ 1


def swap_chip(value, way):
    return lax.ppermute(value, "x", [(i, neighbour(i, way)) for i in range(NX)])


def sum_tensor(value):
    value = value + swap_core(value)
    value = value + lax.ppermute(value, "x", [(i, i ^ 1) for i in range(NX)])
    return value + lax.ppermute(value, "x", [(i, i ^ 2) for i in range(NX)])


def exchange(inputs, out_grad, hidden, up_grad, gate_grad, error_memory):
    chip, core = lax.axis_index("x"), lax.axis_index("c")
    columns = jnp.concatenate([up_grad.T, gate_grad.T, hidden.T], axis=0)

    def tokens_of(first, second):
        starts = [(at * 2 + side) * 128 for at in (first, second) for side in (core, 1 - core)]
        return jnp.concatenate(
            [lax.dynamic_slice_in_dim(columns, start, 128, axis=1) for start in starts], axis=1
        )

    own = [
        jnp.stack([inputs[:, k * WIDE : (k + 1) * WIDE], out_grad[:, k * WIDE : (k + 1) * WIDE]])
        for k in range(CHUNKS)
    ]
    order = (0, 2, 1, 3)
    pair = {k: swap_chip(own[k], k // 2) for k in order}
    u_self, u_far = [], []
    for way in range(2):
        partner = neighbour(chip, 1 - way)
        u_self.append(tokens_of(chip, neighbour(chip, way)))
        u_far.append(swap_chip(tokens_of(partner, neighbour(partner, way)), 1 - way))
    sibling = {k: swap_core(own[k]) for k in order}
    mine, far = {}, {}
    for k in order:
        way = k // 2
        pair_sibling = swap_core(pair[k])
        mine[k], sent = partials(
            u_self[way], u_far[way], own[k], sibling[k], pair[k], pair_sibling, error_memory, k
        )
        far[k] = swap_chip(sent, 1 - way)
    return [mine[k] for k in range(CHUNKS)], [far[k] for k in range(CHUNKS)]


def per_device(inputs, out_grad, hidden, up_grad, gate_grad, error_memory, q_start):
    core = lax.axis_index("c").reshape(1).astype(jnp.int32)
    mine, far = exchange(inputs, out_grad, hidden, up_grad, gate_grad, error_memory)
    matrices, packed = left_product(mine, far, q_start)

    packed = spread(packed, "z", NZ).sum(0)
    packed = spread(packed, "y", NY).sum(0)

    near, away, gram_part = right_product(core, packed, matrices)
    w_core = near + swap_core(away)
    inverse, p_factor = factors(sum_tensor(gram_part), packed)
    w_x = lax.all_to_all(w_core.reshape(NX, UNITS * RANK, 128), "x", 0, 0).sum(0)
    w_x = jnp.pad(w_x, ((0, RANK), (0, 0))).reshape(NY, 4 * RANK, 128)
    w_y = lax.all_to_all(w_x, "y", 0, 0).sum(0).reshape(4, RANK, 128)
    unit_of = jnp.minimum((lax.axis_index("y") * 4 + jnp.arange(4)) // BLOCKS, 2)
    q_y = jnp.einsum("urs,usd->urd", inverse[unit_of], w_y, precision=PRECISE)
    q_z = lax.all_to_all(q_y.reshape(NZ, 8, 128), "z", 0, 0).sum(0)
    q_part = (q_z / (NY * NZ)).astype(BF16)

    q_dp = spread(q_part, ("y", "z"), NY * NZ).reshape(NY * NZ * 8, 128)
    q_x = spread(q_dp[: UNITS * RANK], "x", NX).reshape(NX, UNITS, RANK, 128)
    q_factor, error_next = new_error(core, q_x, swap_core(q_x), p_factor, matrices)
    return (error_next, p_factor, q_factor)


def solution(mesh):
    fine = Mesh(mesh.devices.reshape(NY, NZ, NX, NC), ("y", "z", "x", "c"))
    dp, tensor = ("y", "z"), ("x", "c")
    in_specs = (
        P(dp + tensor, None),
        P(dp + tensor, None),
        P(dp, tensor),
        P(dp, tensor),
        P(dp, tensor),
        P(dp, None, tensor, None),
        P(),
    )
    out_specs = (P(dp, None, tensor, None), P(None, tensor, None), P())
    return jax.shard_map(
        per_device, mesh=fine, in_specs=in_specs, out_specs=out_specs, check_vma=False
    )
```

time: 332 us -> 243 us (0.73)
  waiting for transfers between devices: 150 us -> 50.2 us
  starting transfers between devices: 35.3 us -> 91.9 us
  matrix products: 21.8 us -> 0.19 us
  other arithmetic: 21.7 us -> 1.62 us
  Pallas kernels: 0 us -> 15.1 us
  between operations: 14.4 us -> 1.31 us
  local copies, waits for them, and re-layouts: 16.5 us -> 5.86 us
  blocking collectives: 71.1 us -> 75.8 us
    all_gather x2 -> x0, waiting for transfers between devices: 135 us -> none  [the longest x1 73.4 us: per_device(): lax.all_gather(out_grad, ('x', 'c'), axis=0, tiled=True)]
    ppermute x0 -> x10, waiting for transfers between devices: none -> 34.3 us  [swap_chip(): return lax.ppermute(value, 'x', [(i, neighbour(i, way)) for i in range(NX)])]
    ppermute x0 -> x10, starting transfers between devices: none -> 31.2 us  [swap_chip(): return lax.ppermute(value, 'x', [(i, neighbour(i, way)) for i in range(NX)])]
    ppermute x3 -> x11, starting transfers between devices: 17.5 us -> 47.8 us  [swap_core(): return lax.ppermute(value, 'c', [(0, 1), (1, 0)])]
    dot_general x7 -> x0, matrix products: 21.4 us -> none  [the longest x1 6.72 us: per_device(): jnp.dot(hidden.T, lax.all_gather(out_grad, ('x', 'c'), axis=0, tiled=True...]
    another operation x7 -> x4, other arithmetic: 16.4 us -> 0.25 us  [exchange(): jnp.stack([inputs[:, k * WIDE:(k + 1) * WIDE], out_grad[:, k * WIDE:(k +...]
    pallas_call x0 -> x8, Pallas kernels: none -> 15.1 us  [the longest x4 5.05 us: partials(): pl.pallas_call(partial_kernel, grid=(steps,), in_specs=[u_spec, u_spec, x...]
    all_to_all x3 -> x4, blocking collectives: 53.9 us -> 60.3 us  [spread(): return lax.all_to_all(copies, axis, 0, 0)]
  transfers between devices with their start and end apart: 10 -> 25, of which waited for: 7 -> 11; matrix products, arithmetic and copies ran while one was open for 10% -> 1% of each run, Pallas kernels for 0% -> 4%
where the time goes in v2:
time: 243 us; the launch traced here: 242 us
  starting transfers between devices  91.9 us (38%)
  blocking collectives  75.8 us (31%)
  waiting for transfers between devices  50.2 us (21%)
  Pallas kernels  15.1 us (6%)
  local copies, waits for them, and re-layouts  5.86 us (2%)
    all_to_all x4, blocking collectives, spread(): return lax.all_to_all(copies, axis, 0, 0)  60.3 us
    ppermute x11, starting transfers between devices, swap_core(): return lax.ppermute(value, 'c', [(0, 1), (1, 0)])  47.8 us
    ppermute x10, waiting for transfers between devices, swap_chip(): return lax.ppermute(value, 'x', [(i, neighbour(i, way)) for i in range(NX)])  34.3 us
    ppermute x10, starting transfers between devices, swap_chip(): return lax.ppermute(value, 'x', [(i, neighbour(i, way)) for i in range(NX)])  31.2 us
    all_to_all x1, blocking collectives, per_device(): q_z = lax.all_to_all(q_y.reshape(NZ, 8, 128), 'z', 0, 0).sum(0)  15.5 us
    all_to_all x1, waiting for transfers between devices, per_device(): lax.all_to_all(w_core.reshape(NX, UNITS * RANK, 128), 'x', 0, 0).sum(0)  7.35 us
    pallas_call x4, Pallas kernels, partials(): pl.pallas_call(partial_kernel, grid=(steps,), in_specs=[u_spec, u_spec, x...  5.05 us
  transfers between devices with their start and end apart: 25, of which 11 were waited for; matrix products, arithmetic and copies ran while one was open for 1% of the time, Pallas kernels for 4%

profile of v2, /device:TPU:1, one launch (start us, length us, event | category | flops | bytes accessed | tf_op | source)
XLA Modules:
  0.0 241.9 jit_solution(13713640092368096720)
XLA Ops:
  0.6 2.8 %slice_bitcast_fusion = (bf16[1,128,1280]{2,1,0:T(8,128)(2,1)S(1)}, bf16[1,128,1280]{2,1,0:T(8,128)(2,1)}, bf16[1,128,1280]{2,1,0:T(8,128)(2,1)}, bf16[1,128,128...) fusion(bf16[128,5120]{1,0:T(8,128)(2,1)} %param.8, ...), kind=kLoop, calls=%fused_computation.5 | loop fusion | bytes 5242880 | tf_op jit(solution)/shard_map/stack | solution.py:256
  3.4 0.1 pad_maximum_fusion.3.own
  3.5 5.2 %collective-permute-start.12 = (bf16[2,128,1280]{2,1,0:T(8,128)(2,1)S(1)}, bf16[2,128,1280]{2,1,0:T(8,128)(2,1)S(1)}, u32[]{:S(2)}, u32[]{:S(2)}) collective-permute-start(bf16[2,128,1280]{2,1,0:T(8,128)(2,1)S(1)} %pad_maximum_fusion.3.own), channel_id=1, source_target_pairs={{0,6},{2,4},{4,2},{6,0},{1,7},{3,5},{5,3},{7,1},{8,14},{10,12},{12... | collective-permute-start | bytes 1966088 | tf_op jit(solution)/shard_map/ppermute | solution.py:236
  8.7 5.5 %collective-permute-start.11 = (bf16[2,128,1280]{2,1,0:T(8,128)(2,1)S(1)}, bf16[2,128,1280]{2,1,0:T(8,128)(2,1)S(1)}, u32[]{:S(2)}, u32[]{:S(2)}) collective-permute-start(bf16[2,128,1280]{2,1,0:T(8,128)(2,1)S(1)} %pad_maximum_fusion.3.own), channel_id=1, source_target_pairs={{0,1},{1,0},{2,3},{3,2},{4,5},{5,4},{6,7},{7,6},{8,9},{9,8},{10,11... | collective-permute-start | bytes 1966088 | tf_op jit(solution)/shard_map/ppermute | solution.py:228
  14.2 0.1 pad_maximum_fusion.2.own
  14.3 4.9 %collective-permute-start.9 = (bf16[2,128,1280]{2,1,0:T(8,128)(2,1)S(1)}, bf16[2,128,1280]{2,1,0:T(8,128)(2,1)S(1)}, u32[]{:S(2)}, u32[]{:S(2)}) collective-permute-start(bf16[2,128,1280]{2,1,0:T(8,128)(2,1)S(1)} %pad_maximum_fusion.2.own), channel_id=1, source_target_pairs={{0,6},{2,4},{4,2},{6,0},{1,7},{3,5},{5,3},{7,1},{8,14},{10,12},{12... | collective-permute-start | bytes 1966088 | tf_op jit(solution)/shard_map/ppermute | solution.py:236
  19.2 2.2 collective-permute-start.8
  21.5 0.1 constant_dynamic-slice_fusion.1
  21.7 2.1 collective-permute-start.7
  23.7 0.0 copy-start
  23.7 0.1 pad_maximum_fusion.1.own
  23.8 4.0 %collective-permute-done.7.u_far = bf16[96,512]{1,0:T(8,128)(2,1)S(1)} collective-permute-done((bf16[96,512]{1,0:T(8,128)(2,1)S(1)}, bf16[96,512]{1,0:T(8,128)(2,1)S(1)}, u32[]{:S(2)}, u32[]{:S(2)}) %collective-permute-start.7) | collective-permute-done | bytes 98336 | tf_op jit(solution)/shard_map/ppermute | solution.py:236
  27.9 2.2 collective-permute-start.5
  30.1 0.1 pad_maximum_fusion.own
  30.2 3.0 %collective-permute-start.2 = (bf16[2,128,1280]{2,1,0:T(8,128)(2,1)S(1)}, bf16[2,128,1280]{2,1,0:T(8,128)(2,1)S(1)}, u32[]{:S(2)}, u32[]{:S(2)}) collective-permute-start(bf16[2,128,1280]{2,1,0:T(8,128)(2,1)S(1)} %pad_maximum_fusion.own), channel_id=1, source_target_pairs={{0,2},{2,0},{4,6},{6,4},{1,3},{3,1},{5,7},{7,5},{8,10},{10,8},{12,... | collective-permute-start | bytes 1966088 | tf_op jit(solution)/shard_map/ppermute | solution.py:236
  33.3 3.5 %collective-permute-start.13 = (bf16[2,128,1280]{2,1,0:T(8,128)(2,1)S(1)}, bf16[2,128,1280]{2,1,0:T(8,128)(2,1)S(1)}, u32[]{:S(2)}, u32[]{:S(2)}) collective-permute-start(bf16[2,128,1280]{2,1,0:T(8,128)(2,1)S(1)} %collective-permute-done.12.pair), channel_id=1, source_target_pairs={{0,1},{1,0},{2,3},{3,2},{4,5},{5,4},{6,7},{7,6},{8,9},{9,8},{10,11... | collective-permute-start | bytes 1966088 | tf_op jit(solution)/shard_map/ppermute | solution.py:228
  36.8 3.6 %collective-permute-start.10 = (bf16[2,128,1280]{2,1,0:T(8,128)(2,1)S(1)}, bf16[2,128,1280]{2,1,0:T(8,128)(2,1)S(1)}, u32[]{:S(2)}, u32[]{:S(2)}) collective-permute-start(bf16[2,128,1280]{2,1,0:T(8,128)(2,1)S(1)} %collective-permute-done.9.pair), channel_id=1, source_target_pairs={{0,1},{1,0},{2,3},{3,2},{4,5},{5,4},{6,7},{7,6},{8,9},{9,8},{10,11... | collective-permute-start | bytes 1966088 | tf_op jit(solution)/shard_map/ppermute | solution.py:228
  40.4 1.9 collective-permute-start.4
  42.3 2.7 %collective-permute-done.5.pair = bf16[2,128,1280]{2,1,0:T(8,128)(2,1)S(1)} collective-permute-done((bf16[2,128,1280]{2,1,0:T(8,128)(2,1)S(1)}, bf16[2,128,1280]{2,1,0:T(8,128)(2,1)S(1)}, u32[]{:S(2)}, u32[]{:S(2)}) %collective-permute-start.5) | collective-permute-done | bytes 655392 | tf_op jit(solution)/shard_map/ppermute | solution.py:236
  44.9 5.4 %collective-permute-start.6 = (bf16[2,128,1280]{2,1,0:T(8,128)(2,1)S(1)}, bf16[2,128,1280]{2,1,0:T(8,128)(2,1)S(1)}, u32[]{:S(2)}, u32[]{:S(2)}) collective-permute-start(bf16[2,128,1280]{2,1,0:T(8,128)(2,1)S(1)} %collective-permute-done.5.pair), channel_id=1, source_target_pairs={{0,1},{1,0},{2,3},{3,2},{4,5},{5,4},{6,7},{7,6},{8,9},{9,8},{10,11... | collective-permute-start | bytes 1966088 | tf_op jit(solution)/shard_map/ppermute | solution.py:228
  50.3 8.6 %collective-permute-done.2.pair = bf16[2,128,1280]{2,1,0:T(8,128)(2,1)S(1)} collective-permute-done((bf16[2,128,1280]{2,1,0:T(8,128)(2,1)S(1)}, bf16[2,128,1280]{2,1,0:T(8,128)(2,1)S(1)}, u32[]{:S(2)}, u32[]{:S(2)}) %collective-permute-start.2) | collective-permute-done | bytes 655392 | tf_op jit(solution)/shard_map/ppermute | solution.py:236
  59.0 3.8 %collective-permute-start.1 = (bf16[2,128,1280]{2,1,0:T(8,128)(2,1)S(1)}, bf16[2,128,1280]{2,1,0:T(8,128)(2,1)S(1)}, u32[]{:S(2)}, u32[]{:S(2)}) collective-permute-start(bf16[2,128,1280]{2,1,0:T(8,128)(2,1)S(1)} %pad_maximum_fusion.own), channel_id=1, source_target_pairs={{0,1},{1,0},{2,3},{3,2},{4,5},{5,4},{6,7},{7,6},{8,9},{9,8},{10,11... | collective-permute-start | bytes 1966088 | tf_op jit(solution)/shard_map/ppermute | solution.py:228
  62.9 1.9 collective-permute-start.3
  64.8 1.9 collective-permute-start
  66.7 1.1 partial_gradients.7
  67.8 1.8 partial_gradients.6
  69.6 2.1 collective-permute-done.u_far
  71.8 1.9 collective-permute-start.17
  73.7 3.4 %collective-permute-start.16 = (f32[3,32,1280]{2,1,0:T(8,128)S(1)}, f32[3,32,1280]{2,1,0:T(8,128)S(1)}, u32[]{:S(2)}, u32[]{:S(2)}) collective-permute-start(f32[3,32,1280]{2,1,0:T(8,128)S(1)} %get-tuple-element.26), channel_id=1, source_target_pairs={{0,2},{2,0},{4,6},{6,4},{1,3},{3,1},{5,7},{7,5},{8,10},{10,8},{12,... | collective-permute-start | bytes 1474568 | tf_op jit(solution)/shard_map/ppermute | solution.py:236
  77.1 1.1 partial_gradients.5
  78.2 2.6 %collective-permute-start.15 = (f32[3,32,1280]{2,1,0:T(8,128)S(1)}, f32[3,32,1280]{2,1,0:T(8,128)S(1)}, u32[]{:S(2)}, u32[]{:S(2)}) collective-permute-start(f32[3,32,1280]{2,1,0:T(8,128)S(1)} %get-tuple-element.25), channel_id=1, source_target_pairs={{0,6},{2,4},{4,2},{6,0},{1,7},{3,5},{5,3},{7,1},{8,14},{10,12},{12... | collective-permute-start | bytes 1474568 | tf_op jit(solution)/shard_map/ppermute | solution.py:236
  80.8 1.1 partial_gradients.4
  81.9 4.0 %collective-permute-start.14 = (f32[3,32,1280]{2,1,0:T(8,128)S(1)}, f32[3,32,1280]{2,1,0:T(8,128)S(1)}, u32[]{:S(2)}, u32[]{:S(2)}) collective-permute-start(f32[3,32,1280]{2,1,0:T(8,128)S(1)} %get-tuple-element.24), channel_id=1, source_target_pairs={{0,6},{2,4},{4,2},{6,0},{1,7},{3,5},{5,3},{7,1},{8,14},{10,12},{12... | collective-permute-start | bytes 1474568 | tf_op jit(solution)/shard_map/ppermute | solution.py:236
  85.9 9.6 %collective-permute-done.16.refs_6_ = f32[3,32,1280]{2,1,0:T(8,128)S(1)} collective-permute-done((f32[3,32,1280]{2,1,0:T(8,128)S(1)}, f32[3,32,1280]{2,1,0:T(8,128)S(1)}, u32[]{:S(2)}, u32[]{:S(2)}) %collective-permute-start.16) | collective-permute-done | bytes 491552 | tf_op jit(solution)/shard_map/ppermute | solution.py:236
  95.5 7.2 %collective-permute-done.14.refs_4_ = f32[3,32,1280]{2,1,0:T(8,128)S(1)} collective-permute-done((f32[3,32,1280]{2,1,0:T(8,128)S(1)}, f32[3,32,1280]{2,1,0:T(8,128)S(1)}, u32[]{:S(2)}, u32[]{:S(2)}) %collective-permute-start.14) | collective-permute-done | bytes 491552 | tf_op jit(solution)/shard_map/ppermute | solution.py:236
  102.7 2.1 left_product.1
  104.8 22.4 %all_to_all.35 = f32[16,3,8,128]{3,2,1,0:T(8,128)S(1)} all-to-all(f32[16,3,8,128]{3,2,1,0:T(8,128)S(1)} %broadcast_in_dim.10), channel_id=1, replica_groups=mesh['y'=4,'z'=16,'x'=4,'c'=2] {'z'}, dimensions={0} | all-to-all | bytes 393216 | tf_op jit(solution)/shard_map/all_to_all | solution.py:224
  127.3 8.4 %all_to_all.36 = f32[4,3,8,128]{3,2,1,0:T(8,128)S(1)} all-to-all(f32[4,3,8,128]{3,2,1,0:T(8,128)S(1)} %broadcast_in_dim.11), channel_id=1, replica_groups=mesh['y'=4,'z'=16,'x'=4,'c'=2] {'y'}, dimensions={0} | all-to-all | bytes 98304 | tf_op jit(solution)/shard_map/all_to_all | solution.py:224
  135.7 1.5 copy-done.1
  137.2 2.2 right_product.1
  139.4 9.0 %collective-permute-start.21 = (f32[4,15,32,128]{3,2,1,0:T(8,128)S(1)}, f32[4,15,32,128]{3,2,1,0:T(8,128)S(1)}, u32[]{:S(2)}, u32[]{:S(2)}) collective-permute-start(f32[4,15,32,128]{3,2,1,0:T(8,128)S(1)} %get-tuple-element.33), channel_id=1, source_target_pairs={{0,1},{1,0},{2,3},{3,2},{4,5},{5,4},{6,7},{7,6},{8,9},{9,8},{10,11... | collective-permute-start | bytes 2949128 | tf_op jit(solution)/shard_map/ppermute | solution.py:228
  148.4 2.2 collective-permute-done.21
  150.6 1.1 add.143
  151.7 3.5 %all-to-all-start.2 = ((f32[4,480,128]{2,1,0:T(8,128)}), f32[4,480,128]{2,1,0:T(8,128)S(1)}, u32[]{:S(2)}, u32[]{:S(2)}) async-start(f32[4,480,128]{2,1,0:T(8,128)} %bitcast.13), calls=%async_computation.2 | async-start | bytes 1966080 | tf_op jit(solution)/shard_map/all_to_all | solution.py:289
  155.2 2.3 collective-permute-start.18
  157.5 0.9 collective-permute-done.18
  158.4 3.6 %collective-permute-start.19 = (f32[3,32,32]{2,1,0:T(8,128)S(1)}, f32[3,32,32]{2,1,0:T(8,128)S(1)}, u32[]{:S(2)}, u32[]{:S(2)}) collective-permute-start(f32[3,32,32]{2,1,0:T(8,128)S(1)} %add.137), channel_id=1, source_target_pairs={{0,2},{2,0},{4,6},{6,4},{1,3},{3,1},{5,7},{7,5},{8,10},{10,8},{12,... | collective-permute-start | bytes 36872 | tf_op jit(solution)/shard_map/ppermute | solution.py:241
  162.0 7.3 %all-to-all-done.2 = f32[4,480,128]{2,1,0:T(8,128)S(1)} async-done(((f32[4,480,128]{2,1,0:T(8,128)}), f32[4,480,128]{2,1,0:T(8,128)S(1)}, u32[]{:S(2)}, u32[]{:S(2)}) %all-to-all-start.2) | async-done | bytes 983072 | tf_op jit(solution)/shard_map/all_to_all | solution.py:289
  169.3 0.1 reduce_sum.47
  169.4 0.7 pad.4
  170.1 3.4 %all-to-all-start.3 = ((f32[4,128,128]{2,1,0:T(8,128)}), f32[4,128,128]{2,1,0:T(8,128)S(1)}, u32[]{:S(2)}, u32[]{:S(2)}) async-start(f32[4,128,128]{2,1,0:T(8,128)} %bitcast.14), calls=%async_computation.3 | async-start | bytes 524288 | tf_op jit(solution)/shard_map/all_to_all | solution.py:291
  173.6 2.3 collective-permute-start.20
  175.9 4.0 %collective-permute-done.20 = f32[3,32,32]{2,1,0:T(8,128)S(1)} collective-permute-done((f32[3,32,32]{2,1,0:T(8,128)S(1)}, f32[3,32,32]{2,1,0:T(8,128)S(1)}, u32[]{:S(2)}, u32[]{:S(2)}) %collective-permute-start.20) | collective-permute-done | bytes 12320 | tf_op jit(solution)/shard_map/ppermute | solution.py:242
  179.9 3.5 %factors.1 = (f32[3,32,32]{2,1,0:T(8,128)S(1)}, f32[3,32,32]{2,1,0:T(8,128)}) custom-call(f32[3,32,32]{2,1,0:T(8,128)S(1)} %add.139.gram, f32[3,8,128]{2,1,0:T(8,128)S(1)} %reduce_sum.46.packed), custom_call_target="tpu_custom_call" | custom-call | tf_op jit(solution)/shard_map/factors/pallas_call | solution.py:176
  183.4 0.6 gather_fusion
  184.1 0.0 copy-start.4
  184.1 0.2 fusion.1
  184.3 15.5 %all_to_all.37 = f32[16,8,128]{2,1,0:T(8,128)S(1)} all-to-all(f32[16,8,128]{2,1,0:T(8,128)S(1)} %bitcast.34), channel_id=1, replica_groups=mesh['y'=4,'z'=16,'x'=4,'c'=2] {'z'}, dimensions={0} | all-to-all | bytes 131072 | tf_op jit(solution)/shard_map/all_to_all | solution.py:294
  199.9 20.3 %all_to_all.38 = bf16[64,8,128]{2,1,0:T(8,128)(2,1)S(1)} all-to-all(bf16[64,8,128]{2,1,0:T(8,128)(2,1)S(1)} %broadcast_in_dim.12), channel_id=1, replica_groups=mesh['y'=4,'z'=16,'x'=4,'c'=2] {'y','z'}, dimensions={0} | all-to-all | bytes 262144 | tf_op jit(solution)/shard_map/all_to_all | solution.py:224
  220.2 0.1 broadcast_in_dim.14
  220.3 9.1 %all_to_all.39 = bf16[4,480,128]{2,1,0:T(8,128)(2,1)S(1)} all-to-all(bf16[4,480,128]{2,1,0:T(8,128)(2,1)S(1)} %broadcast_in_dim.14), channel_id=1, replica_groups=mesh['y'=4,'z'=16,'x'=4,'c'=2] {'x'}, dimensions={0} | all-to-all | bytes 983040 | tf_op jit(solution)/shard_map/all_to_all | solution.py:224
  229.4 8.8 %collective-permute-start.22 = (bf16[4,15,32,128]{3,2,1,0:T(8,128)(2,1)S(1)}, bf16[4,15,32,128]{3,2,1,0:T(8,128)(2,1)S(1)}, u32[]{:S(2)}, u32[]{:S(2)}) collective-permute-start(bf16[4,15,32,128]{3,2,1,0:T(8,128)(2,1)S(1)} %bitcast.31), channel_id=1, source_target_pairs={{0,1},{1,0},{2,3},{3,2},{4,5},{5,4},{6,7},{7,6},{8,9},{9,8},{10,11... | collective-permute-start | bytes 1474568 | tf_op jit(solution)/shard_map/ppermute | solution.py:228
  238.2 1.5 collective-permute-done.22.q_far
  239.7 2.3 new_error.1
  (51 shorter events, 0.3 us)
Async XLA Ops:
  3.4 18.0 %copy-start.9 = (bf16[1024,32]{0,1:T(8,128)(2,1)S(1)}, bf16[1024,32]{0,1:T(8,128)(2,1)}, u32[]{:S(2)}) copy-start(bf16[1024,32]{0,1:T(8,128)(2,1)} %param.9) | copy-start | bytes 196612
  3.4 18.0 %copy-start.10 = (bf16[1024,32]{0,1:T(8,128)(2,1)S(1)}, bf16[1024,32]{0,1:T(8,128)(2,1)}, u32[]{:S(2)}) copy-start(bf16[1024,32]{0,1:T(8,128)(2,1)} %param.11) | copy-start | bytes 196612
  3.4 18.0 %copy-start.11 = (bf16[1024,32]{0,1:T(8,128)(2,1)S(1)}, bf16[1024,32]{0,1:T(8,128)(2,1)}, u32[]{:S(2)}) copy-start(bf16[1024,32]{0,1:T(8,128)(2,1)} %param.10) | copy-start | bytes 196612
  3.5 26.7 %collective-permute-start.12 = (bf16[2,128,1280]{2,1,0:T(8,128)(2,1)S(1)}, bf16[2,128,1280]{2,1,0:T(8,128)(2,1)S(1)}, u32[]{:S(2)}, u32[]{:S(2)}) collective-permute-start(bf16[2,128,1280]{2,1,0:T(8,128)(2,1)S(1)} %pad_maximum_fusion.3.own), channel_id=1, source_target_pairs={{0,6},{2,4},{4,2},{6,0},{1,7},{3,5},{5,3},{7,1},{8,14},{10,12},{12... | collective-permute-start | bytes 1966088 | tf_op jit(solution)/shard_map/ppermute | solution.py:236
  8.7 24.5 %collective-permute-start.11 = (bf16[2,128,1280]{2,1,0:T(8,128)(2,1)S(1)}, bf16[2,128,1280]{2,1,0:T(8,128)(2,1)S(1)}, u32[]{:S(2)}, u32[]{:S(2)}) collective-permute-start(bf16[2,128,1280]{2,1,0:T(8,128)(2,1)S(1)} %pad_maximum_fusion.3.own), channel_id=1, source_target_pairs={{0,1},{1,0},{2,3},{3,2},{4,5},{5,4},{6,7},{7,6},{8,9},{9,8},{10,11... | collective-permute-start | bytes 1966088 | tf_op jit(solution)/shard_map/ppermute | solution.py:228
  14.3 22.5 %collective-permute-start.9 = (bf16[2,128,1280]{2,1,0:T(8,128)(2,1)S(1)}, bf16[2,128,1280]{2,1,0:T(8,128)(2,1)S(1)}, u32[]{:S(2)}, u32[]{:S(2)}) collective-permute-start(bf16[2,128,1280]{2,1,0:T(8,128)(2,1)S(1)} %pad_maximum_fusion.2.own), channel_id=1, source_target_pairs={{0,6},{2,4},{4,2},{6,0},{1,7},{3,5},{5,3},{7,1},{8,14},{10,12},{12... | collective-permute-start | bytes 1966088 | tf_op jit(solution)/shard_map/ppermute | solution.py:236
  19.2 21.2 %collective-permute-start.8 = (bf16[2,128,1280]{2,1,0:T(8,128)(2,1)S(1)}, bf16[2,128,1280]{2,1,0:T(8,128)(2,1)}, u32[]{:S(2)}, u32[]{:S(2)}) collective-permute-start(bf16[2,128,1280]{2,1,0:T(8,128)(2,1)S(1)} %pad_maximum_fusion.2.own), channel_id=1, source_target_pairs={{0,1},{1,0},{2,3},{3,2},{4,5},{5,4},{6,7},{7,6},{8,9},{9,8},{10,11... | collective-permute-start | bytes 1966088 | tf_op jit(solution)/shard_map/ppermute | solution.py:228
  21.4 2.3 copy-start.7
  21.4 2.3 copy-start.8
  21.5 8.6 %copy-start.5 = (bf16[1,128,1280]{2,1,0:T(8,128)(2,1)S(1)}, bf16[1,128,1280]{2,1,0:T(8,128)(2,1)}, u32[]{:S(2)}) copy-start(bf16[1,128,1280]{2,1,0:T(8,128)(2,1)} %get-tuple-element.43) | copy-start | bytes 983044
  21.5 8.6 %copy-start.6 = (bf16[1,128,1280]{2,1,0:T(8,128)(2,1)S(1)}, bf16[1,128,1280]{2,1,0:T(8,128)(2,1)}, u32[]{:S(2)}) copy-start(bf16[1,128,1280]{2,1,0:T(8,128)(2,1)} %get-tuple-element.60) | copy-start | bytes 983044
  21.7 6.2 %collective-permute-start.7 = (bf16[96,512]{1,0:T(8,128)(2,1)S(1)}, bf16[96,512]{1,0:T(8,128)(2,1)S(1)}, u32[]{:S(2)}, u32[]{:S(2)}) collective-permute-start(bf16[96,512]{1,0:T(8,128)(2,1)S(1)} %get-tuple-element.55), channel_id=1, source_target_pairs={{0,2},{2,0},{4,6},{6,4},{1,3},{3,1},{5,7},{7,5},{8,10},{10,8},{12,... | collective-permute-start | bytes 294920 | tf_op jit(solution)/shard_map/ppermute | solution.py:236
  23.7 43.0 %copy-start = (bf16[1,3,32,5120]{3,2,1,0:T(8,128)(2,1)S(1)}, bf16[1,3,32,5120]{3,2,1,0:T(8,128)(2,1)}, u32[]{:S(2)}) copy-start(bf16[1,3,32,5120]{3,2,1,0:T(8,128)(2,1)} %error.7) | copy-start | bytes 2949124
  27.9 17.1 %collective-permute-start.5 = (bf16[2,128,1280]{2,1,0:T(8,128)(2,1)S(1)}, bf16[2,128,1280]{2,1,0:T(8,128)(2,1)S(1)}, u32[]{:S(2)}, u32[]{:S(2)}) collective-permute-start(bf16[2,128,1280]{2,1,0:T(8,128)(2,1)S(1)} %pad_maximum_fusion.1.own), channel_id=1, source_target_pairs={{0,2},{2,0},{4,6},{6,4},{1,3},{3,1},{5,7},{7,5},{8,10},{10,8},{12,... | collective-permute-start | bytes 1966088 | tf_op jit(solution)/shard_map/ppermute | solution.py:236
  30.2 28.8 %collective-permute-start.2 = (bf16[2,128,1280]{2,1,0:T(8,128)(2,1)S(1)}, bf16[2,128,1280]{2,1,0:T(8,128)(2,1)S(1)}, u32[]{:S(2)}, u32[]{:S(2)}) collective-permute-start(bf16[2,128,1280]{2,1,0:T(8,128)(2,1)S(1)} %pad_maximum_fusion.own), channel_id=1, source_target_pairs={{0,2},{2,0},{4,6},{6,4},{1,3},{3,1},{5,7},{7,5},{8,10},{10,8},{12,... | collective-permute-start | bytes 1966088 | tf_op jit(solution)/shard_map/ppermute | solution.py:236
  33.3 29.6 %collective-permute-start.13 = (bf16[2,128,1280]{2,1,0:T(8,128)(2,1)S(1)}, bf16[2,128,1280]{2,1,0:T(8,128)(2,1)S(1)}, u32[]{:S(2)}, u32[]{:S(2)}) collective-permute-start(bf16[2,128,1280]{2,1,0:T(8,128)(2,1)S(1)} %collective-permute-done.12.pair), channel_id=1, source_target_pairs={{0,1},{1,0},{2,3},{3,2},{4,5},{5,4},{6,7},{7,6},{8,9},{9,8},{10,11... | collective-permute-start | bytes 1966088 | tf_op jit(solution)/shard_map/ppermute | solution.py:228
  36.8 28.0 %collective-permute-start.10 = (bf16[2,128,1280]{2,1,0:T(8,128)(2,1)S(1)}, bf16[2,128,1280]{2,1,0:T(8,128)(2,1)S(1)}, u32[]{:S(2)}, u32[]{:S(2)}) collective-permute-start(bf16[2,128,1280]{2,1,0:T(8,128)(2,1)S(1)} %collective-permute-done.9.pair), channel_id=1, source_target_pairs={{0,1},{1,0},{2,3},{3,2},{4,5},{5,4},{6,7},{7,6},{8,9},{9,8},{10,11... | collective-permute-start | bytes 1966088 | tf_op jit(solution)/shard_map/ppermute | solution.py:228
  40.4 33.3 %collective-permute-start.4 = (bf16[2,128,1280]{2,1,0:T(8,128)(2,1)S(1)}, bf16[2,128,1280]{2,1,0:T(8,128)(2,1)S(1)}, u32[]{:S(2)}, u32[]{:S(2)}) collective-permute-start(bf16[2,128,1280]{2,1,0:T(8,128)(2,1)S(1)} %pad_maximum_fusion.1.own), channel_id=1, source_target_pairs={{0,1},{1,0},{2,3},{3,2},{4,5},{5,4},{6,7},{7,6},{8,9},{9,8},{10,11... | collective-permute-start | bytes 1966088 | tf_op jit(solution)/shard_map/ppermute | solution.py:228
  44.9 32.1 %collective-permute-start.6 = (bf16[2,128,1280]{2,1,0:T(8,128)(2,1)S(1)}, bf16[2,128,1280]{2,1,0:T(8,128)(2,1)S(1)}, u32[]{:S(2)}, u32[]{:S(2)}) collective-permute-start(bf16[2,128,1280]{2,1,0:T(8,128)(2,1)S(1)} %collective-permute-done.5.pair), channel_id=1, source_target_pairs={{0,1},{1,0},{2,3},{3,2},{4,5},{5,4},{6,7},{7,6},{8,9},{9,8},{10,11... | collective-permute-start | bytes 1966088 | tf_op jit(solution)/shard_map/ppermute | solution.py:228
  59.0 21.8 %collective-permute-start.1 = (bf16[2,128,1280]{2,1,0:T(8,128)(2,1)S(1)}, bf16[2,128,1280]{2,1,0:T(8,128)(2,1)S(1)}, u32[]{:S(2)}, u32[]{:S(2)}) collective-permute-start(bf16[2,128,1280]{2,1,0:T(8,128)(2,1)S(1)} %pad_maximum_fusion.own), channel_id=1, source_target_pairs={{0,1},{1,0},{2,3},{3,2},{4,5},{5,4},{6,7},{7,6},{8,9},{9,8},{10,11... | collective-permute-start | bytes 1966088 | tf_op jit(solution)/shard_map/ppermute | solution.py:228
  62.9 17.9 %collective-permute-start.3 = (bf16[2,128,1280]{2,1,0:T(8,128)(2,1)S(1)}, bf16[2,128,1280]{2,1,0:T(8,128)(2,1)S(1)}, u32[]{:S(2)}, u32[]{:S(2)}) collective-permute-start(bf16[2,128,1280]{2,1,0:T(8,128)(2,1)S(1)} %collective-permute-done.2.pair), channel_id=1, source_target_pairs={{0,1},{1,0},{2,3},{3,2},{4,5},{5,4},{6,7},{7,6},{8,9},{9,8},{10,11... | collective-permute-start | bytes 1966088 | tf_op jit(solution)/shard_map/ppermute | solution.py:228
  64.8 7.0 %collective-permute-start = (bf16[96,512]{1,0:T(8,128)(2,1)S(1)}, bf16[96,512]{1,0:T(8,128)(2,1)S(1)}, u32[]{:S(2)}, u32[]{:S(2)}) collective-permute-start(bf16[96,512]{1,0:T(8,128)(2,1)S(1)} %get-tuple-element.58), channel_id=1, source_target_pairs={{0,6},{2,4},{4,2},{6,0},{1,7},{3,5},{5,3},{7,1},{8,14},{10,12},{12... | collective-permute-start | bytes 294920 | tf_op jit(solution)/shard_map/ppermute | solution.py:236
  71.8 14.2 %collective-permute-start.17 = (f32[3,32,1280]{2,1,0:T(8,128)S(1)}, f32[3,32,1280]{2,1,0:T(8,128)S(1)}, u32[]{:S(2)}, u32[]{:S(2)}) collective-permute-start(f32[3,32,1280]{2,1,0:T(8,128)S(1)} %get-tuple-element.27), channel_id=1, source_target_pairs={{0,2},{2,0},{4,6},{6,4},{1,3},{3,1},{5,7},{7,5},{8,10},{10,8},{12,... | collective-permute-start | bytes 1474568 | tf_op jit(solution)/shard_map/ppermute | solution.py:236
  73.7 21.9 %collective-permute-start.16 = (f32[3,32,1280]{2,1,0:T(8,128)S(1)}, f32[3,32,1280]{2,1,0:T(8,128)S(1)}, u32[]{:S(2)}, u32[]{:S(2)}) collective-permute-start(f32[3,32,1280]{2,1,0:T(8,128)S(1)} %get-tuple-element.26), channel_id=1, source_target_pairs={{0,2},{2,0},{4,6},{6,4},{1,3},{3,1},{5,7},{7,5},{8,10},{10,8},{12,... | collective-permute-start | bytes 1474568 | tf_op jit(solution)/shard_map/ppermute | solution.py:236
  78.2 24.6 %copy-start.3 = (bf16[3,32,5120]{2,1,0:T(8,128)(2,1)S(1)}, bf16[3,32,5120]{2,1,0:T(8,128)(2,1)}, u32[]{:S(2)}) copy-start(bf16[3,32,5120]{2,1,0:T(8,128)(2,1)} %refs_8_.1) | copy-start | bytes 2949124
  78.2 17.4 %collective-permute-start.15 = (f32[3,32,1280]{2,1,0:T(8,128)S(1)}, f32[3,32,1280]{2,1,0:T(8,128)S(1)}, u32[]{:S(2)}, u32[]{:S(2)}) collective-permute-start(f32[3,32,1280]{2,1,0:T(8,128)S(1)} %get-tuple-element.25), channel_id=1, source_target_pairs={{0,6},{2,4},{4,2},{6,0},{1,7},{3,5},{5,3},{7,1},{8,14},{10,12},{12... | collective-permute-start | bytes 1474568 | tf_op jit(solution)/shard_map/ppermute | solution.py:236
  81.9 20.8 %collective-permute-start.14 = (f32[3,32,1280]{2,1,0:T(8,128)S(1)}, f32[3,32,1280]{2,1,0:T(8,128)S(1)}, u32[]{:S(2)}, u32[]{:S(2)}) collective-permute-start(f32[3,32,1280]{2,1,0:T(8,128)S(1)} %get-tuple-element.24), channel_id=1, source_target_pairs={{0,6},{2,4},{4,2},{6,0},{1,7},{3,5},{5,3},{7,1},{8,14},{10,12},{12... | collective-permute-start | bytes 1474568 | tf_op jit(solution)/shard_map/ppermute | solution.py:236
  135.7 1.5 copy-start.1
  139.4 11.2 %collective-permute-start.21 = (f32[4,15,32,128]{3,2,1,0:T(8,128)S(1)}, f32[4,15,32,128]{3,2,1,0:T(8,128)S(1)}, u32[]{:S(2)}, u32[]{:S(2)}) collective-permute-start(f32[4,15,32,128]{3,2,1,0:T(8,128)S(1)} %get-tuple-element.33), channel_id=1, source_target_pairs={{0,1},{1,0},{2,3},{3,2},{4,5},{5,4},{6,7},{7,6},{8,9},{9,8},{10,11... | collective-permute-start | bytes 2949128 | tf_op jit(solution)/shard_map/ppermute | solution.py:228
  151.7 17.6 %all-to-all-start.2 = ((f32[4,480,128]{2,1,0:T(8,128)}), f32[4,480,128]{2,1,0:T(8,128)S(1)}, u32[]{:S(2)}, u32[]{:S(2)}) async-start(f32[4,480,128]{2,1,0:T(8,128)} %bitcast.13), calls=%async_computation.2 | async-start | bytes 1966080 | tf_op jit(solution)/shard_map/all_to_all | solution.py:289
  155.2 3.1 %collective-permute-start.18 = (f32[3,32,32]{2,1,0:T(8,128)S(1)}, f32[3,32,32]{2,1,0:T(8,128)S(1)}, u32[]{:S(2)}, u32[]{:S(2)}) collective-permute-start(f32[3,32,32]{2,1,0:T(8,128)S(1)} %get-tuple-element.30), channel_id=1, source_target_pairs={{0,1},{1,0},{2,3},{3,2},{4,5},{5,4},{6,7},{7,6},{8,9},{9,8},{10,11... | collective-permute-start | bytes 36872 | tf_op jit(solution)/shard_map/ppermute | solution.py:228
  158.4 15.2 %collective-permute-start.19 = (f32[3,32,32]{2,1,0:T(8,128)S(1)}, f32[3,32,32]{2,1,0:T(8,128)S(1)}, u32[]{:S(2)}, u32[]{:S(2)}) collective-permute-start(f32[3,32,32]{2,1,0:T(8,128)S(1)} %add.137), channel_id=1, source_target_pairs={{0,2},{2,0},{4,6},{6,4},{1,3},{3,1},{5,7},{7,5},{8,10},{10,8},{12,... | collective-permute-start | bytes 36872 | tf_op jit(solution)/shard_map/ppermute | solution.py:241
  170.1 13.9 %all-to-all-start.3 = ((f32[4,128,128]{2,1,0:T(8,128)}), f32[4,128,128]{2,1,0:T(8,128)S(1)}, u32[]{:S(2)}, u32[]{:S(2)}) async-start(f32[4,128,128]{2,1,0:T(8,128)} %bitcast.14), calls=%async_computation.3 | async-start | bytes 524288 | tf_op jit(solution)/shard_map/all_to_all | solution.py:291
  173.6 6.3 %collective-permute-start.20 = (f32[3,32,32]{2,1,0:T(8,128)S(1)}, f32[3,32,32]{2,1,0:T(8,128)S(1)}, u32[]{:S(2)}, u32[]{:S(2)}) collective-permute-start(f32[3,32,32]{2,1,0:T(8,128)S(1)} %add.138), channel_id=1, source_target_pairs={{0,4},{2,6},{4,0},{6,2},{1,5},{3,7},{5,1},{7,3},{8,12},{10,14},{12... | collective-permute-start | bytes 36872 | tf_op jit(solution)/shard_map/ppermute | solution.py:242
  184.0 55.6 %copy-start.2 = (f32[3,32,5120]{2,1,0:T(8,128)S(1)}, f32[3,32,5120]{2,1,0:T(8,128)}, u32[]{:S(2)}) copy-start(f32[3,32,5120]{2,1,0:T(8,128)} %get-tuple-element.29.matrices) | copy-start | bytes 5898244
  184.1 55.6 %copy-start.4 = (f32[3,32,32]{2,1,0:T(8,128)S(1)}, f32[3,32,32]{2,1,0:T(8,128)}, u32[]{:S(2)}) copy-start(f32[3,32,32]{2,1,0:T(8,128)} %get-tuple-element.18.p_factor) | copy-start | bytes 36868
  229.4 10.2 %collective-permute-start.22 = (bf16[4,15,32,128]{3,2,1,0:T(8,128)(2,1)S(1)}, bf16[4,15,32,128]{3,2,1,0:T(8,128)(2,1)S(1)}, u32[]{:S(2)}, u32[]{:S(2)}) collective-permute-start(bf16[4,15,32,128]{3,2,1,0:T(8,128)(2,1)S(1)} %bitcast.31), channel_id=1, source_target_pairs={{0,1},{1,0},{2,3},{3,2},{4,5},{5,4},{6,7},{7,6},{8,9},{9,8},{10,11... | collective-permute-start | bytes 1474568 | tf_op jit(solution)/shard_map/ppermute | solution.py:228

commit v3 on v2

v3 whole, which is shorter than its diff:
```python
import jax
import jax.numpy as jnp
from jax import lax
from jax.experimental import pallas as pl
from jax.experimental.pallas import tpu as pltpu
from jax.sharding import Mesh, PartitionSpec as P

NY, NZ, NX, NC = 4, 16, 4, 2
D = 5120
RANK = 32
ROWS = 32
HALF = D // NC
PIECE = HALF // NX
BLOCKS = PIECE // 128
UNITS = 3 * BLOCKS
F32, BF16 = jnp.float32, jnp.bfloat16
VMEM_BYTES = 48 * 1024 * 1024
PRECISE = lax.Precision.HIGHEST


def params():
    return pltpu.CompilerParams(vmem_limit_bytes=VMEM_BYTES)


def split3(value):
    high = value.astype(BF16)
    rest = value - high.astype(F32)
    middle = rest.astype(BF16)
    low = (rest - middle.astype(F32)).astype(BF16)
    return high, middle, low


def pack_rows(p_rows):
    packed = p_rows[0:8]
    for group in range(1, 4):
        packed = packed + pltpu.roll(p_rows[8 * group : 8 * group + 8], 32 * group, 1)
    return packed


def unpack_rows(packed):
    parts = [packed] + [pltpu.roll(packed, 128 - 32 * group, 1) for group in range(1, 4)]
    return jnp.concatenate(parts, axis=0)


def partial_kernel(u_self, u_far, own, sibling, pair, pair_sibling, error, q_ref, mine, far, p_mine, p_far, total):
    step = pl.program_id(0)

    @pl.when(step == 0)
    def _():
        total[...] = jnp.zeros_like(total)

    width = own.shape[2]
    for at, first, last in ((0, 0, 2), (1, 2, 3)):
        tokens = jnp.concatenate([own[at], sibling[at], pair[at], pair_sibling[at]], axis=0)
        rows = slice(first * ROWS, last * ROWS)
        columns = jnp.concatenate([u_self[rows, :], u_far[rows, :]], axis=0)
        sums = jnp.dot(columns, tokens, preferred_element_type=F32)
        count = last - first
        for k in range(count):
            m = first + k
            mine_m = sums[k * ROWS : (k + 1) * ROWS] + error[0, m].astype(F32)
            far_m = sums[(count + k) * ROWS : (count + k + 1) * ROWS]
            mine[m] = mine_m
            far[m] = far_m
            stacked = jnp.concatenate(split3(mine_m) + split3(far_m), axis=0)
            right = jnp.concatenate([q_ref[m], jnp.zeros((128 - RANK, width), BF16)], axis=0)
            total[m] += lax.dot_general(
                stacked, right, (((1,), (1,)), ((), ())), preferred_element_type=F32
            )

    @pl.when(step == pl.num_programs(0) - 1)
    def _():
        for m in range(3):
            for at, out in ((0, p_mine), (3, p_far)):
                parts = [total[m, (at + k) * ROWS : (at + k + 1) * ROWS] for k in range(3)]
                out[m] = pack_rows(parts[0] + (parts[1] + parts[2]))


def partials(u_self, u_far, own, sibling, pair, pair_sibling, error, q_start, way):
    steps = 4
    width = HALF // steps
    u_spec = pl.BlockSpec((3 * ROWS, 512), lambda i: (0, 0))
    x_spec = pl.BlockSpec((2, 128, width), lambda i: (0, 0, i))
    e_spec = pl.BlockSpec((1, 3, ROWS, width), lambda i: (0, 0, 0, way * steps + i))
    q_spec = pl.BlockSpec((3, RANK, width), lambda i: (0, 0, way * steps + i))
    o_spec = pl.BlockSpec((3, ROWS, width), lambda i: (0, 0, i))
    p_spec = pl.BlockSpec((3, 8, 128), lambda i: (0, 0, 0))
    shape = jax.ShapeDtypeStruct((3, ROWS, HALF), F32)
    p_shape = jax.ShapeDtypeStruct((3, 8, 128), F32)
    return pl.pallas_call(
        partial_kernel,
        grid=(steps,),
        in_specs=[u_spec, u_spec, x_spec, x_spec, x_spec, x_spec, e_spec, q_spec],
        out_specs=[o_spec, o_spec, p_spec, p_spec],
        out_shape=[shape, shape, p_shape, p_shape],
        scratch_shapes=[pltpu.VMEM((3, 6 * ROWS, 128), F32)],
        compiler_params=params(),
        name="partial_gradients",
    )(u_self, u_far, own, sibling, pair, pair_sibling, error, q_start)


def right_kernel(core_ref, packed, mine_0, far_0, mine_1, far_1, near, away):
    m = pl.program_id(0)
    first = core_ref[0] == 0
    wide = unpack_rows(packed[0])
    lane = lax.broadcasted_iota(jnp.int32, wide.shape, 1)
    wide = jnp.where(lane < RANK, wide, 0.0)
    p_rows = wide[:, :RANK]
    gram = lax.dot_general(
        p_rows,
        pltpu.roll(wide, RANK * m, 1),
        (((0,), (0,)), ((), ())),
        preferred_element_type=F32,
        precision=PRECISE,
    )
    for out in (near, away):
        for at in range(NX):
            out[at, UNITS] = jnp.where(m == 0, gram, out[at, UNITS] + gram)
    high, middle, low = split3(p_rows)
    left = jnp.concatenate([high, high, middle, high, low, middle], axis=0)
    for at in range(NX):
        columns = slice(at * PIECE, (at + 1) * PIECE)
        value_0 = mine_0[0, :, columns] + far_0[0, :, columns]
        value_1 = mine_1[0, :, columns] + far_1[0, :, columns]
        halves = jnp.where(first, value_0, value_1), jnp.where(first, value_1, value_0)
        for out, value in zip((near, away), halves):
            high, middle, low = split3(value)
            right = jnp.concatenate([high, middle, high, low, high, middle], axis=0)
            product = lax.dot_general(
                left, right, (((0,), (0,)), ((), ())), preferred_element_type=F32
            )
            for block in range(BLOCKS):
                out[at, m * BLOCKS + block] = product[:, block * 128 : (block + 1) * 128]


def right_product(core, packed, mine, far):
    wide_spec = pl.BlockSpec((1, ROWS, HALF), lambda m: (m, 0, 0))
    out_spec = pl.BlockSpec((NX, UNITS + 1, RANK, 128), lambda m: (0, 0, 0, 0))
    out_shape = jax.ShapeDtypeStruct((NX, UNITS + 1, RANK, 128), F32)
    return pl.pallas_call(
        right_kernel,
        grid=(3,),
        in_specs=[
            pl.BlockSpec(memory_space=pltpu.SMEM),
            pl.BlockSpec((1, 8, 128), lambda m: (m, 0, 0)),
        ]
        + [wide_spec] * 4,
        out_specs=[out_spec, out_spec],
        out_shape=[out_shape, out_shape],
        compiler_params=params(),
        name="right_product",
    )(core, packed, mine[0], far[0], mine[1], far[1])


def factor_kernel(gram, packed, inverse, p_factor):
    lane = lax.broadcasted_iota(jnp.int32, (3, RANK, RANK), 2)
    row = lax.broadcasted_iota(jnp.int32, (3, RANK, RANK), 1)
    wide = gram[...]
    left = jnp.stack(
        [wide[:, :RANK]] + [pltpu.roll(wide, 128 - RANK * m, 1)[:, :RANK] for m in (1, 2)]
    )
    right = jnp.where(lane == row, 1.0, 0.0).astype(F32)
    for step in range(RANK):
        pivot = left[:, step : step + 1, :]
        column = left[:, :, step : step + 1] / pivot[:, :, step : step + 1]
        scale = jnp.where(row[:, :, :1] > step, column, 0.0)
        right = right - scale * right[:, step : step + 1, :]
        left = left - scale * pivot
    diagonal = jnp.sum(jnp.where(lane == row, left, 0.0), axis=2, keepdims=True)
    result = right / jnp.sqrt(diagonal)
    inverse[...] = result
    for m in range(3):
        p_factor[m] = lax.dot_general(
            unpack_rows(packed[m])[:, :RANK],
            result[m],
            (((1,), (1,)), ((), ())),
            preferred_element_type=F32,
            precision=PRECISE,
        )


def factors(gram, packed):
    shape = jax.ShapeDtypeStruct((3, RANK, RANK), F32)
    return pl.pallas_call(
        factor_kernel,
        out_shape=[shape, shape],
        compiler_params=params(),
        name="factors",
    )(gram, packed)


def error_kernel(core_ref, q_near, q_far, p_factor, mine_0, far_0, mine_1, far_1, q_factor, error_next):
    first = core_ref[0] == 0
    left = jnp.concatenate(split3(p_factor[0]), axis=1)
    for at in range(NX):
        columns = slice(at * PIECE, (at + 1) * PIECE)
        near = jnp.concatenate([q_near[at, block] for block in range(BLOCKS)], axis=1)
        away = jnp.concatenate([q_far[at, block] for block in range(BLOCKS)], axis=1)
        halves = jnp.where(first, near, away), jnp.where(first, away, near)
        for half, mine, far in ((0, mine_0, far_0), (1, mine_1, far_1)):
            right = halves[half]
            there = slice(half * HALF + at * PIECE, half * HALF + (at + 1) * PIECE)
            q_factor[0, :, there] = right
            rebuilt = jnp.dot(
                left, jnp.concatenate([right] * 3, axis=0), preferred_element_type=F32
            )
            value = mine[0, :, columns] + far[0, :, columns]
            error_next[0, 0, :, there] = (value - rebuilt).astype(BF16)


def new_error(core, q_near, q_far, p_factor, mine, far):
    q_spec = pl.BlockSpec((NX, BLOCKS, RANK, 128), lambda m: (0, m, 0, 0))
    half_spec = pl.BlockSpec((1, ROWS, HALF), lambda m: (m, 0, 0))
    return pl.pallas_call(
        error_kernel,
        grid=(3,),
        in_specs=[
            pl.BlockSpec(memory_space=pltpu.SMEM),
            q_spec,
            q_spec,
            pl.BlockSpec((1, ROWS, RANK), lambda m: (m, 0, 0)),
        ]
        + [half_spec] * 4,
        out_specs=[
            pl.BlockSpec((1, RANK, D), lambda m: (m, 0, 0)),
            pl.BlockSpec((1, 1, ROWS, D), lambda m: (0, m, 0, 0)),
        ],
        out_shape=[
            jax.ShapeDtypeStruct((3, RANK, D), BF16),
            jax.ShapeDtypeStruct((1, 3, ROWS, D), BF16),
        ],
        compiler_params=params(),
        name="new_error",
    )(core, q_near, q_far, p_factor, mine[0], far[0], mine[1], far[1])


def spread(value, axis, count):
    copies = jnp.broadcast_to(value[None], (count,) + value.shape)
    return lax.all_to_all(copies, axis, 0, 0)


def swap_core(value):
    return lax.ppermute(value, "c", [(0, 1), (1, 0)])


def neighbour(at, way):
    return 3 - at if way else at ^ 1


def swap_chip(value, way):
    return lax.ppermute(value, "x", [(i, neighbour(i, way)) for i in range(NX)])


def exchange(inputs, out_grad, hidden, up_grad, gate_grad, error_memory, q_start):
    chip, core = lax.axis_index("x"), lax.axis_index("c")
    columns = jnp.concatenate([up_grad.T, gate_grad.T, hidden.T], axis=0)

    def tokens_of(first, second):
        starts = [(at * 2 + side) * 128 for at in (first, second) for side in (core, 1 - core)]
        return jnp.concatenate(
            [lax.dynamic_slice_in_dim(columns, start, 128, axis=1) for start in starts], axis=1
        )

    own, pair, u_self, u_far = [], [], [], []
    for way in range(2):
        here = slice(way * HALF, (way + 1) * HALF)
        own.append(jnp.stack([inputs[:, here], out_grad[:, here]]))
        pair.append(swap_chip(own[way], way))
    for way in range(2):
        partner = neighbour(chip, 1 - way)
        u_self.append(tokens_of(chip, neighbour(chip, way)))
        u_far.append(swap_chip(tokens_of(partner, neighbour(partner, way)), 1 - way))
    sibling = [swap_core(own[way]) for way in range(2)]
    mine, sent, packed, p_sent = [], [], [], []
    for way in range(2):
        results = partials(
            u_self[way],
            u_far[way],
            own[way],
            sibling[way],
            pair[way],
            swap_core(pair[way]),
            error_memory,
            q_start,
            way,
        )
        for values, value in zip((mine, sent, packed, p_sent), results):
            values.append(value)
    p_far = [swap_chip(p_sent[way], 1 - way) for way in range(2)]
    far = [swap_chip(sent[way], 1 - way) for way in range(2)]
    return mine, far, (packed[0] + packed[1]) + (p_far[0] + p_far[1])


def per_device(inputs, out_grad, hidden, up_grad, gate_grad, error_memory, q_start):
    core = lax.axis_index("c").reshape(1).astype(jnp.int32)
    mine, far, packed = exchange(
        inputs, out_grad, hidden, up_grad, gate_grad, error_memory, q_start
    )
    packed = spread(packed, "z", NZ).sum(0)
    packed = spread(packed, "y", NY).sum(0)

    near, away = right_product(core, packed, mine, far)
    w_core = near + swap_core(away)
    w_x = lax.all_to_all(w_core, "x", 0, 0).sum(0)
    inverse, p_factor = factors(w_x[UNITS], packed)
    w_y = lax.all_to_all(w_x.reshape(NY, 4, RANK, 128), "y", 0, 0).sum(0)
    unit_of = jnp.minimum((lax.axis_index("y") * 4 + jnp.arange(4)) // BLOCKS, 2)
    q_y = jnp.einsum("urs,usd->urd", inverse[unit_of], w_y, precision=PRECISE)
    q_z = lax.all_to_all(q_y.reshape(NZ, 8, 128), "z", 0, 0).sum(0)
    q_part = (q_z / (NY * NZ)).astype(BF16)

    q_dp = spread(q_part, "z", NZ).reshape(4, RANK, 128)
    q_near = spread(q_dp, ("x", "y"), NX * NY).reshape(NX, UNITS + 1, RANK, 128)
    q_factor, error_next = new_error(core, q_near, swap_core(q_near), p_factor, mine, far)
    return (error_next, p_factor, q_factor)


def solution(mesh):
    fine = Mesh(mesh.devices.reshape(NY, NZ, NX, NC), ("y", "z", "x", "c"))
    dp, tensor = ("y", "z"), ("x", "c")
    in_specs = (
        P(dp + tensor, None),
        P(dp + tensor, None),
        P(dp, tensor),
        P(dp, tensor),
        P(dp, tensor),
        P(dp, None, tensor, None),
        P(),
    )
    out_specs = (P(dp, None, tensor, None), P(None, tensor, None), P())
    return jax.shard_map(
        per_device, mesh=fine, in_specs=in_specs, out_specs=out_specs, check_vma=False
    )
```

time: 243 us -> 219 us (0.901)
  starting transfers between devices: 91.9 us -> 65.8 us
  waiting for transfers between devices: 50.2 us -> 40.7 us
  Pallas kernels: 15.1 us -> 22.4 us
  blocking collectives: 75.8 us -> 78.4 us
    ppermute x11 -> x6, starting transfers between devices: 47.8 us -> 32.9 us  [swap_core(): return lax.ppermute(value, 'c', [(0, 1), (1, 0)])]
    ppermute x10 -> x8, waiting for transfers between devices: 34.3 us -> 21.4 us  [swap_chip(): return lax.ppermute(value, 'x', [(i, neighbour(i, way)) for i in range(NX)])]
    all_to_all x2, waiting for transfers between devices: 7.35 us -> 15.5 us  [the longest x1 14.9 us: per_device(): w_x = lax.all_to_all(w_core, 'x', 0, 0).sum(0)]
    pallas_call x4 -> x2, Pallas kernels: 5.05 us -> 11.8 us  [partials(): pl.pallas_call(partial_kernel, grid=(steps,), in_specs=[u_spec, u_spec, x...]
    ppermute x10 -> x8, starting transfers between devices: 31.2 us -> 25.2 us  [swap_chip(): return lax.ppermute(value, 'x', [(i, neighbour(i, way)) for i in range(NX)])]
    ppermute x2 -> x0, starting transfers between devices: 5.88 us -> none  [the longest x1 3.6 us: sum_tensor(): value = value + lax.ppermute(value, 'x', [(i, i ^ 1) for i in range(NX)])]
    ppermute x2 -> x0, waiting for transfers between devices: 4.03 us -> none  [the longest x1 4.03 us: sum_tensor(): return value + lax.ppermute(value, 'x', [(i, i ^ 2) for i in range(NX)])]
    all_to_all x4, blocking collectives: 60.3 us -> 62.8 us  [spread(): return lax.all_to_all(copies, axis, 0, 0)]
  transfers between devices with their start and end apart: 25 -> 16, of which waited for: 11 -> 6; matrix products, arithmetic and copies ran while one was open for 1% -> 1% of each run, Pallas kernels for 4% -> 7%
where the time goes in v3:
time: 219 us; the launch traced here: 218 us
  blocking collectives  78.4 us (36%)
  starting transfers between devices  65.8 us (30%)
  waiting for transfers between devices  40.7 us (19%)
  Pallas kernels  22.4 us (10%)
  local copies, waits for them, and re-layouts  5.53 us (3%)
  other arithmetic  3.62 us (2%)
    all_to_all x4, blocking collectives, spread(): return lax.all_to_all(copies, axis, 0, 0)  62.8 us
    ppermute x6, starting transfers between devices, swap_core(): return lax.ppermute(value, 'c', [(0, 1), (1, 0)])  32.9 us
    ppermute x8, starting transfers between devices, swap_chip(): return lax.ppermute(value, 'x', [(i, neighbour(i, way)) for i in range(NX)])  25.2 us
    ppermute x8, waiting for transfers between devices, swap_chip(): return lax.ppermute(value, 'x', [(i, neighbour(i, way)) for i in range(NX)])  21.4 us
    all_to_all x1, blocking collectives, per_device(): q_z = lax.all_to_all(q_y.reshape(NZ, 8, 128), 'z', 0, 0).sum(0)  15.6 us
    all_to_all x1, waiting for transfers between devices, per_device(): w_x = lax.all_to_all(w_core, 'x', 0, 0).sum(0)  14.9 us
    pallas_call x2, Pallas kernels, partials(): pl.pallas_call(partial_kernel, grid=(steps,), in_specs=[u_spec, u_spec, x...  11.8 us
  transfers between devices with their start and end apart: 16, of which 6 were waited for; matrix products, arithmetic and copies ran while one was open for 1% of the time, Pallas kernels for 7%

profile of v3, /device:TPU:1, one launch (start us, length us, event | category | flops | bytes accessed | tf_op | source)
XLA Modules:
  0.0 217.7 jit_solution(9710001411526027734)
XLA Ops:
  0.6 1.9 slice_bitcast_fusion
  2.5 0.1 pad_maximum_fusion.1.own
  2.6 5.2 %collective-permute-start.6 = (bf16[2,128,2560]{2,1,0:T(8,128)(2,1)S(1)}, bf16[2,128,2560]{2,1,0:T(8,128)(2,1)}, u32[]{:S(2)}, u32[]{:S(2)}) collective-permute-start(bf16[2,128,2560]{2,1,0:T(8,128)(2,1)S(1)} %pad_maximum_fusion.1.own), channel_id=1, source_target_pairs={{0,6},{2,4},{4,2},{6,0},{1,7},{3,5},{5,3},{7,1},{8,14},{10,12},{12... | collective-permute-start | bytes 3932168 | tf_op jit(solution)/shard_map/ppermute | solution.py:251
  7.8 0.0 copy-start.5
  7.9 0.0 copy-start.6
  7.9 0.0 copy-start.7
  7.9 0.1 pad_maximum_fusion.own
  8.0 1.9 collective-permute-start.2
  9.9 5.5 %collective-permute-start.5 = (bf16[2,128,2560]{2,1,0:T(8,128)(2,1)S(1)}, bf16[2,128,2560]{2,1,0:T(8,128)(2,1)}, u32[]{:S(2)}, u32[]{:S(2)}) collective-permute-start(bf16[2,128,2560]{2,1,0:T(8,128)(2,1)S(1)} %pad_maximum_fusion.1.own), channel_id=1, source_target_pairs={{0,1},{1,0},{2,3},{3,2},{4,5},{5,4},{6,7},{7,6},{8,9},{9,8},{10,11... | collective-permute-start | bytes 3932168 | tf_op jit(solution)/shard_map/ppermute | solution.py:243
  15.4 17.1 %collective-permute-done.6.pair = bf16[2,128,2560]{2,1,0:T(8,128)(2,1)} collective-permute-done((bf16[2,128,2560]{2,1,0:T(8,128)(2,1)S(1)}, bf16[2,128,2560]{2,1,0:T(8,128)(2,1)}, u32[]{:S(2)}, u32[]{:S(2)}) %collective-permute-start.6) | collective-permute-done | bytes 1310752 | tf_op jit(solution)/shard_map/ppermute | solution.py:251
  32.6 7.0 %collective-permute-start.7 = (bf16[2,128,2560]{2,1,0:T(8,128)(2,1)}, bf16[2,128,2560]{2,1,0:T(8,128)(2,1)}, u32[]{:S(2)}, u32[]{:S(2)}) collective-permute-start(bf16[2,128,2560]{2,1,0:T(8,128)(2,1)} %collective-permute-done.6.pair), channel_id=1, source_target_pairs={{0,1},{1,0},{2,3},{3,2},{4,5},{5,4},{6,7},{7,6},{8,9},{9,8},{10,11... | collective-permute-start | bytes 3932168 | tf_op jit(solution)/shard_map/ppermute | solution.py:243
  39.6 1.9 collective-permute-start.1
  41.5 0.0 collective-permute-done.2.pair
  41.5 2.4 %collective-permute-start.3 = (bf16[2,128,2560]{2,1,0:T(8,128)(2,1)}, bf16[2,128,2560]{2,1,0:T(8,128)(2,1)}, u32[]{:S(2)}, u32[]{:S(2)}) collective-permute-start(bf16[2,128,2560]{2,1,0:T(8,128)(2,1)} %collective-permute-done.2.pair), channel_id=1, source_target_pairs={{0,1},{1,0},{2,3},{3,2},{4,5},{5,4},{6,7},{7,6},{8,9},{9,8},{10,11... | collective-permute-start | bytes 3932168 | tf_op jit(solution)/shard_map/ppermute | solution.py:243
  44.0 0.0 copy-start
  44.0 0.0 copy-done.5
  44.0 0.0 copy-done.6
  44.0 0.0 copy-done.7
  44.0 0.1 constant_dynamic-slice_fusion.1
  44.2 2.2 %collective-permute-start.4 = (bf16[96,512]{1,0:T(8,128)(2,1)S(1)}, bf16[96,512]{1,0:T(8,128)(2,1)S(1)}, u32[]{:S(2)}, u32[]{:S(2)}) collective-permute-start(bf16[96,512]{1,0:T(8,128)(2,1)S(1)} %get-tuple-element.45), channel_id=1, source_target_pairs={{0,2},{2,0},{4,6},{6,4},{1,3},{3,1},{5,7},{7,5},{8,10},{10,8},{12,... | collective-permute-start | bytes 294920 | tf_op jit(solution)/shard_map/ppermute | solution.py:251
  46.4 4.2 %collective-permute-done.4.u_far = bf16[96,512]{1,0:T(8,128)(2,1)S(1)} collective-permute-done((bf16[96,512]{1,0:T(8,128)(2,1)S(1)}, bf16[96,512]{1,0:T(8,128)(2,1)S(1)}, u32[]{:S(2)}, u32[]{:S(2)}) %collective-permute-start.4) | collective-permute-done | bytes 98336 | tf_op jit(solution)/shard_map/ppermute | solution.py:251
  50.6 4.6 %collective-permute-start = (bf16[96,512]{1,0:T(8,128)(2,1)S(1)}, bf16[96,512]{1,0:T(8,128)(2,1)S(1)}, u32[]{:S(2)}, u32[]{:S(2)}) collective-permute-start(bf16[96,512]{1,0:T(8,128)(2,1)S(1)} %get-tuple-element.48), channel_id=1, source_target_pairs={{0,6},{2,4},{4,2},{6,0},{1,7},{3,5},{5,3},{7,1},{8,14},{10,12},{12... | collective-permute-start | bytes 294920 | tf_op jit(solution)/shard_map/ppermute | solution.py:251
  55.2 0.0 collective-permute-done.5.sibling
  55.2 0.0 collective-permute-done.7.pair_sibling
  55.2 0.0 copy-start.1
  55.2 1.2 copy-done.1
  56.4 5.9 %partial_gradients.3 = (f32[3,32,2560]{2,1,0:T(8,128)S(1)}, f32[3,32,2560]{2,1,0:T(8,128)}, f32[3,8,128]{2,1,0:T(8,128)S(1)}, f32[3,8,128]{2,1,0:T(8,128)S(1)}) custom-call(bf16[96,512]{1,0:T(8,128)(2,1)S(1)} %get-tuple-element.47.u_self, bf16[96,512]{1,0:T(8,128)(2,1)S(1)} %collective-permute-done.4.u_far, bf16[2,128,2560]{2,1,0:T(8,128)(2,1)S(1)} %pad_maximum_fusion.1.own, ...), custom_call_target="tpu_custom_call" | custom-call | tf_op jit(solution)/shard_map/partial_gradients/pallas_call | solution.py:90
  62.3 1.0 copy-done.2
  63.3 1.9 collective-permute-start.9
  65.2 0.0 collective-permute-done.u_far
  65.2 0.0 collective-permute-done.1.sibling
  65.2 0.0 collective-permute-done.3.pair_sibling
  65.2 5.9 %partial_gradients.2 = (f32[3,32,2560]{2,1,0:T(8,128)S(1)}, f32[3,32,2560]{2,1,0:T(8,128)}, f32[3,8,128]{2,1,0:T(8,128)S(1)}, f32[3,8,128]{2,1,0:T(8,128)S(1)}) custom-call(bf16[96,512]{1,0:T(8,128)(2,1)S(1)} %get-tuple-element.46.u_self, bf16[96,512]{1,0:T(8,128)(2,1)S(1)} %collective-permute-done.u_far, bf16[2,128,2560]{2,1,0:T(8,128)(2,1)S(1)} %pad_maximum_fusion.own, ...), custom_call_target="tpu_custom_call" | custom-call | tf_op jit(solution)/shard_map/partial_gradients/pallas_call | solution.py:90
  71.2 2.2 %collective-permute-start.8 = (f32[3,8,128]{2,1,0:T(8,128)S(1)}, f32[3,8,128]{2,1,0:T(8,128)S(1)}, u32[]{:S(2)}, u32[]{:S(2)}) collective-permute-start(f32[3,8,128]{2,1,0:T(8,128)S(1)} %get-tuple-element.19), channel_id=1, source_target_pairs={{0,6},{2,4},{4,2},{6,0},{1,7},{3,5},{5,3},{7,1},{8,14},{10,12},{12... | collective-permute-start | bytes 36872 | tf_op jit(solution)/shard_map/ppermute | solution.py:251
  73.4 3.2 %collective-permute-start.11 = (f32[3,32,2560]{2,1,0:T(8,128)}, f32[3,32,2560]{2,1,0:T(8,128)S(1)}, u32[]{:S(2)}, u32[]{:S(2)}) collective-permute-start(f32[3,32,2560]{2,1,0:T(8,128)} %get-tuple-element.24), channel_id=1, source_target_pairs={{0,2},{2,0},{4,6},{6,4},{1,3},{3,1},{5,7},{7,5},{8,10},{10,8},{12,... | collective-permute-start | bytes 2949128 | tf_op jit(solution)/shard_map/ppermute | solution.py:251
  76.6 4.0 %collective-permute-start.10 = (f32[3,32,2560]{2,1,0:T(8,128)}, f32[3,32,2560]{2,1,0:T(8,128)}, u32[]{:S(2)}, u32[]{:S(2)}) collective-permute-start(f32[3,32,2560]{2,1,0:T(8,128)} %get-tuple-element.22), channel_id=1, source_target_pairs={{0,6},{2,4},{4,2},{6,0},{1,7},{3,5},{5,3},{7,1},{8,14},{10,12},{12... | collective-permute-start | bytes 2949128 | tf_op jit(solution)/shard_map/ppermute | solution.py:251
  80.5 0.0 collective-permute-done.9
  80.6 0.0 collective-permute-done.8
  80.6 27.1 %all_to_all.35 = f32[16,3,8,128]{3,2,1,0:T(8,128)S(1)} all-to-all(f32[16,3,8,128]{3,2,1,0:T(8,128)S(1)} %broadcast_in_dim.10), channel_id=1, replica_groups=mesh['y'=4,'z'=16,'x'=4,'c'=2] {'z'}, dimensions={0} | all-to-all | bytes 393216 | tf_op jit(solution)/shard_map/all_to_all | solution.py:239
  107.7 8.4 %all_to_all.36 = f32[4,3,8,128]{3,2,1,0:T(8,128)S(1)} all-to-all(f32[4,3,8,128]{3,2,1,0:T(8,128)S(1)} %broadcast_in_dim.11), channel_id=1, replica_groups=mesh['y'=4,'z'=16,'x'=4,'c'=2] {'y'}, dimensions={0} | all-to-all | bytes 98304 | tf_op jit(solution)/shard_map/all_to_all | solution.py:239
  116.1 0.0 collective-permute-done.11.far_1
  116.1 0.0 collective-permute-done.10.far_0
  116.1 0.0 copy-done.3
  116.1 3.4 %right_product.1 = (f32[4,16,32,128]{3,2,1,0:T(8,128)S(1)}, f32[4,16,32,128]{3,2,1,0:T(8,128)S(1)}) custom-call(s32[1]{0:T(128)} %bitcast.core_ref, f32[3,8,128]{2,1,0:T(8,128)S(1)} %reduce_sum.46.packed, f32[3,32,2560]{2,1,0:T(8,128)S(1)} %get-tuple-element.21.mine_0, f32[3,32,2560]{2,1,0:T(8,128)} %collective-permute-done.10.far_0, ...), custom_call_target="tpu_custom_call" | custom-call | tf_op jit(solution)/shard_map/right_product/pallas_call | solution.py:140
  119.5 8.8 %collective-permute-start.12 = (f32[4,16,32,128]{3,2,1,0:T(8,128)S(1)}, f32[4,16,32,128]{3,2,1,0:T(8,128)S(1)}, u32[]{:S(2)}, u32[]{:S(2)}) collective-permute-start(f32[4,16,32,128]{3,2,1,0:T(8,128)S(1)} %get-tuple-element.26), channel_id=1, source_target_pairs={{0,1},{1,0},{2,3},{3,2},{4,5},{5,4},{6,7},{7,6},{8,9},{9,8},{10,11... | collective-permute-start | bytes 3145736 | tf_op jit(solution)/shard_map/ppermute | solution.py:243
  128.3 2.3 %collective-permute-done.12 = f32[4,16,32,128]{3,2,1,0:T(8,128)S(1)} collective-permute-done((f32[4,16,32,128]{3,2,1,0:T(8,128)S(1)}, f32[4,16,32,128]{3,2,1,0:T(8,128)S(1)}, u32[]{:S(2)}, u32[]{:S(2)}) %collective-permute-start.12) | collective-permute-done | bytes 1048608 | tf_op jit(solution)/shard_map/ppermute | solution.py:243
  130.6 1.2 add.138
  131.7 4.2 %all-to-all-start.2 = ((f32[4,16,32,128]{3,2,1,0:T(8,128)}), f32[4,16,32,128]{3,2,1,0:T(8,128)}, u32[]{:S(2)}, u32[]{:S(2)}) async-start(f32[4,16,32,128]{3,2,1,0:T(8,128)} %add.138), calls=%async_computation.2 | async-start | bytes 2097152 | tf_op jit(solution)/shard_map/all_to_all | solution.py:304
  136.0 14.9 %all-to-all-done.2 = f32[4,16,32,128]{3,2,1,0:T(8,128)} async-done(((f32[4,16,32,128]{3,2,1,0:T(8,128)}), f32[4,16,32,128]{3,2,1,0:T(8,128)}, u32[]{:S(2)}, u32[]{:S(2)}) %all-to-all-start.2) | async-done | bytes 1048608 | tf_op jit(solution)/shard_map/all_to_all | solution.py:304
  150.9 2.0 reduce_sum.47
  152.9 3.4 %all-to-all-start.3 = ((f32[4,4,32,128]{3,2,1,0:T(8,128)}), f32[4,4,32,128]{3,2,1,0:T(8,128)S(1)}, u32[]{:S(2)}, u32[]{:S(2)}) async-start(f32[4,4,32,128]{3,2,1,0:T(8,128)} %bitcast.10), calls=%async_computation.3 | async-start | bytes 524288 | tf_op jit(solution)/shard_map/all_to_all | solution.py:306
  156.3 0.7 slice_bitcast_fusion.4.gram
  157.1 3.6 %factors.1 = (f32[3,32,32]{2,1,0:T(8,128)S(1)}, f32[3,32,32]{2,1,0:T(8,128)}) custom-call(f32[32,128]{1,0:T(8,128)S(1)} %slice_bitcast_fusion.4.gram, f32[3,8,128]{2,1,0:T(8,128)S(1)} %reduce_sum.46.packed), custom_call_target="tpu_custom_call" | custom-call | tf_op jit(solution)/shard_map/factors/pallas_call | solution.py:184
  160.6 0.6 gather_fusion
  161.2 0.6 all-to-all-done.3
  161.9 0.2 fusion.1
  162.1 15.6 %all_to_all.37 = f32[16,8,128]{2,1,0:T(8,128)S(1)} all-to-all(f32[16,8,128]{2,1,0:T(8,128)S(1)} %bitcast.24), channel_id=1, replica_groups=mesh['y'=4,'z'=16,'x'=4,'c'=2] {'z'}, dimensions={0} | all-to-all | bytes 131072 | tf_op jit(solution)/shard_map/all_to_all | solution.py:309
  177.7 14.3 %all_to_all.38 = bf16[16,8,128]{2,1,0:T(8,128)(2,1)S(1)} all-to-all(bf16[16,8,128]{2,1,0:T(8,128)(2,1)S(1)} %broadcast_in_dim.12), channel_id=1, replica_groups=mesh['y'=4,'z'=16,'x'=4,'c'=2] {'z'}, dimensions={0} | all-to-all | bytes 65536 | tf_op jit(solution)/shard_map/all_to_all | solution.py:239
  192.0 0.1 broadcast_in_dim.14
  192.1 13.1 %all_to_all.39 = bf16[16,4,32,128]{3,2,1,0:T(8,128)(2,1)S(1)} all-to-all(bf16[16,4,32,128]{3,2,1,0:T(8,128)(2,1)S(1)} %broadcast_in_dim.14), channel_id=1, replica_groups=mesh['y'=4,'z'=16,'x'=4,'c'=2] {'x','y'}, dimensions={0} | all-to-all | bytes 1048576 | tf_op jit(solution)/shard_map/all_to_all | solution.py:239
  205.2 7.4 %collective-permute-start.13 = (bf16[4,16,32,128]{3,2,1,0:T(8,128)(2,1)S(1)}, bf16[4,16,32,128]{3,2,1,0:T(8,128)(2,1)S(1)}, u32[]{:S(2)}, u32[]{:S(2)}) collective-permute-start(bf16[4,16,32,128]{3,2,1,0:T(8,128)(2,1)S(1)} %bitcast.22), channel_id=1, source_target_pairs={{0,1},{1,0},{2,3},{3,2},{4,5},{5,4},{6,7},{7,6},{8,9},{9,8},{10,11... | collective-permute-start | bytes 1572872 | tf_op jit(solution)/shard_map/ppermute | solution.py:243
  212.5 1.5 collective-permute-done.13.q_far
  214.0 0.0 copy-done.4
  214.0 3.6 %new_error.1 = (bf16[3,32,5120]{2,1,0:T(8,128)(2,1)}, bf16[1,3,32,5120]{3,2,1,0:T(8,128)(2,1)}) custom-call(s32[1]{0:T(128)} %bitcast.core_ref, bf16[4,16,32,128]{3,2,1,0:T(8,128)(2,1)S(1)} %bitcast.23, bf16[4,16,32,128]{3,2,1,0:T(8,128)(2,1)S(1)} %collective-permute-done.13.q_far, f32[3,32,32]{2,1,0:T(8,128)S(1)} %copy-done.4, ...), custom_call_target="tpu_custom_call" | custom-call | tf_op jit(solution)/shard_map/new_error/pallas_call | solution.py:214
  (17 shorter events, 0.2 us)
Async XLA Ops:
  2.6 30.0 %collective-permute-start.6 = (bf16[2,128,2560]{2,1,0:T(8,128)(2,1)S(1)}, bf16[2,128,2560]{2,1,0:T(8,128)(2,1)}, u32[]{:S(2)}, u32[]{:S(2)}) collective-permute-start(bf16[2,128,2560]{2,1,0:T(8,128)(2,1)S(1)} %pad_maximum_fusion.1.own), channel_id=1, source_target_pairs={{0,6},{2,4},{4,2},{6,0},{1,7},{3,5},{5,3},{7,1},{8,14},{10,12},{12... | collective-permute-start | bytes 3932168 | tf_op jit(solution)/shard_map/ppermute | solution.py:251
  7.8 36.1 %copy-start.5 = (bf16[1024,32]{0,1:T(8,128)(2,1)S(1)}, bf16[1024,32]{0,1:T(8,128)(2,1)}, u32[]{:S(2)}) copy-start(bf16[1024,32]{0,1:T(8,128)(2,1)} %param.9) | copy-start | bytes 196612
  7.9 36.1 %copy-start.6 = (bf16[1024,32]{0,1:T(8,128)(2,1)S(1)}, bf16[1024,32]{0,1:T(8,128)(2,1)}, u32[]{:S(2)}) copy-start(bf16[1024,32]{0,1:T(8,128)(2,1)} %param.11) | copy-start | bytes 196612
  7.9 36.1 %copy-start.7 = (bf16[1024,32]{0,1:T(8,128)(2,1)S(1)}, bf16[1024,32]{0,1:T(8,128)(2,1)}, u32[]{:S(2)}) copy-start(bf16[1024,32]{0,1:T(8,128)(2,1)} %param.10) | copy-start | bytes 196612
  8.0 33.5 %collective-permute-start.2 = (bf16[2,128,2560]{2,1,0:T(8,128)(2,1)S(1)}, bf16[2,128,2560]{2,1,0:T(8,128)(2,1)}, u32[]{:S(2)}, u32[]{:S(2)}) collective-permute-start(bf16[2,128,2560]{2,1,0:T(8,128)(2,1)S(1)} %pad_maximum_fusion.own), channel_id=1, source_target_pairs={{0,2},{2,0},{4,6},{6,4},{1,3},{3,1},{5,7},{7,5},{8,10},{10,8},{12,... | collective-permute-start | bytes 3932168 | tf_op jit(solution)/shard_map/ppermute | solution.py:251
  9.9 45.3 %collective-permute-start.5 = (bf16[2,128,2560]{2,1,0:T(8,128)(2,1)S(1)}, bf16[2,128,2560]{2,1,0:T(8,128)(2,1)}, u32[]{:S(2)}, u32[]{:S(2)}) collective-permute-start(bf16[2,128,2560]{2,1,0:T(8,128)(2,1)S(1)} %pad_maximum_fusion.1.own), channel_id=1, source_target_pairs={{0,1},{1,0},{2,3},{3,2},{4,5},{5,4},{6,7},{7,6},{8,9},{9,8},{10,11... | collective-permute-start | bytes 3932168 | tf_op jit(solution)/shard_map/ppermute | solution.py:243
  32.6 22.6 %collective-permute-start.7 = (bf16[2,128,2560]{2,1,0:T(8,128)(2,1)}, bf16[2,128,2560]{2,1,0:T(8,128)(2,1)}, u32[]{:S(2)}, u32[]{:S(2)}) collective-permute-start(bf16[2,128,2560]{2,1,0:T(8,128)(2,1)} %collective-permute-done.6.pair), channel_id=1, source_target_pairs={{0,1},{1,0},{2,3},{3,2},{4,5},{5,4},{6,7},{7,6},{8,9},{9,8},{10,11... | collective-permute-start | bytes 3932168 | tf_op jit(solution)/shard_map/ppermute | solution.py:243
  39.6 25.6 %collective-permute-start.1 = (bf16[2,128,2560]{2,1,0:T(8,128)(2,1)S(1)}, bf16[2,128,2560]{2,1,0:T(8,128)(2,1)}, u32[]{:S(2)}, u32[]{:S(2)}) collective-permute-start(bf16[2,128,2560]{2,1,0:T(8,128)(2,1)S(1)} %pad_maximum_fusion.own), channel_id=1, source_target_pairs={{0,1},{1,0},{2,3},{3,2},{4,5},{5,4},{6,7},{7,6},{8,9},{9,8},{10,11... | collective-permute-start | bytes 3932168 | tf_op jit(solution)/shard_map/ppermute | solution.py:243
  41.5 23.7 %collective-permute-start.3 = (bf16[2,128,2560]{2,1,0:T(8,128)(2,1)}, bf16[2,128,2560]{2,1,0:T(8,128)(2,1)}, u32[]{:S(2)}, u32[]{:S(2)}) collective-permute-start(bf16[2,128,2560]{2,1,0:T(8,128)(2,1)} %collective-permute-done.2.pair), channel_id=1, source_target_pairs={{0,1},{1,0},{2,3},{3,2},{4,5},{5,4},{6,7},{7,6},{8,9},{9,8},{10,11... | collective-permute-start | bytes 3932168 | tf_op jit(solution)/shard_map/ppermute | solution.py:243
  44.0 11.2 %copy-start = (bf16[1,3,32,5120]{3,2,1,0:T(8,128)(2,1)S(1)}, bf16[1,3,32,5120]{3,2,1,0:T(8,128)(2,1)}, u32[]{:S(2)}) copy-start(bf16[1,3,32,5120]{3,2,1,0:T(8,128)(2,1)} %error.3) | copy-start | bytes 2949124
  44.2 6.4 %collective-permute-start.4 = (bf16[96,512]{1,0:T(8,128)(2,1)S(1)}, bf16[96,512]{1,0:T(8,128)(2,1)S(1)}, u32[]{:S(2)}, u32[]{:S(2)}) collective-permute-start(bf16[96,512]{1,0:T(8,128)(2,1)S(1)} %get-tuple-element.45), channel_id=1, source_target_pairs={{0,2},{2,0},{4,6},{6,4},{1,3},{3,1},{5,7},{7,5},{8,10},{10,8},{12,... | collective-permute-start | bytes 294920 | tf_op jit(solution)/shard_map/ppermute | solution.py:251
  50.6 14.6 %collective-permute-start = (bf16[96,512]{1,0:T(8,128)(2,1)S(1)}, bf16[96,512]{1,0:T(8,128)(2,1)S(1)}, u32[]{:S(2)}, u32[]{:S(2)}) collective-permute-start(bf16[96,512]{1,0:T(8,128)(2,1)S(1)} %get-tuple-element.48), channel_id=1, source_target_pairs={{0,6},{2,4},{4,2},{6,0},{1,7},{3,5},{5,3},{7,1},{8,14},{10,12},{12... | collective-permute-start | bytes 294920 | tf_op jit(solution)/shard_map/ppermute | solution.py:251
  55.2 1.2 copy-start.1
  62.3 1.0 copy-start.2
  63.3 17.3 %collective-permute-start.9 = (f32[3,8,128]{2,1,0:T(8,128)S(1)}, f32[3,8,128]{2,1,0:T(8,128)S(1)}, u32[]{:S(2)}, u32[]{:S(2)}) collective-permute-start(f32[3,8,128]{2,1,0:T(8,128)S(1)} %get-tuple-element.20), channel_id=1, source_target_pairs={{0,2},{2,0},{4,6},{6,4},{1,3},{3,1},{5,7},{7,5},{8,10},{10,8},{12,... | collective-permute-start | bytes 36872 | tf_op jit(solution)/shard_map/ppermute | solution.py:251
  71.2 44.9 %copy-start.3 = (f32[3,32,2560]{2,1,0:T(8,128)S(1)}, f32[3,32,2560]{2,1,0:T(8,128)}, u32[]{:S(2)}) copy-start(f32[3,32,2560]{2,1,0:T(8,128)} %copy-done.2) | copy-start | bytes 2949124
  71.2 9.4 %collective-permute-start.8 = (f32[3,8,128]{2,1,0:T(8,128)S(1)}, f32[3,8,128]{2,1,0:T(8,128)S(1)}, u32[]{:S(2)}, u32[]{:S(2)}) collective-permute-start(f32[3,8,128]{2,1,0:T(8,128)S(1)} %get-tuple-element.19), channel_id=1, source_target_pairs={{0,6},{2,4},{4,2},{6,0},{1,7},{3,5},{5,3},{7,1},{8,14},{10,12},{12... | collective-permute-start | bytes 36872 | tf_op jit(solution)/shard_map/ppermute | solution.py:251
  73.4 42.7 %collective-permute-start.11 = (f32[3,32,2560]{2,1,0:T(8,128)}, f32[3,32,2560]{2,1,0:T(8,128)S(1)}, u32[]{:S(2)}, u32[]{:S(2)}) collective-permute-start(f32[3,32,2560]{2,1,0:T(8,128)} %get-tuple-element.24), channel_id=1, source_target_pairs={{0,2},{2,0},{4,6},{6,4},{1,3},{3,1},{5,7},{7,5},{8,10},{10,8},{12,... | collective-permute-start | bytes 2949128 | tf_op jit(solution)/shard_map/ppermute | solution.py:251
  76.6 39.5 %collective-permute-start.10 = (f32[3,32,2560]{2,1,0:T(8,128)}, f32[3,32,2560]{2,1,0:T(8,128)}, u32[]{:S(2)}, u32[]{:S(2)}) collective-permute-start(f32[3,32,2560]{2,1,0:T(8,128)} %get-tuple-element.22), channel_id=1, source_target_pairs={{0,6},{2,4},{4,2},{6,0},{1,7},{3,5},{5,3},{7,1},{8,14},{10,12},{12... | collective-permute-start | bytes 2949128 | tf_op jit(solution)/shard_map/ppermute | solution.py:251
  119.5 11.1 %collective-permute-start.12 = (f32[4,16,32,128]{3,2,1,0:T(8,128)S(1)}, f32[4,16,32,128]{3,2,1,0:T(8,128)S(1)}, u32[]{:S(2)}, u32[]{:S(2)}) collective-permute-start(f32[4,16,32,128]{3,2,1,0:T(8,128)S(1)} %get-tuple-element.26), channel_id=1, source_target_pairs={{0,1},{1,0},{2,3},{3,2},{4,5},{5,4},{6,7},{7,6},{8,9},{9,8},{10,11... | collective-permute-start | bytes 3145736 | tf_op jit(solution)/shard_map/ppermute | solution.py:243
  131.7 19.1 %all-to-all-start.2 = ((f32[4,16,32,128]{3,2,1,0:T(8,128)}), f32[4,16,32,128]{3,2,1,0:T(8,128)}, u32[]{:S(2)}, u32[]{:S(2)}) async-start(f32[4,16,32,128]{3,2,1,0:T(8,128)} %add.138), calls=%async_computation.2 | async-start | bytes 2097152 | tf_op jit(solution)/shard_map/all_to_all | solution.py:304
  152.9 8.9 %all-to-all-start.3 = ((f32[4,4,32,128]{3,2,1,0:T(8,128)}), f32[4,4,32,128]{3,2,1,0:T(8,128)S(1)}, u32[]{:S(2)}, u32[]{:S(2)}) async-start(f32[4,4,32,128]{3,2,1,0:T(8,128)} %bitcast.10), calls=%async_computation.3 | async-start | bytes 524288 | tf_op jit(solution)/shard_map/all_to_all | solution.py:306
  160.6 53.4 %copy-start.4 = (f32[3,32,32]{2,1,0:T(8,128)S(1)}, f32[3,32,32]{2,1,0:T(8,128)}, u32[]{:S(2)}) copy-start(f32[3,32,32]{2,1,0:T(8,128)} %get-tuple-element.15.p_factor) | copy-start | bytes 36868
  205.2 8.9 %collective-permute-start.13 = (bf16[4,16,32,128]{3,2,1,0:T(8,128)(2,1)S(1)}, bf16[4,16,32,128]{3,2,1,0:T(8,128)(2,1)S(1)}, u32[]{:S(2)}, u32[]{:S(2)}) collective-permute-start(bf16[4,16,32,128]{3,2,1,0:T(8,128)(2,1)S(1)} %bitcast.22), channel_id=1, source_target_pairs={{0,1},{1,0},{2,3},{3,2},{4,5},{5,4},{6,7},{7,6},{8,9},{9,8},{10,11... | collective-permute-start | bytes 1572872 | tf_op jit(solution)/shard_map/ppermute | solution.py:243

commit v4 on v0

v4 whole, which is shorter than its diff:
```python
import jax
import jax.numpy as jnp
from jax import lax
from jax.experimental import pallas as pl
from jax.experimental.pallas import tpu as pltpu
from jax.sharding import Mesh, PartitionSpec as P

NY, NZ, NX, NC = 4, 16, 4, 2
SHARDS = NX * NC
D = 5120
RANK = 32
ROWS = 32
TOK = 1024
OWN = TOK // SHARDS
HALF = D // NC
PIECE = HALF // NX
BLOCKS = PIECE // 128
F32, BF16 = jnp.float32, jnp.bfloat16
VMEM_BYTES = 48 * 1024 * 1024
PRECISE = lax.Precision.HIGHEST
SMEM = pl.BlockSpec(memory_space=pltpu.SMEM)
ROWS_ON_ROWS = (((0,), (0,)), ((), ()))
LANES_ON_LANES = (((1,), (1,)), ((), ()))


def params():
    return pltpu.CompilerParams(vmem_limit_bytes=VMEM_BYTES)


def split3(value):
    high = value.astype(BF16)
    rest = value - high.astype(F32)
    middle = rest.astype(BF16)
    low = (rest - middle.astype(F32)).astype(BF16)
    return high, middle, low


def own_lanes(values):
    lane = lax.broadcasted_iota(jnp.int32, values[0].shape, 1)
    first = jnp.where(lane < RANK, values[0], values[1])
    return jnp.where(lane < 2 * RANK, first, jnp.where(lane < 3 * RANK, values[2], 0.0))


def token_kernel(inputs, out_grad, error, q_ref, token_q, error_q):
    @pl.when(pl.program_id(0) == 0)
    def _():
        token_q[...] = jnp.zeros_like(token_q)
        error_q[...] = jnp.zeros_like(error_q)

    width = inputs.shape[1]
    right = jnp.concatenate(
        [q_ref[0], q_ref[1], q_ref[2], jnp.zeros((128 - 3 * RANK, width), BF16)], axis=0
    )
    left = jnp.concatenate([inputs[...], out_grad[...], error[0, 0], error[0, 1], error[0, 2]], axis=0)
    product = lax.dot_general(left, right, LANES_ON_LANES, preferred_element_type=F32)
    of_inputs, of_out_grad, of_error = product[:OWN], product[OWN : 2 * OWN], product[2 * OWN :]
    token_q[...] += own_lanes([of_inputs, of_inputs, of_out_grad])
    error_q[...] += own_lanes([of_error[m * ROWS : (m + 1) * ROWS] for m in range(3)])


def token_products(inputs, out_grad, error, q_start):
    steps = 4
    width = D // steps
    x_spec = pl.BlockSpec((OWN, width), lambda i: (0, i))
    return pl.pallas_call(
        token_kernel,
        grid=(steps,),
        in_specs=[
            x_spec,
            x_spec,
            pl.BlockSpec((1, 3, ROWS, width), lambda i: (0, 0, 0, i)),
            pl.BlockSpec((3, RANK, width), lambda i: (0, 0, i)),
        ],
        out_specs=[
            pl.BlockSpec((OWN, 128), lambda i: (0, 0)),
            pl.BlockSpec((ROWS, 128), lambda i: (0, 0)),
        ],
        out_shape=[
            jax.ShapeDtypeStruct((OWN, 128), F32),
            jax.ShapeDtypeStruct((ROWS, 128), F32),
        ],
        compiler_params=params(),
        name="token_products",
    )(inputs, out_grad, error, q_start)


def left_kernel(shard_ref, units, token_q, error_q, p_part):
    rows = units[...].reshape(SHARDS * 3 * ROWS, OWN)
    product = jnp.zeros((SHARDS * 3 * ROWS, 128), F32)
    for part in split3(token_q[...])[::-1]:
        product = product + jnp.dot(rows, part, preferred_element_type=F32)
    for shard in range(SHARDS):
        at = shard * 3 * ROWS
        p_part[shard * ROWS : (shard + 1) * ROWS] = own_lanes(
            [product[at + m * ROWS : at + (m + 1) * ROWS] for m in range(3)]
        )
    mine = pl.ds(pl.multiple_of(shard_ref[0] * ROWS, ROWS), ROWS)
    p_part[mine] = p_part[mine] + error_q[...]


def left_product(shard, units, token_q, error_q):
    return pl.pallas_call(
        left_kernel,
        in_specs=[SMEM] + [pl.BlockSpec(memory_space=pltpu.VMEM)] * 3,
        out_shape=jax.ShapeDtypeStruct((SHARDS * ROWS, 128), F32),
        compiler_params=params(),
        name="left_product",
    )(shard, units, token_q, error_q)


def right_kernel(
    place, p_sum, units, x_near, x_away, o_near, o_away, e_near, e_away, near, away, token_p, error_p
):
    @pl.when(pl.program_id(0) == 0)
    def _():
        parts = split3(p_sum[...])
        for m in range(3):
            columns = jnp.concatenate(
                [units[shard, m * ROWS : (m + 1) * ROWS] for shard in range(SHARDS)], axis=0
            )
            total = jnp.zeros((128, OWN), F32)
            for part in parts[::-1]:
                total = total + lax.dot_general(
                    part, columns, ROWS_ON_ROWS, preferred_element_type=F32
                )
            token_p[m * RANK : (m + 1) * RANK] = jnp.concatenate(
                split3(total[m * RANK : (m + 1) * RANK]), axis=1
            )
        mine = p_sum[pl.ds(pl.multiple_of(place[1] * ROWS, ROWS), ROWS)]
        error_p[...] = jnp.concatenate(split3(mine), axis=0)

    for out, x_ref, o_ref, e_ref in ((near, x_near, o_near, e_near), (away, x_away, o_away, e_away)):
        branch = jnp.dot(
            token_p[: 2 * RANK], jnp.concatenate([x_ref[...]] * 3, axis=0), preferred_element_type=F32
        )
        down = jnp.dot(
            token_p[2 * RANK :], jnp.concatenate([o_ref[...]] * 3, axis=0), preferred_element_type=F32
        )
        for m, product in enumerate((branch[:RANK], branch[RANK:], down)):
            of_error = lax.dot_general(
                error_p[...],
                jnp.concatenate([e_ref[0, m]] * 3, axis=0),
                ROWS_ON_ROWS,
                preferred_element_type=F32,
            )
            product = product + of_error[m * RANK : (m + 1) * RANK]
            for block in range(BLOCKS):
                unit = m * BLOCKS + block
                out[0, unit // 4, unit % 4] = product[:, block * 128 : (block + 1) * 128]
        out[0, NY - 1, 3] = jnp.zeros((RANK, 128), F32)


def right_product(place, p_sum, units, inputs, out_grad, error):
    x_near = pl.BlockSpec((OWN, PIECE), lambda i, at: (0, at[0] * NX + i))
    x_away = pl.BlockSpec((OWN, PIECE), lambda i, at: (0, (1 - at[0]) * NX + i))
    e_near = pl.BlockSpec((1, 3, ROWS, PIECE), lambda i, at: (0, 0, 0, at[0] * NX + i))
    e_away = pl.BlockSpec((1, 3, ROWS, PIECE), lambda i, at: (0, 0, 0, (1 - at[0]) * NX + i))
    out_spec = pl.BlockSpec((1, NY, 4, RANK, 128), lambda i, at: (i, 0, 0, 0, 0))
    out_shape = jax.ShapeDtypeStruct((NX, NY, 4, RANK, 128), F32)
    return pl.pallas_call(
        right_kernel,
        grid_spec=pltpu.PrefetchScalarGridSpec(
            num_scalar_prefetch=1,
            grid=(NX,),
            in_specs=[
                pl.BlockSpec((SHARDS * ROWS, 128), lambda i, at: (0, 0)),
                pl.BlockSpec((SHARDS, 3 * ROWS, OWN), lambda i, at: (0, 0, 0)),
                x_near,
                x_away,
                x_near,
                x_away,
                e_near,
                e_away,
            ],
            out_specs=[out_spec, out_spec],
            scratch_shapes=[
                pltpu.VMEM((3 * RANK, 3 * OWN), BF16),
                pltpu.VMEM((3 * ROWS, 128), BF16),
            ],
        ),
        out_shape=[out_shape, out_shape],
        compiler_params=params(),
        name="right_product",
    )(place, p_sum, units, inputs, inputs, out_grad, out_grad, error, error)


def factor_kernel(place, p_sum, inverse, p_factor):
    lane = lax.broadcasted_iota(jnp.int32, (3, RANK, RANK), 2)
    row = lax.broadcasted_iota(jnp.int32, (3, RANK, RANK), 1)
    whole = p_sum[...]
    gram = lax.dot_general(
        whole, whole, ROWS_ON_ROWS, preferred_element_type=F32, precision=PRECISE
    )

    def columns_of(value, m):
        return (pltpu.roll(value, 128 - RANK * m, 1) if m else value)[:, :RANK]

    left = jnp.stack([columns_of(gram[m * RANK : (m + 1) * RANK], m) for m in range(3)])
    right = jnp.where(lane == row, 1.0, 0.0).astype(F32)
    for step in range(RANK):
        pivot = left[:, step : step + 1, :]
        column = left[:, :, step : step + 1] / pivot[:, :, step : step + 1]
        scale = jnp.where(row[:, :, :1] > step, column, 0.0)
        right = right - scale * right[:, step : step + 1, :]
        left = left - scale * pivot
    diagonal = jnp.sum(jnp.where(lane == row, left, 0.0), axis=2, keepdims=True)
    result = right / jnp.sqrt(diagonal)
    inverse[...] = result
    mine = p_sum[pl.ds(pl.multiple_of(place[1] * ROWS, ROWS), ROWS)]
    for m in range(3):
        p_factor[m] = lax.dot_general(
            columns_of(mine, m),
            result[m],
            LANES_ON_LANES,
            preferred_element_type=F32,
            precision=PRECISE,
        )


def factors(place, p_sum):
    shape = jax.ShapeDtypeStruct((3, RANK, RANK), F32)
    return pl.pallas_call(
        factor_kernel,
        in_specs=[SMEM, pl.BlockSpec(memory_space=pltpu.VMEM)],
        out_shape=[shape, shape],
        compiler_params=params(),
        name="factors",
    )(place, p_sum)


def scale_kernel(place, received, inverse, q_part):
    for slot in range(4):
        unit = place[2] * 4 + slot
        of_unit = jnp.where(
            unit < BLOCKS, inverse[0], jnp.where(unit < 2 * BLOCKS, inverse[1], inverse[2])
        )
        total = received[0, slot]
        for source in range(1, NX * NY):
            total = total + received[source, slot]
        q_part[slot] = jnp.dot(of_unit, total, preferred_element_type=F32, precision=PRECISE)


def scaled_sum(place, received, inverse):
    return pl.pallas_call(
        scale_kernel,
        in_specs=[SMEM] + [pl.BlockSpec(memory_space=pltpu.VMEM)] * 2,
        out_shape=jax.ShapeDtypeStruct((4, RANK, 128), F32),
        compiler_params=params(),
        name="scaled_sum",
    )(place, received, inverse)


def gradient_kernel(columns, tokens, error, matrices):
    product = jnp.dot(columns[...], tokens[...], preferred_element_type=F32)
    for k in range(matrices.shape[0]):
        matrices[k] = product[k * ROWS : (k + 1) * ROWS] + error[0, k].astype(F32)


def gradients(columns, tokens, error):
    count = columns.shape[0] // ROWS
    steps = 10
    width = D // steps
    first = 0 if count == 2 else 2
    return pl.pallas_call(
        gradient_kernel,
        grid=(steps,),
        in_specs=[
            pl.BlockSpec((count * ROWS, TOK), lambda i: (0, 0)),
            pl.BlockSpec((TOK, width), lambda i: (0, i)),
            pl.BlockSpec((1, count, ROWS, width), lambda i: (0, first // count, 0, i)),
        ],
        out_specs=pl.BlockSpec((count, ROWS, width), lambda i: (0, 0, i)),
        out_shape=jax.ShapeDtypeStruct((count, ROWS, D), F32),
        compiler_params=params(),
        name="gradients",
    )(columns, tokens, error)


def spread(value, axis, count):
    copies = jnp.broadcast_to(value[None], (count,) + value.shape)
    return lax.all_to_all(copies, axis, 0, 0)


def swap_core(value):
    return lax.ppermute(value, "c", [(0, 1), (1, 0)])


def error_kernel(place, q_near, q_far, p_factor, branch, down, q_factor, error_next):
    first = place[0] == 0
    for m in range(3):
        left = jnp.concatenate(split3(p_factor[m]), axis=1)
        for at in range(NX):
            units = range(m * BLOCKS, (m + 1) * BLOCKS)
            near = jnp.concatenate([q_near[at, unit] for unit in units], axis=1)
            away = jnp.concatenate([q_far[at, unit] for unit in units], axis=1)
            halves = jnp.where(first, near, away), jnp.where(first, away, near)
            for half, right in enumerate(halves):
                columns = slice(half * HALF + at * PIECE, half * HALF + (at + 1) * PIECE)
                q_factor[m, :, columns] = right
                rebuilt = jnp.dot(
                    left, jnp.concatenate([right] * 3, axis=0), preferred_element_type=F32
                )
                value = branch[m, :, columns] if m < 2 else down[0, :, columns]
                error_next[0, m, :, columns] = (value - rebuilt).astype(BF16)


def new_error(place, q_near, q_far, p_factor, branch, down):
    return pl.pallas_call(
        error_kernel,
        in_specs=[SMEM] + [pl.BlockSpec(memory_space=pltpu.VMEM)] * 5,
        out_shape=[
            jax.ShapeDtypeStruct((3, RANK, D), BF16),
            jax.ShapeDtypeStruct((1, 3, ROWS, D), BF16),
        ],
        compiler_params=params(),
        name="new_error",
    )(place, q_near, q_far, p_factor, branch, down)


def per_device(inputs, out_grad, hidden, up_grad, gate_grad, error_memory, q_start):
    core, row = lax.axis_index("c"), lax.axis_index("y")
    shard = lax.axis_index("x") * NC + core
    place = jnp.stack([core, shard, row]).astype(jnp.int32)
    tensor, scatter = ("x", "c"), ("x", "c", "y")
    all_inputs = lax.all_gather(inputs, tensor, axis=0, tiled=True)
    all_out_grad = lax.all_gather(out_grad, tensor, axis=0, tiled=True)

    columns = jnp.concatenate([up_grad.T, gate_grad.T, hidden.T], axis=0)
    units = columns.reshape(3 * ROWS, SHARDS, OWN).transpose(1, 0, 2)
    units = lax.all_to_all(units, tensor, 0, 0)
    token_q, error_q = token_products(inputs, out_grad, error_memory, q_start)
    p_part = left_product(place[1:2], units, token_q, error_q)
    p_rows = lax.all_to_all(p_part.reshape(SHARDS * NY, 8, 128), scatter, 0, 0).sum(0)
    p_rows = spread(p_rows, "z", NZ).sum(0)
    p_sum = spread(p_rows, scatter, SHARDS * NY).reshape(SHARDS * ROWS, 128)

    near, away = right_product(place, p_sum, units, inputs, out_grad, error_memory)
    w_core = (near + swap_core(away)).reshape(NX * NY, 4, RANK, 128)
    inverse, p_factor = factors(place, p_sum)
    received = lax.all_to_all(w_core, ("x", "y"), 0, 0)
    q_y = scaled_sum(place, received, inverse)
    q_z = lax.all_to_all(q_y.reshape(NZ, 8, 128), "z", 0, 0).sum(0)
    q_part = (q_z / (NY * NZ)).astype(BF16)

    q_dp = spread(q_part, "z", NZ).reshape(4, RANK, 128)
    q_near = spread(q_dp, ("x", "y"), NX * NY).reshape(NX, NY * 4, RANK, 128)

    branch = gradients(columns[: 2 * ROWS], all_inputs, error_memory)
    down = gradients(columns[2 * ROWS :], all_out_grad, error_memory)
    q_factor, error_next = new_error(place, q_near, swap_core(q_near), p_factor, branch, down)
    return (error_next, p_factor, q_factor)


def solution(mesh):
    fine = Mesh(mesh.devices.reshape(NY, NZ, NX, NC), ("y", "z", "x", "c"))
    dp, tensor = ("y", "z"), ("x", "c")
    in_specs = (
        P(dp + tensor, None),
        P(dp + tensor, None),
        P(dp, tensor),
        P(dp, tensor),
        P(dp, tensor),
        P(dp, None, tensor, None),
        P(),
    )
    out_specs = (P(dp, None, tensor, None), P(None, tensor, None), P())
    return jax.shard_map(
        per_device, mesh=fine, in_specs=in_specs, out_specs=out_specs, check_vma=False
    )
```

time: 957 us -> 188 us (0.20)
  waiting for transfers between devices: 600 us -> 26.7 us
  blocking collectives: 301 us -> 80.5 us
  Pallas kernels: 0 us -> 30.6 us
  starting transfers between devices: 0.11 us -> 27.1 us
  matrix products: 20.6 us -> 0 us
  other arithmetic: 18.3 us -> 2.91 us
    psum x1 -> x0, waiting for transfers between devices: 463 us -> none  [per_device(): q_sum = lax.psum(q_part, ('dp', 'tensor'))]
    psum x2 -> x0, blocking collectives: 301 us -> none  [the longest x1 225 us: per_device(): p_local = lax.psum(p_part, 'dp')]
    all_gather x2, waiting for transfers between devices: 135 us -> 0.04 us  [the longest x1 0.02 us: per_device(): all_out_grad = lax.all_gather(out_grad, tensor, axis=0, tiled=True)]
    all_to_all x0 -> x5, blocking collectives: none -> 80.5 us  [the longest x3 54.1 us: spread(): return lax.all_to_all(copies, axis, 0, 0)]
    pallas_call x0 -> x8, Pallas kernels: none -> 30.6 us  [the longest x2 16.6 us: gradients(): pl.pallas_call(gradient_kernel, grid=(steps,), in_specs=[pl.BlockSpec((co...]
    all_to_all x0 -> x3, waiting for transfers between devices: none -> 23.1 us  [the longest x1 12.1 us: per_device(): received = lax.all_to_all(w_core, ('x', 'y'), 0, 0)]
    dot_general x6 -> x0, matrix products: 20.3 us -> none  [the longest x1 6.72 us: per_device(): jnp.dot(hidden.T, lax.all_gather(out_grad, 'tensor', axis=0, tiled=True),...]
    all_to_all x0 -> x3, starting transfers between devices: none -> 19.6 us  [the longest x1 10.2 us: per_device(): units = lax.all_to_all(units, tensor, 0, 0)]
  transfers between devices with their start and end apart: 3 -> 7, of which waited for: 3 -> 4; matrix products, arithmetic and copies ran while one was open for 1% -> 2% of each run, Pallas kernels for 0% -> 15%
where the time goes in v4:
time: 188 us; the launch traced here: 187 us
  blocking collectives  80.5 us (43%)
  Pallas kernels  30.6 us (16%)
  starting transfers between devices  27.1 us (14%)
  waiting for transfers between devices  26.7 us (14%)
  between operations  14.3 us (8%)
  local copies, waits for them, and re-layouts  4.91 us (3%)
  other arithmetic  2.91 us (2%)
    all_to_all x3, blocking collectives, spread(): return lax.all_to_all(copies, axis, 0, 0)  54.1 us
    pallas_call x2, Pallas kernels, gradients(): pl.pallas_call(gradient_kernel, grid=(steps,), in_specs=[pl.BlockSpec((co...  16.6 us
    all_to_all x1, blocking collectives, per_device(): q_z = lax.all_to_all(q_y.reshape(NZ, 8, 128), 'z', 0, 0).sum(0)  15.2 us
    all_to_all x1, waiting for transfers between devices, per_device(): received = lax.all_to_all(w_core, ('x', 'y'), 0, 0)  12.1 us
    all_to_all x1, blocking collectives, per_device(): lax.all_to_all(p_part.reshape(SHARDS * NY, 8, 128), scatter, 0, 0).sum(0)  11.3 us
    all_to_all x1, starting transfers between devices, per_device(): units = lax.all_to_all(units, tensor, 0, 0)  10.2 us
    all_to_all x1, waiting for transfers between devices, spread(): return lax.all_to_all(copies, axis, 0, 0)  8.96 us
    ppermute x2, starting transfers between devices, swap_core(): return lax.ppermute(value, 'c', [(0, 1), (1, 0)])  7.48 us
  transfers between devices with their start and end apart: 7, of which 4 were waited for; matrix products, arithmetic and copies ran while one was open for 2% of the time, Pallas kernels for 15%

profile of v4, /device:TPU:1, one launch (start us, length us, event | category | flops | bytes accessed | tf_op | source)
XLA Modules:
  0.0 187.1 jit_solution(12952195746410796795)
XLA Ops:
  7.2 0.0 copy-start.9
  7.2 0.0 copy-start.5
  7.2 0.0 all-gather.5.cloned.1.call-start
  7.2 0.0 copy-start.1
  7.2 0.7 all-gather.5.cloned.1.call-update
  7.9 0.0 copy-start
  7.9 0.0 copy-start.4
  7.9 0.0 all-gather.3.cloned.1.call-start
  8.0 0.7 all-gather.3.cloned.1.call-update
  8.7 0.0 copy-done.9
  8.7 0.0 copy-done.5
  8.7 1.6 bitcast_bitcast_fusion
  10.3 10.2 %all-to-all-start = ((bf16[8,96,128]{2,1,0:T(8,128)(2,1)}), bf16[8,96,128]{2,1,0:T(8,128)(2,1)S(1)}, u32[]{:S(2)}, u32[]{:S(2)}) async-start(bf16[8,96,128]{2,1,0:T(8,128)(2,1)} %bitcast_bitcast_fusion), calls=%async_computation | async-start | bytes 393216 | tf_op jit(solution)/shard_map/all_to_all | solution.py:330
  20.4 0.0 copy-done.1
  20.4 0.0 copy-done
  20.4 0.0 copy-done.4
  20.5 0.0 copy-start.2
  20.5 1.3 copy-done.2
  21.8 2.0 %token_products.1 = (f32[128,128]{1,0:T(8,128)S(1)}, f32[32,128]{1,0:T(8,128)S(1)}) custom-call(bf16[128,5120]{1,0:T(8,128)(2,1)S(1)} %copy-done.2, bf16[128,5120]{1,0:T(8,128)(2,1)S(1)} %copy-done.1, bf16[1,3,32,5120]{3,2,1,0:T(8,128)(2,1)S(1)} %copy-done, bf16[3,32,5120]{2,1,0:T(8,128)(2,1)S(1)} %copy-done.4), custom_call_target="tpu_custom_call" | custom-call | tf_op jit(solution)/shard_map/token_products/pallas_call | solution.py:65
  23.7 0.0 copy-start.6
  23.8 0.6 copy-done.6
  24.4 2.0 %all-to-all-done.units = bf16[8,96,128]{2,1,0:T(8,128)(2,1)S(1)} async-done(((bf16[8,96,128]{2,1,0:T(8,128)(2,1)}), bf16[8,96,128]{2,1,0:T(8,128)(2,1)S(1)}, u32[]{:S(2)}, u32[]{:S(2)}) %all-to-all-start) | async-done | bytes 196640 | tf_op jit(solution)/shard_map/all_to_all | solution.py:330
  26.3 0.0 copy-start.7
  26.3 0.8 copy-done.7
  27.2 0.3 left_product.1
  27.5 11.3 %all_to_all.40 = f32[32,8,128]{2,1,0:T(8,128)S(1)} all-to-all(f32[32,8,128]{2,1,0:T(8,128)S(1)} %bitcast.23), channel_id=1, replica_groups=mesh['y'=4,'z'=16,'x'=4,'c'=2] {'x','c','y'}, dimensions={0} | all-to-all | bytes 262144 | tf_op jit(solution)/shard_map/all_to_all | solution.py:333
  38.8 24.2 %all_to_all.41 = f32[16,8,128]{2,1,0:T(8,128)S(1)} all-to-all(f32[16,8,128]{2,1,0:T(8,128)S(1)} %broadcast_in_dim.10), channel_id=1, replica_groups=mesh['y'=4,'z'=16,'x'=4,'c'=2] {'z'}, dimensions={0} | all-to-all | bytes 131072 | tf_op jit(solution)/shard_map/all_to_all | solution.py:281
  63.0 0.7 broadcast_in_dim.11
  63.7 5.8 %all-to-all-start.3 = ((f32[32,8,128]{2,1,0:T(8,128)}), f32[32,8,128]{2,1,0:T(8,128)S(1)}, u32[]{:S(2)}, u32[]{:S(2)}) async-start(f32[32,8,128]{2,1,0:T(8,128)} %broadcast_in_dim.11), calls=%async_computation.3 | async-start | bytes 262144 | tf_op jit(solution)/shard_map/all_to_all | solution.py:281
  69.5 0.1 pad_add_fusion.place
  69.5 9.0 %all-to-all-done.3 = f32[32,8,128]{2,1,0:T(8,128)S(1)} async-done(((f32[32,8,128]{2,1,0:T(8,128)}), f32[32,8,128]{2,1,0:T(8,128)S(1)}, u32[]{:S(2)}, u32[]{:S(2)}) %all-to-all-start.3) | async-done | bytes 131104 | tf_op jit(solution)/shard_map/all_to_all | solution.py:281
  78.5 0.0 copy-start.3
  78.5 1.3 copy-done.3
  79.8 4.3 %right_product.1 = (f32[4,4,4,32,128]{4,3,2,1,0:T(8,128)S(1)}, f32[4,4,4,32,128]{4,3,2,1,0:T(8,128)S(1)}) custom-call(s32[3]{0:T(128)S(1)} %pad_add_fusion.place, f32[256,128]{1,0:T(8,128)S(1)} %bitcast.21, bf16[8,96,128]{2,1,0:T(8,128)(2,1)S(1)} %all-to-all-done.units, bf16[128,5120]{1,0:T(8,128)(2,1)S(1)} %copy-done.3, bf16[128,5120]{1,0:T(8,128)(2,1)S(1)} %copy-done.3, ...), custom_call_target="tpu_custom_call" | custom-call | tf_op jit(solution)/shard_map/right_product/pallas_call | solution.py:160
  84.1 2.6 %collective-permute-start = (f32[4,4,4,32,128]{4,3,2,1,0:T(8,128)S(1)}, f32[4,4,4,32,128]{4,3,2,1,0:T(8,128)S(1)}, u32[]{:S(2)}, u32[]{:S(2)}) collective-permute-start(f32[4,4,4,32,128]{4,3,2,1,0:T(8,128)S(1)} %get-tuple-element.14), channel_id=1, source_target_pairs={{0,1},{1,0},{2,3},{3,2},{4,5},{5,4},{6,7},{7,6},{8,9},{9,8},{10,11... | collective-permute-start | bytes 3145736 | tf_op jit(solution)/shard_map/ppermute | solution.py:285
  86.7 2.3 %collective-permute-done = f32[4,4,4,32,128]{4,3,2,1,0:T(8,128)S(1)} collective-permute-done((f32[4,4,4,32,128]{4,3,2,1,0:T(8,128)S(1)}, f32[4,4,4,32,128]{4,3,2,1,0:T(8,128)S(1)}, u32[]{:S(2)}, u32[]{:S(2)}) %collective-permute-start) | collective-permute-done | bytes 1048608 | tf_op jit(solution)/shard_map/ppermute | solution.py:285
  88.9 1.2 add.7
  90.1 3.7 %all-to-all-start.4 = ((f32[16,4,32,128]{3,2,1,0:T(8,128)}), f32[16,4,32,128]{3,2,1,0:T(8,128)S(1)}, u32[]{:S(2)}, u32[]{:S(2)}) async-start(f32[16,4,32,128]{3,2,1,0:T(8,128)} %bitcast.27), calls=%async_computation.4 | async-start | bytes 2097152 | tf_op jit(solution)/shard_map/all_to_all | solution.py:340
  93.8 4.4 %factors.1 = (f32[3,32,32]{2,1,0:T(8,128)S(1)}, f32[3,32,32]{2,1,0:T(8,128)}) custom-call(s32[3]{0:T(128)S(1)} %pad_add_fusion.place, f32[256,128]{1,0:T(8,128)S(1)} %bitcast.22), custom_call_target="tpu_custom_call" | custom-call | tf_op jit(solution)/shard_map/factors/pallas_call | solution.py:222
  98.2 12.1 %all-to-all-done.4.received = f32[16,4,32,128]{3,2,1,0:T(8,128)S(1)} async-done(((f32[16,4,32,128]{3,2,1,0:T(8,128)}), f32[16,4,32,128]{3,2,1,0:T(8,128)S(1)}, u32[]{:S(2)}, u32[]{:S(2)}) %all-to-all-start.4) | async-done | bytes 1048608 | tf_op jit(solution)/shard_map/all_to_all | solution.py:340
  110.3 0.0 copy-start.10
  110.3 0.8 scaled_sum.1
  111.1 0.0 copy-start.11
  111.1 15.2 %all_to_all.42 = f32[16,8,128]{2,1,0:T(8,128)S(1)} all-to-all(f32[16,8,128]{2,1,0:T(8,128)S(1)} %bitcast.26), channel_id=1, replica_groups=mesh['y'=4,'z'=16,'x'=4,'c'=2] {'z'}, dimensions={0} | all-to-all | bytes 131072 | tf_op jit(solution)/shard_map/all_to_all | solution.py:342
  126.3 14.4 %all_to_all.43 = bf16[16,8,128]{2,1,0:T(8,128)(2,1)S(1)} all-to-all(bf16[16,8,128]{2,1,0:T(8,128)(2,1)S(1)} %broadcast_in_dim.12), channel_id=1, replica_groups=mesh['y'=4,'z'=16,'x'=4,'c'=2] {'z'}, dimensions={0} | all-to-all | bytes 65536 | tf_op jit(solution)/shard_map/all_to_all | solution.py:281
  140.7 0.1 broadcast_in_dim.14
  140.8 15.5 %all_to_all.44 = bf16[16,4,32,128]{3,2,1,0:T(8,128)(2,1)S(1)} all-to-all(bf16[16,4,32,128]{3,2,1,0:T(8,128)(2,1)S(1)} %broadcast_in_dim.14), channel_id=1, replica_groups=mesh['y'=4,'z'=16,'x'=4,'c'=2] {'x','y'}, dimensions={0} | all-to-all | bytes 1048576 | tf_op jit(solution)/shard_map/all_to_all | solution.py:281
  156.3 4.9 %collective-permute-start.1 = (bf16[4,16,32,128]{3,2,1,0:T(8,128)(2,1)S(1)}, bf16[4,16,32,128]{3,2,1,0:T(8,128)(2,1)S(1)}, u32[]{:S(2)}, u32[]{:S(2)}) collective-permute-start(bf16[4,16,32,128]{3,2,1,0:T(8,128)(2,1)S(1)} %bitcast.19), channel_id=1, source_target_pairs={{0,1},{1,0},{2,3},{3,2},{4,5},{5,4},{6,7},{7,6},{8,9},{9,8},{10,11... | collective-permute-start | bytes 1572872 | tf_op jit(solution)/shard_map/ppermute | solution.py:285
  161.2 0.0 copy-done.10
  161.2 0.0 copy-done.11
  161.2 0.0 all-gather.5.cloned.1.call-done.tokens
  161.2 8.3 %gradients.3.down = f32[1,32,5120]{2,1,0:T(8,128)S(1)} custom-call(bf16[32,1024]{1,0:T(8,128)(2,1)S(1)} %bitcast.25, bf16[1024,5120]{1,0:T(8,128)(2,1)} %all-gather.5.cloned.1.call-done.tokens, bf16[1,3,32,5120]{3,2,1,0:T(8,128)(2,1)S(1)} %copy-done), custom_call_target="tpu_custom_call" | custom-call | tf_op jit(solution)/shard_map/gradients/pallas_call | solution.py:264
  169.5 0.0 copy-start.8
  169.5 0.0 all-gather.3.cloned.1.call-done.tokens
  169.6 8.3 %gradients.2.branch = f32[2,32,5120]{2,1,0:T(8,128)S(1)} custom-call(bf16[64,1024]{1,0:T(8,128)(2,1)S(1)} %pad_maximum_fusion.columns, bf16[1024,5120]{1,0:T(8,128)(2,1)} %all-gather.3.cloned.1.call-done.tokens, bf16[1,3,32,5120]{3,2,1,0:T(8,128)(2,1)S(1)} %copy-done), custom_call_target="tpu_custom_call" | custom-call | tf_op jit(solution)/shard_map/gradients/pallas_call | solution.py:264
  177.9 0.0 collective-permute-done.1.q_far
  177.9 0.0 copy-done.8
  178.0 2.3 %new_error.1 = (bf16[3,32,5120]{2,1,0:T(8,128)(2,1)}, bf16[1,3,32,5120]{3,2,1,0:T(8,128)(2,1)}) custom-call(s32[3]{0:T(128)S(1)} %pad_add_fusion.place, bf16[4,16,32,128]{3,2,1,0:T(8,128)(2,1)S(1)} %bitcast.20, bf16[4,16,32,128]{3,2,1,0:T(8,128)(2,1)S(1)} %collective-permute-done.1.q_far, f32[3,32,32]{2,1,0:T(8,128)S(1)} %copy-done.8, ...), custom_call_target="tpu_custom_call" | custom-call | tf_op jit(solution)/shard_map/new_error/pallas_call | solution.py:308
  (7 shorter events, 0.1 us)
Async XLA Ops:
  7.2 1.5 copy-start.9
  7.2 1.5 copy-start.5
  7.2 154.1 %all-gather.5.cloned.1.call-start = ((), (), s32[]{:S(2)}) async-start(), calls=%async_computation.9 | async-start | bytes 11796480 | tf_op jit(solution)/shard_map/all_gather | solution.py:326
  7.2 13.2 %copy-start.1 = (bf16[128,5120]{1,0:T(8,128)(2,1)S(1)}, bf16[128,5120]{1,0:T(8,128)(2,1)}, u32[]{:S(2)}) copy-start(bf16[128,5120]{1,0:T(8,128)(2,1)} %o_away.1) | copy-start | bytes 3932164
  7.9 12.5 %copy-start = (bf16[1,3,32,5120]{3,2,1,0:T(8,128)(2,1)S(1)}, bf16[1,3,32,5120]{3,2,1,0:T(8,128)(2,1)}, u32[]{:S(2)}) copy-start(bf16[1,3,32,5120]{3,2,1,0:T(8,128)(2,1)} %error.5) | copy-start | bytes 2949124
  7.9 12.5 %copy-start.4 = (bf16[3,32,5120]{2,1,0:T(8,128)(2,1)S(1)}, bf16[3,32,5120]{2,1,0:T(8,128)(2,1)}, u32[]{:S(2)}) copy-start(bf16[3,32,5120]{2,1,0:T(8,128)(2,1)} %q_ref.1) | copy-start | bytes 2949124
  7.9 161.6 %all-gather.3.cloned.1.call-start = ((), (), s32[]{:S(2)}) async-start(), calls=%async_computation.8 | async-start | bytes 11796480 | tf_op jit(solution)/shard_map/all_gather | solution.py:325
  10.3 16.1 %all-to-all-start = ((bf16[8,96,128]{2,1,0:T(8,128)(2,1)}), bf16[8,96,128]{2,1,0:T(8,128)(2,1)S(1)}, u32[]{:S(2)}, u32[]{:S(2)}) async-start(bf16[8,96,128]{2,1,0:T(8,128)(2,1)} %bitcast_bitcast_fusion), calls=%async_computation | async-start | bytes 393216 | tf_op jit(solution)/shard_map/all_to_all | solution.py:330
  20.5 1.3 copy-start.2
  23.7 0.6 copy-start.6
  26.3 0.8 copy-start.7
  63.7 14.8 %all-to-all-start.3 = ((f32[32,8,128]{2,1,0:T(8,128)}), f32[32,8,128]{2,1,0:T(8,128)S(1)}, u32[]{:S(2)}, u32[]{:S(2)}) async-start(f32[32,8,128]{2,1,0:T(8,128)} %broadcast_in_dim.11), calls=%async_computation.3 | async-start | bytes 262144 | tf_op jit(solution)/shard_map/all_to_all | solution.py:281
  78.5 1.3 copy-start.3
  84.1 4.9 %collective-permute-start = (f32[4,4,4,32,128]{4,3,2,1,0:T(8,128)S(1)}, f32[4,4,4,32,128]{4,3,2,1,0:T(8,128)S(1)}, u32[]{:S(2)}, u32[]{:S(2)}) collective-permute-start(f32[4,4,4,32,128]{4,3,2,1,0:T(8,128)S(1)} %get-tuple-element.14), channel_id=1, source_target_pairs={{0,1},{1,0},{2,3},{3,2},{4,5},{5,4},{6,7},{7,6},{8,9},{9,8},{10,11... | collective-permute-start | bytes 3145736 | tf_op jit(solution)/shard_map/ppermute | solution.py:285
  90.1 20.2 %all-to-all-start.4 = ((f32[16,4,32,128]{3,2,1,0:T(8,128)}), f32[16,4,32,128]{3,2,1,0:T(8,128)S(1)}, u32[]{:S(2)}, u32[]{:S(2)}) async-start(f32[16,4,32,128]{3,2,1,0:T(8,128)} %bitcast.27), calls=%async_computation.4 | async-start | bytes 2097152 | tf_op jit(solution)/shard_map/all_to_all | solution.py:340
  110.3 50.9 %copy-start.10 = (bf16[1024,32]{0,1:T(8,128)(2,1)S(1)}, bf16[1024,32]{0,1:T(8,128)(2,1)}, u32[]{:S(2)}) copy-start(bf16[1024,32]{0,1:T(8,128)(2,1)} %param.11) | copy-start | bytes 196612
  111.1 50.1 %copy-start.11 = (bf16[1024,32]{0,1:T(8,128)(2,1)S(1)}, bf16[1024,32]{0,1:T(8,128)(2,1)}, u32[]{:S(2)}) copy-start(bf16[1024,32]{0,1:T(8,128)(2,1)} %param.10) | copy-start | bytes 196612
  156.3 21.7 %collective-permute-start.1 = (bf16[4,16,32,128]{3,2,1,0:T(8,128)(2,1)S(1)}, bf16[4,16,32,128]{3,2,1,0:T(8,128)(2,1)S(1)}, u32[]{:S(2)}, u32[]{:S(2)}) collective-permute-start(bf16[4,16,32,128]{3,2,1,0:T(8,128)(2,1)S(1)} %bitcast.19), channel_id=1, source_target_pairs={{0,1},{1,0},{2,3},{3,2},{4,5},{5,4},{6,7},{7,6},{8,9},{9,8},{10,11... | collective-permute-start | bytes 1572872 | tf_op jit(solution)/shard_map/ppermute | solution.py:285
  169.5 8.4 %copy-start.8 = (f32[3,32,32]{2,1,0:T(8,128)S(1)}, f32[3,32,32]{2,1,0:T(8,128)}, u32[]{:S(2)}) copy-start(f32[3,32,32]{2,1,0:T(8,128)} %get-tuple-element.9.p_factor) | copy-start | bytes 36868
Sparse Core Ops, SparseCore 0:
  10.1 73.2 all-gather.4
  85.6 70.5 all-gather.2

commit v5 on v4

--- a/solution.py
+++ b/solution.py
@@ -15,16 +15,18 @@
 HALF = D // NC
 PIECE = HALF // NX
 BLOCKS = PIECE // 128
+TOKEN_STEPS = 2
 F32, BF16 = jnp.float32, jnp.bfloat16
 VMEM_BYTES = 48 * 1024 * 1024
+WIDE_VMEM_BYTES = 60 * 1024 * 1024
 PRECISE = lax.Precision.HIGHEST
 SMEM = pl.BlockSpec(memory_space=pltpu.SMEM)
 ROWS_ON_ROWS = (((0,), (0,)), ((), ()))
 LANES_ON_LANES = (((1,), (1,)), ((), ()))
 
 
-def params():
-    return pltpu.CompilerParams(vmem_limit_bytes=VMEM_BYTES)
+def params(limit=VMEM_BYTES):
+    return pltpu.CompilerParams(vmem_limit_bytes=limit)
 
 
 def split3(value):
@@ -41,11 +43,20 @@
     return jnp.where(lane < 2 * RANK, first, jnp.where(lane < 3 * RANK, values[2], 0.0))
 
 
-def token_kernel(inputs, out_grad, error, q_ref, token_q, error_q):
-    @pl.when(pl.program_id(0) == 0)
+def token_kernel(place, inputs, out_grad, error, q_ref, token_q, error_q, keep, sent):
+    step = pl.program_id(0)
+
+    @pl.when(step == 0)
     def _():
         token_q[...] = jnp.zeros_like(token_q)
         error_q[...] = jnp.zeros_like(error_q)
+
+    for out, wanted in ((keep, step < TOKEN_STEPS // 2), (sent, step >= TOKEN_STEPS // 2)):
+
+        @pl.when(wanted)
+        def _(out=out):
+            out[0] = inputs[...]
+            out[1] = out_grad[...]
 
     width = inputs.shape[1]
     right = jnp.concatenate(
@@ -58,30 +69,42 @@
     error_q[...] += own_lanes([of_error[m * ROWS : (m + 1) * ROWS] for m in range(3)])
 
 
-def token_products(inputs, out_grad, error, q_start):
-    steps = 4
-    width = D // steps
-    x_spec = pl.BlockSpec((OWN, width), lambda i: (0, i))
+def token_products(place, inputs, out_grad, error, q_start):
+    width = D // TOKEN_STEPS
+    half = TOKEN_STEPS // 2
+
+    def column(i, at):
+        return (at[0] * half + i) % TOKEN_STEPS
+
+    x_spec = pl.BlockSpec((OWN, width), lambda i, at: (0, column(i, at)))
+    half_shape = jax.ShapeDtypeStruct((2, OWN, HALF), BF16)
     return pl.pallas_call(
         token_kernel,
-        grid=(steps,),
-        in_specs=[
-            x_spec,
-            x_spec,
-            pl.BlockSpec((1, 3, ROWS, width), lambda i: (0, 0, 0, i)),
-            pl.BlockSpec((3, RANK, width), lambda i: (0, 0, i)),
-        ],
-        out_specs=[
-            pl.BlockSpec((OWN, 128), lambda i: (0, 0)),
-            pl.BlockSpec((ROWS, 128), lambda i: (0, 0)),
-        ],
+        grid_spec=pltpu.PrefetchScalarGridSpec(
+            num_scalar_prefetch=1,
+            grid=(TOKEN_STEPS,),
+            in_specs=[
+                x_spec,
+                x_spec,
+                pl.BlockSpec((1, 3, ROWS, width), lambda i, at: (0, 0, 0, column(i, at))),
+                pl.BlockSpec((3, RANK, width), lambda i, at: (0, 0, column(i, at))),
+            ],
+            out_specs=[
+                pl.BlockSpec((OWN, 128), lambda i, at: (0, 0)),
+                pl.BlockSpec((ROWS, 128), lambda i, at: (0, 0)),
+                pl.BlockSpec((2, OWN, width), lambda i, at: (0, 0, jnp.minimum(i, half - 1))),
+                pl.BlockSpec((2, OWN, width), lambda i, at: (0, 0, jnp.maximum(i - half, 0))),
+            ],
+        ),
         out_shape=[
             jax.ShapeDtypeStruct((OWN, 128), F32),
             jax.ShapeDtypeStruct((ROWS, 128), F32),
+            half_shape,
+            half_shape,
         ],
         compiler_params=params(),
         name="token_products",
-    )(inputs, out_grad, error, q_start)
+    )(place, inputs, out_grad, error, q_start)
 
 
 def left_kernel(shard_ref, units, token_q, error_q, p_part):
@@ -250,30 +273,44 @@
     )(place, received, inverse)
 
 
-def gradient_kernel(columns, tokens, error, matrices):
-    product = jnp.dot(columns[...], tokens[...], preferred_element_type=F32)
-    for k in range(matrices.shape[0]):
-        matrices[k] = product[k * ROWS : (k + 1) * ROWS] + error[0, k].astype(F32)
-
-
-def gradients(columns, tokens, error):
-    count = columns.shape[0] // ROWS
-    steps = 10
-    width = D // steps
-    first = 0 if count == 2 else 2
+def gradient_kernel(near, away, own, sibling, pair, pair_sibling, mine, beside, far):
+    for at, first, last in ((0, 0, 2), (1, 2, 3)):
+        tokens = jnp.concatenate([own[at], sibling[at], pair[at], pair_sibling[at]], axis=0)
+        count = last - first
+        columns = jnp.concatenate(
+            [
+                chip[side * 3 * ROWS + first * ROWS : side * 3 * ROWS + last * ROWS]
+                for chip in (near, away)
+                for side in range(NC)
+            ],
+            axis=0,
+        )
+        product = jnp.dot(columns, tokens, preferred_element_type=F32)
+        for group, out in enumerate((mine, beside, far.at[0], far.at[1])):
+            for k in range(count):
+                start = (group * count + k) * ROWS
+                out[first + k] = product[start : start + ROWS]
+
+
+def gradients(near, away, tokens):
+    steps = 2
+    width = HALF // steps
+    u_spec = pl.BlockSpec((NC * 3 * ROWS, 4 * OWN), lambda i: (0, 0))
+    out_spec = pl.BlockSpec((3, ROWS, width), lambda i: (0, 0, i))
+    shape = jax.ShapeDtypeStruct((3, ROWS, HALF), F32)
     return pl.pallas_call(
         gradient_kernel,
         grid=(steps,),
-        in_specs=[
-            pl.BlockSpec((count * ROWS, TOK), lambda i: (0, 0)),
-            pl.BlockSpec((TOK, width), lambda i: (0, i)),
-            pl.BlockSpec((1, count, ROWS, width), lambda i: (0, first // count, 0, i)),
+        in_specs=[u_spec, u_spec] + [pl.BlockSpec((2, OWN, width), lambda i: (0, 0, i))] * 4,
+        out_specs=[
+            out_spec,
+            out_spec,
+            pl.BlockSpec((NC, 3, ROWS, width), lambda i: (0, 0, 0, i)),
         ],
-        out_specs=pl.BlockSpec((count, ROWS, width), lambda i: (0, 0, i)),
-        out_shape=jax.ShapeDtypeStruct((count, ROWS, D), F32),
-        compiler_params=params(),
+        out_shape=[shape, shape, jax.ShapeDtypeStruct((NC, 3, ROWS, HALF), F32)],
+        compiler_params=params(WIDE_VMEM_BYTES),
         name="gradients",
-    )(columns, tokens, error)
+    )(near, away, *tokens)
 
 
 def spread(value, axis, count):
@@ -285,7 +322,9 @@
     return lax.ppermute(value, "c", [(0, 1), (1, 0)])
 
 
-def error_kernel(place, q_near, q_far, p_factor, branch, down, q_factor, error_next):
+def error_kernel(
+    place, q_near, q_far, p_factor, mine, far, other, error, q_factor, error_next
+):
     first = place[0] == 0
     for m in range(3):
         left = jnp.concatenate(split3(p_factor[m]), axis=1)
@@ -294,27 +333,59 @@
             near = jnp.concatenate([q_near[at, unit] for unit in units], axis=1)
             away = jnp.concatenate([q_far[at, unit] for unit in units], axis=1)
             halves = jnp.where(first, near, away), jnp.where(first, away, near)
-            for half, right in enumerate(halves):
+            piece = slice(at * PIECE, (at + 1) * PIECE)
+            here = mine[m, :, piece] + far[0, m, :, piece]
+            there = other[m, :, piece]
+            values = jnp.where(first, here, there), jnp.where(first, there, here)
+            for half in range(NC):
+                right, value = halves[half], values[half]
                 columns = slice(half * HALF + at * PIECE, half * HALF + (at + 1) * PIECE)
                 q_factor[m, :, columns] = right
                 rebuilt = jnp.dot(
                     left, jnp.concatenate([right] * 3, axis=0), preferred_element_type=F32
                 )
-                value = branch[m, :, columns] if m < 2 else down[0, :, columns]
+                value = value + error[0, m, :, columns].astype(F32)
                 error_next[0, m, :, columns] = (value - rebuilt).astype(BF16)
 
 
-def new_error(place, q_near, q_far, p_factor, branch, down):
+def new_error(place, q_near, q_far, p_factor, mine, far, other, error):
     return pl.pallas_call(
         error_kernel,
-        in_specs=[SMEM] + [pl.BlockSpec(memory_space=pltpu.VMEM)] * 5,
+        in_specs=[SMEM] + [pl.BlockSpec(memory_space=pltpu.VMEM)] * 7,
         out_shape=[
             jax.ShapeDtypeStruct((3, RANK, D), BF16),
             jax.ShapeDtypeStruct((1, 3, ROWS, D), BF16),
         ],
         compiler_params=params(),
         name="new_error",
-    )(place, q_near, q_far, p_factor, branch, down)
+    )(place, q_near, q_far, p_factor, mine, far, other, error)
+
+
+def partner(chip, core, step):
+    return jnp.where(core == step, chip ^ 1, 3 - chip)
+
+
+def swap_chip(value, step):
+    perm = []
+    for chip in range(NX):
+        for core in range(NC):
+            to = chip ^ 1 if core == step else 3 - chip
+            perm.append((chip * NC + core, to * NC + core))
+    return lax.ppermute(value, ("x", "c"), perm)
+
+
+def pair_columns(columns, beside):
+    chip, core = lax.axis_index("x"), lax.axis_index("c")
+    both = jnp.concatenate([columns, beside], axis=0)
+
+    def at_tokens_of(first):
+        pair = (first, partner(first, core, 0))
+        starts = [(at * NC + side) * OWN for at in pair for side in (core, 1 - core)]
+        return jnp.concatenate(
+            [lax.dynamic_slice_in_dim(both, start, OWN, axis=1) for start in starts], axis=1
+        )
+
+    return at_tokens_of(chip), swap_chip(at_tokens_of(partner(chip, core, 1)), 1)
 
 
 def per_device(inputs, out_grad, hidden, up_grad, gate_grad, error_memory, q_start):
@@ -322,22 +393,36 @@
     shard = lax.axis_index("x") * NC + core
     place = jnp.stack([core, shard, row]).astype(jnp.int32)
     tensor, scatter = ("x", "c"), ("x", "c", "y")
-    all_inputs = lax.all_gather(inputs, tensor, axis=0, tiled=True)
-    all_out_grad = lax.all_gather(out_grad, tensor, axis=0, tiled=True)
+    token_q, error_q, keep, sent = token_products(
+        place, inputs, out_grad, error_memory, q_start
+    )
+    sibling = swap_core(sent)
 
     columns = jnp.concatenate([up_grad.T, gate_grad.T, hidden.T], axis=0)
     units = columns.reshape(3 * ROWS, SHARDS, OWN).transpose(1, 0, 2)
     units = lax.all_to_all(units, tensor, 0, 0)
-    token_q, error_q = token_products(inputs, out_grad, error_memory, q_start)
     p_part = left_product(place[1:2], units, token_q, error_q)
     p_rows = lax.all_to_all(p_part.reshape(SHARDS * NY, 8, 128), scatter, 0, 0).sum(0)
+    p_rows, late_keep, late_sibling, late_columns = lax.optimization_barrier(
+        (p_rows, keep, sibling, columns)
+    )
+    columns_beside = swap_core(late_columns)
+    pair, pair_sibling = swap_chip(late_keep, 0), swap_chip(late_sibling, 0)
     p_rows = spread(p_rows, "z", NZ).sum(0)
+    p_rows, columns_beside, pair = lax.optimization_barrier((p_rows, columns_beside, pair))
+    u_near, u_away = pair_columns(columns, columns_beside)
     p_sum = spread(p_rows, scatter, SHARDS * NY).reshape(SHARDS * ROWS, 128)
+    p_sum, u_away, pair_sibling = lax.optimization_barrier((p_sum, u_away, pair_sibling))
 
     near, away = right_product(place, p_sum, units, inputs, out_grad, error_memory)
     w_core = (near + swap_core(away)).reshape(NX * NY, 4, RANK, 128)
     inverse, p_factor = factors(place, p_sum)
     received = lax.all_to_all(w_core, ("x", "y"), 0, 0)
+    mine, beside, away_sums = gradients(u_near, u_away, (keep, sibling, pair, pair_sibling))
+    received, mine, beside, away_sums, inverse = lax.optimization_barrier(
+        (received, mine, beside, away_sums, inverse)
+    )
+    far = swap_chip(away_sums, 1)
     q_y = scaled_sum(place, received, inverse)
     q_z = lax.all_to_all(q_y.reshape(NZ, 8, 128), "z", 0, 0).sum(0)
     q_part = (q_z / (NY * NZ)).astype(BF16)
@@ -345,9 +430,10 @@
     q_dp = spread(q_part, "z", NZ).reshape(4, RANK, 128)
     q_near = spread(q_dp, ("x", "y"), NX * NY).reshape(NX, NY * 4, RANK, 128)
 
-    branch = gradients(columns[: 2 * ROWS], all_inputs, error_memory)
-    down = gradients(columns[2 * ROWS :], all_out_grad, error_memory)
-    q_factor, error_next = new_error(place, q_near, swap_core(q_near), p_factor, branch, down)
+    other = swap_core(beside + far[1])
+    q_factor, error_next = new_error(
+        place, q_near, swap_core(q_near), p_factor, mine, far, other, error_memory
+    )
     return (error_next, p_factor, q_factor)
 
 

time: 188 us -> 182 us (0.968)
  starting transfers between devices: 27.1 us -> 67.7 us
  blocking collectives: 80.5 us -> 48 us
  between operations: 14.3 us -> 0.98 us
  Pallas kernels: 30.6 us -> 21.5 us
  local copies, waits for them, and re-layouts: 4.91 us -> 10.9 us
    all_to_all x3 -> x1, blocking collectives: 54.1 us -> 14.3 us  [spread(): return lax.all_to_all(copies, axis, 0, 0)]
    ppermute x2 -> x5, starting transfers between devices: 7.48 us -> 28.6 us  [swap_core(): return lax.ppermute(value, 'c', [(0, 1), (1, 0)])]
    all_to_all x1 -> x3, starting transfers between devices: 5.77 us -> 25.2 us  [spread(): return lax.all_to_all(copies, axis, 0, 0)]
    ppermute x0 -> x4, starting transfers between devices: none -> 10.3 us  [swap_chip(): return lax.ppermute(value, ('x', 'c'), perm)]
    all_to_all x1 -> x0, starting transfers between devices: 10.2 us -> none  [per_device(): units = lax.all_to_all(units, tensor, 0, 0)]
    pallas_call x3 -> x2, Pallas kernels: 18.6 us -> 8.78 us  [the longest x1 4.72 us: gradients(): pl.pallas_call(gradient_kernel, grid=(steps,), in_specs=[u_spec, u_spec]...]
    all_to_all x0 -> x1, blocking collectives: none -> 8.29 us  [per_device(): units = lax.all_to_all(units, tensor, 0, 0)]
    all_to_all x1 -> x3, waiting for transfers between devices: 8.96 us -> 17.1 us  [spread(): return lax.all_to_all(copies, axis, 0, 0)]
  transfers between devices with their start and end apart: 7 -> 13, of which waited for: 4 -> 5; matrix products, arithmetic and copies ran while one was open for 2% -> 3% of each run, Pallas kernels for 15% -> 6%
where the time goes in v5:
time: 182 us; the launch traced here: 181 us
  starting transfers between devices  67.7 us (37%)
  blocking collectives  48 us (26%)
  waiting for transfers between devices  27.6 us (15%)
  Pallas kernels  21.5 us (12%)
  local copies, waits for them, and re-layouts  10.9 us (6%)
  other arithmetic  4.49 us (2%)
    ppermute x5, starting transfers between devices, swap_core(): return lax.ppermute(value, 'c', [(0, 1), (1, 0)])  28.6 us
    all_to_all x3, starting transfers between devices, spread(): return lax.all_to_all(copies, axis, 0, 0)  25.2 us
    all_to_all x3, waiting for transfers between devices, spread(): return lax.all_to_all(copies, axis, 0, 0)  17.1 us
    all_to_all x1, blocking collectives, spread(): return lax.all_to_all(copies, axis, 0, 0)  14.3 us
    all_to_all x1, blocking collectives, per_device(): q_z = lax.all_to_all(q_y.reshape(NZ, 8, 128), 'z', 0, 0).sum(0)  14.2 us
    all_to_all x1, blocking collectives, per_device(): lax.all_to_all(p_part.reshape(SHARDS * NY, 8, 128), scatter, 0, 0).sum(0)  11.3 us
    ppermute x4, starting transfers between devices, swap_chip(): return lax.ppermute(value, ('x', 'c'), perm)  10.3 us
    unnamed x28, local copies, waits for them, and re-layouts  8.53 us
  transfers between devices with their start and end apart: 13, of which 5 were waited for; matrix products, arithmetic and copies ran while one was open for 3% of the time, Pallas kernels for 6%

profile of v5, /device:TPU:1, one launch (start us, length us, event | category | flops | bytes accessed | tf_op | source)
XLA Modules:
  0.0 181.2 jit_solution(8975085540400008736)
XLA Ops:
  0.6 0.1 pad_add_fusion.place
  0.7 0.0 copy-start
  0.7 1.2 copy-done
  1.9 1.3 copy-done.2
  3.2 1.2 copy-done.7
  4.4 4.1 %token_products.1 = (f32[128,128]{1,0:T(8,128)S(1)}, f32[32,128]{1,0:T(8,128)S(1)}, bf16[2,128,2560]{2,1,0:T(8,128)(2,1)}, bf16[2,128,2560]{2,1,0:T(8,128)(2,1)S(1)}) custom-call(s32[3]{0:T(128)S(1)} %pad_add_fusion.place, bf16[128,5120]{1,0:T(8,128)(2,1)S(1)} %copy-done.2, bf16[128,5120]{1,0:T(8,128)(2,1)} %o_away.1, bf16[1,3,32,5120]{3,2,1,0:T(8,128)(2,1)S(1)} %copy-done, ...), custom_call_target="tpu_custom_call" | custom-call | tf_op jit(solution)/shard_map/token_products/pallas_call | solution.py:81
  8.5 8.8 %collective-permute-start = (bf16[2,128,2560]{2,1,0:T(8,128)(2,1)S(1)}, bf16[2,128,2560]{2,1,0:T(8,128)(2,1)}, u32[]{:S(2)}, u32[]{:S(2)}) collective-permute-start(bf16[2,128,2560]{2,1,0:T(8,128)(2,1)S(1)} %get-tuple-element.34), channel_id=1, source_target_pairs={{0,1},{1,0},{2,3},{3,2},{4,5},{5,4},{6,7},{7,6},{8,9},{9,8},{10,11... | collective-permute-start | bytes 3932168 | tf_op jit(solution)/shard_map/ppermute | solution.py:322
  17.3 0.0 copy-done.10
  17.3 0.0 copy-done.11
  17.3 0.0 copy-done.12
  17.3 0.1 pad_maximum_fusion.1
  17.4 8.3 %all_to_all.40.units = bf16[8,96,128]{2,1,0:T(8,128)(2,1)S(1)} all-to-all(bf16[8,96,128]{2,1,0:T(8,128)(2,1)S(1)} %bitcast.31), channel_id=1, replica_groups=mesh['y'=4,'z'=16,'x'=4,'c'=2] {'x','c'}, dimensions={0} | all-to-all | bytes 393216 | tf_op jit(solution)/shard_map/all_to_all | solution.py:403
  25.7 0.3 left_product.1
  26.0 11.3 %all_to_all.41 = f32[32,8,128]{2,1,0:T(8,128)S(1)} all-to-all(f32[32,8,128]{2,1,0:T(8,128)S(1)} %bitcast.28), channel_id=1, replica_groups=mesh['y'=4,'z'=16,'x'=4,'c'=2] {'x','c','y'}, dimensions={0} | all-to-all | bytes 262144 | tf_op jit(solution)/shard_map/all_to_all | solution.py:405
  37.3 0.0 collective-permute-done.sibling
  37.3 2.8 %collective-permute-start.2 = (bf16[2,128,2560]{2,1,0:T(8,128)(2,1)}, bf16[2,128,2560]{2,1,0:T(8,128)(2,1)}, u32[]{:S(2)}, u32[]{:S(2)}) collective-permute-start(bf16[2,128,2560]{2,1,0:T(8,128)(2,1)} %get-tuple-element.37.own), channel_id=1, source_target_pairs={{0,2},{1,7},{2,0},{3,5},{4,6},{5,3},{6,4},{7,1},{8,10},{9,15},{10,... | collective-permute-start | bytes 3932168 | tf_op jit(solution)/shard_map/ppermute | solution.py:374
  40.1 3.7 %collective-permute-start.4 = (bf16[2,128,2560]{2,1,0:T(8,128)(2,1)}, bf16[2,128,2560]{2,1,0:T(8,128)(2,1)}, u32[]{:S(2)}, u32[]{:S(2)}) collective-permute-start(bf16[2,128,2560]{2,1,0:T(8,128)(2,1)} %collective-permute-done.sibling), channel_id=1, source_target_pairs={{0,2},{1,7},{2,0},{3,5},{4,6},{5,3},{6,4},{7,1},{8,10},{9,15},{10,... | collective-permute-start | bytes 3932168 | tf_op jit(solution)/shard_map/ppermute | solution.py:374
  43.8 0.6 broadcast_in_dim.10
  44.5 13.8 %all-to-all-start.2 = ((f32[16,8,128]{2,1,0:T(8,128)}), f32[16,8,128]{2,1,0:T(8,128)S(1)}, u32[]{:S(2)}, u32[]{:S(2)}) async-start(f32[16,8,128]{2,1,0:T(8,128)} %broadcast_in_dim.10), calls=%async_computation.2 | async-start | bytes 131072 | tf_op jit(solution)/shard_map/all_to_all | solution.py:318
  58.2 2.0 %collective-permute-start.1 = (bf16[96,1024]{1,0:T(8,128)(2,1)S(1)}, bf16[96,1024]{1,0:T(8,128)(2,1)S(1)}, u32[]{:S(2)}, u32[]{:S(2)}) collective-permute-start(bf16[96,1024]{1,0:T(8,128)(2,1)S(1)} %get-tuple-element.36), channel_id=1, source_target_pairs={{0,1},{1,0},{2,3},{3,2},{4,5},{5,4},{6,7},{7,6},{8,9},{9,8},{10,11... | collective-permute-start | bytes 589832 | tf_op jit(solution)/shard_map/ppermute | solution.py:322
  60.3 9.5 %all-to-all-done.2 = f32[16,8,128]{2,1,0:T(8,128)S(1)} async-done(((f32[16,8,128]{2,1,0:T(8,128)}), f32[16,8,128]{2,1,0:T(8,128)S(1)}, u32[]{:S(2)}, u32[]{:S(2)}) %all-to-all-start.2) | async-done | bytes 65568 | tf_op jit(solution)/shard_map/all_to_all | solution.py:318
  69.8 0.0 collective-permute-done.1
  69.8 0.0 collective-permute-done.2.pair
  69.9 0.1 constant_dynamic-slice_fusion.3
  70.1 1.9 %collective-permute-start.3 = (bf16[192,512]{1,0:T(8,128)(2,1)S(1)}, bf16[192,512]{1,0:T(8,128)(2,1)S(1)}, u32[]{:S(2)}, u32[]{:S(2)}) collective-permute-start(bf16[192,512]{1,0:T(8,128)(2,1)S(1)} %pad_maximum_fusion.2), channel_id=1, source_target_pairs={{0,6},{1,3},{2,4},{3,1},{4,2},{5,7},{6,0},{7,5},{8,14},{9,11},{10,... | collective-permute-start | bytes 589832 | tf_op jit(solution)/shard_map/ppermute | solution.py:374
  72.0 0.7 broadcast_in_dim.11
  72.7 7.1 %all-to-all-start.3 = ((f32[32,8,128]{2,1,0:T(8,128)}), f32[32,8,128]{2,1,0:T(8,128)S(1)}, u32[]{:S(2)}, u32[]{:S(2)}) async-start(f32[32,8,128]{2,1,0:T(8,128)} %broadcast_in_dim.11), calls=%async_computation.3 | async-start | bytes 262144 | tf_op jit(solution)/shard_map/all_to_all | solution.py:318
  79.8 0.0 collective-permute-done.4.pair_sibling
  79.8 7.6 %all-to-all-done.3 = f32[32,8,128]{2,1,0:T(8,128)S(1)} async-done(((f32[32,8,128]{2,1,0:T(8,128)}), f32[32,8,128]{2,1,0:T(8,128)S(1)}, u32[]{:S(2)}, u32[]{:S(2)}) %all-to-all-start.3) | async-done | bytes 131104 | tf_op jit(solution)/shard_map/all_to_all | solution.py:318
  87.3 0.0 collective-permute-done.3.away
  87.4 0.0 copy-done.1
  87.4 0.0 copy-done.3
  87.4 0.0 copy-start.4
  87.4 1.4 copy-done.4
  88.8 4.3 %right_product.1 = (f32[4,4,4,32,128]{4,3,2,1,0:T(8,128)S(1)}, f32[4,4,4,32,128]{4,3,2,1,0:T(8,128)S(1)}) custom-call(s32[3]{0:T(128)S(1)} %pad_add_fusion.place, f32[256,128]{1,0:T(8,128)S(1)} %bitcast.26, bf16[8,96,128]{2,1,0:T(8,128)(2,1)S(1)} %all_to_all.40.units, bf16[128,5120]{1,0:T(8,128)(2,1)S(1)} %copy-done.3, bf16[128,5120]{1,0:T(8,128)(2,1)S(1)} %copy-done.3, ...), custom_call_target="tpu_custom_call" | custom-call | tf_op jit(solution)/shard_map/right_product/pallas_call | solution.py:183
  93.0 0.0 copy-done.13
  93.0 2.4 %collective-permute-start.5 = (f32[4,4,4,32,128]{4,3,2,1,0:T(8,128)S(1)}, f32[4,4,4,32,128]{4,3,2,1,0:T(8,128)S(1)}, u32[]{:S(2)}, u32[]{:S(2)}) collective-permute-start(f32[4,4,4,32,128]{4,3,2,1,0:T(8,128)S(1)} %get-tuple-element.43), channel_id=1, source_target_pairs={{0,1},{1,0},{2,3},{3,2},{4,5},{5,4},{6,7},{7,6},{8,9},{9,8},{10,11... | collective-permute-start | bytes 3145736 | tf_op jit(solution)/shard_map/ppermute | solution.py:322
  95.4 2.3 %collective-permute-done.5 = f32[4,4,4,32,128]{4,3,2,1,0:T(8,128)S(1)} collective-permute-done((f32[4,4,4,32,128]{4,3,2,1,0:T(8,128)S(1)}, f32[4,4,4,32,128]{4,3,2,1,0:T(8,128)S(1)}, u32[]{:S(2)}, u32[]{:S(2)}) %collective-permute-start.5) | collective-permute-done | bytes 1048608 | tf_op jit(solution)/shard_map/ppermute | solution.py:322
  97.7 1.3 add.64
  99.0 3.7 %all-to-all-start.4 = ((f32[16,4,32,128]{3,2,1,0:T(8,128)}), f32[16,4,32,128]{3,2,1,0:T(8,128)S(1)}, u32[]{:S(2)}, u32[]{:S(2)}) async-start(f32[16,4,32,128]{3,2,1,0:T(8,128)} %bitcast.30), calls=%async_computation.4 | async-start | bytes 2097152 | tf_op jit(solution)/shard_map/all_to_all | solution.py:420
  102.6 0.7 pad_maximum_fusion.3.near
  103.3 4.4 %factors.1 = (f32[3,32,32]{2,1,0:T(8,128)S(1)}, f32[3,32,32]{2,1,0:T(8,128)}) custom-call(s32[3]{0:T(128)S(1)} %pad_add_fusion.place, f32[256,128]{1,0:T(8,128)S(1)} %bitcast.27), custom_call_target="tpu_custom_call" | custom-call | tf_op jit(solution)/shard_map/factors/pallas_call | solution.py:245
  107.7 4.7 %gradients.1 = (f32[3,32,2560]{2,1,0:T(8,128)}, f32[3,32,2560]{2,1,0:T(8,128)}, f32[2,3,32,2560]{3,2,1,0:T(8,128)}) custom-call(bf16[192,512]{1,0:T(8,128)(2,1)} %pad_maximum_fusion.3.near, bf16[192,512]{1,0:T(8,128)(2,1)} %copy-done.13, bf16[2,128,2560]{2,1,0:T(8,128)(2,1)} %get-tuple-element.37.own, bf16[2,128,2560]{2,1,0:T(8,128)(2,1)} %collective-permute-done.sibling, ...), custom_call_target="tpu_custom_call" | custom-call | tf_op jit(solution)/shard_map/gradients/pallas_call | solution.py:301
  112.4 6.7 %all-to-all-done.4.received = f32[16,4,32,128]{3,2,1,0:T(8,128)S(1)} async-done(((f32[16,4,32,128]{3,2,1,0:T(8,128)}), f32[16,4,32,128]{3,2,1,0:T(8,128)S(1)}, u32[]{:S(2)}, u32[]{:S(2)}) %all-to-all-start.4) | async-done | bytes 1048608 | tf_op jit(solution)/shard_map/all_to_all | solution.py:420
  119.2 1.0 copy-done.5
  120.1 1.9 %collective-permute-start.7 = (f32[2,3,32,2560]{3,2,1,0:T(8,128)}, f32[2,3,32,2560]{3,2,1,0:T(8,128)S(1)}, u32[]{:S(2)}, u32[]{:S(2)}) collective-permute-start(f32[2,3,32,2560]{3,2,1,0:T(8,128)} %get-tuple-element.55), channel_id=1, source_target_pairs={{0,6},{1,3},{2,4},{3,1},{4,2},{5,7},{6,0},{7,5},{8,14},{9,11},{10,... | collective-permute-start | bytes 5898248 | tf_op jit(solution)/shard_map/ppermute | solution.py:374
  122.1 0.0 copy-start.6
  122.1 1.2 copy-done.6
  123.3 0.8 scaled_sum.1
  124.0 14.2 %all_to_all.42 = f32[16,8,128]{2,1,0:T(8,128)S(1)} all-to-all(f32[16,8,128]{2,1,0:T(8,128)S(1)} %bitcast.29), channel_id=1, replica_groups=mesh['y'=4,'z'=16,'x'=4,'c'=2] {'z'}, dimensions={0} | all-to-all | bytes 131072 | tf_op jit(solution)/shard_map/all_to_all | solution.py:427
  138.3 14.3 %all_to_all.43 = bf16[16,8,128]{2,1,0:T(8,128)(2,1)S(1)} all-to-all(bf16[16,8,128]{2,1,0:T(8,128)(2,1)S(1)} %broadcast_in_dim.12), channel_id=1, replica_groups=mesh['y'=4,'z'=16,'x'=4,'c'=2] {'z'}, dimensions={0} | all-to-all | bytes 65536 | tf_op jit(solution)/shard_map/all_to_all | solution.py:318
  152.6 0.9 broadcast_in_dim.14
  153.5 4.3 %all-to-all-start.7 = ((bf16[16,4,32,128]{3,2,1,0:T(8,128)(2,1)}), bf16[16,4,32,128]{3,2,1,0:T(8,128)(2,1)S(1)}, u32[]{:S(2)}, u32[]{:S(2)}) async-start(bf16[16,4,32,128]{3,2,1,0:T(8,128)(2,1)} %broadcast_in_dim.14), calls=%async_computation.7 | async-start | bytes 1048576 | tf_op jit(solution)/shard_map/all_to_all | solution.py:318
  157.8 0.0 copy-start.9
  157.8 0.0 collective-permute-done.7.far
  157.8 2.3 %fusion = f32[3,32,2560]{2,1,0:T(8,128)} fusion(f32[3,32,2560]{2,1,0:T(8,128)} %get-tuple-element.56, f32[2,3,32,2560]{3,2,1,0:T(8,128)S(1)} %collective-permute-done.7.far), kind=kLoop, calls=%fused_computation.1 | loop fusion | flops 245760 | bytes 2949120 | tf_op jit(solution)/shard_map/add | solution.py:433
  160.0 7.6 %collective-permute-start.8 = (f32[3,32,2560]{2,1,0:T(8,128)}, f32[3,32,2560]{2,1,0:T(8,128)}, u32[]{:S(2)}, u32[]{:S(2)}) collective-permute-start(f32[3,32,2560]{2,1,0:T(8,128)} %fusion), channel_id=1, source_target_pairs={{0,1},{1,0},{2,3},{3,2},{4,5},{5,4},{6,7},{7,6},{8,9},{9,8},{10,11... | collective-permute-start | bytes 2949128 | tf_op jit(solution)/shard_map/ppermute | solution.py:322
  167.7 0.0 all-to-all-done.7
  167.7 7.8 %collective-permute-start.6 = (bf16[4,16,32,128]{3,2,1,0:T(8,128)(2,1)S(1)}, bf16[4,16,32,128]{3,2,1,0:T(8,128)(2,1)S(1)}, u32[]{:S(2)}, u32[]{:S(2)}) collective-permute-start(bf16[4,16,32,128]{3,2,1,0:T(8,128)(2,1)S(1)} %bitcast.24), channel_id=1, source_target_pairs={{0,1},{1,0},{2,3},{3,2},{4,5},{5,4},{6,7},{7,6},{8,9},{9,8},{10,11... | collective-permute-start | bytes 1572872 | tf_op jit(solution)/shard_map/ppermute | solution.py:322
  175.5 1.5 collective-permute-done.6.q_far
  177.0 0.0 collective-permute-done.8.other
  177.0 0.0 copy-done.9
  177.0 1.2 copy-done.8
  178.2 3.0 %new_error.1 = (bf16[3,32,5120]{2,1,0:T(8,128)(2,1)}, bf16[1,3,32,5120]{3,2,1,0:T(8,128)(2,1)}) custom-call(s32[3]{0:T(128)S(1)} %pad_add_fusion.place, bf16[4,16,32,128]{3,2,1,0:T(8,128)(2,1)S(1)} %bitcast.25, bf16[4,16,32,128]{3,2,1,0:T(8,128)(2,1)S(1)} %collective-permute-done.6.q_far, f32[3,32,32]{2,1,0:T(8,128)S(1)} %copy-done.9, ...), custom_call_target="tpu_custom_call" | custom-call | tf_op jit(solution)/shard_map/new_error/pallas_call | solution.py:352
  (18 shorter events, 0.2 us)
Async XLA Ops:
  0.7 1.2 copy-start
  1.9 1.3 copy-start.2
  3.2 1.2 copy-start.7
  4.4 12.8 %copy-start.10 = (bf16[1024,32]{0,1:T(8,128)(2,1)S(1)}, bf16[1024,32]{0,1:T(8,128)(2,1)}, u32[]{:S(2)}) copy-start(bf16[1024,32]{0,1:T(8,128)(2,1)} %param.9) | copy-start | bytes 196612
  4.4 12.9 %copy-start.11 = (bf16[1024,32]{0,1:T(8,128)(2,1)S(1)}, bf16[1024,32]{0,1:T(8,128)(2,1)}, u32[]{:S(2)}) copy-start(bf16[1024,32]{0,1:T(8,128)(2,1)} %param.11) | copy-start | bytes 196612
  4.4 12.9 %copy-start.12 = (bf16[1024,32]{0,1:T(8,128)(2,1)S(1)}, bf16[1024,32]{0,1:T(8,128)(2,1)}, u32[]{:S(2)}) copy-start(bf16[1024,32]{0,1:T(8,128)(2,1)} %param.10) | copy-start | bytes 196612
  8.5 28.8 %collective-permute-start = (bf16[2,128,2560]{2,1,0:T(8,128)(2,1)S(1)}, bf16[2,128,2560]{2,1,0:T(8,128)(2,1)}, u32[]{:S(2)}, u32[]{:S(2)}) collective-permute-start(bf16[2,128,2560]{2,1,0:T(8,128)(2,1)S(1)} %get-tuple-element.34), channel_id=1, source_target_pairs={{0,1},{1,0},{2,3},{3,2},{4,5},{5,4},{6,7},{7,6},{8,9},{9,8},{10,11... | collective-permute-start | bytes 3932168 | tf_op jit(solution)/shard_map/ppermute | solution.py:322
  37.3 32.5 %collective-permute-start.2 = (bf16[2,128,2560]{2,1,0:T(8,128)(2,1)}, bf16[2,128,2560]{2,1,0:T(8,128)(2,1)}, u32[]{:S(2)}, u32[]{:S(2)}) collective-permute-start(bf16[2,128,2560]{2,1,0:T(8,128)(2,1)} %get-tuple-element.37.own), channel_id=1, source_target_pairs={{0,2},{1,7},{2,0},{3,5},{4,6},{5,3},{6,4},{7,1},{8,10},{9,15},{10,... | collective-permute-start | bytes 3932168 | tf_op jit(solution)/shard_map/ppermute | solution.py:374
  40.1 39.6 %collective-permute-start.4 = (bf16[2,128,2560]{2,1,0:T(8,128)(2,1)}, bf16[2,128,2560]{2,1,0:T(8,128)(2,1)}, u32[]{:S(2)}, u32[]{:S(2)}) collective-permute-start(bf16[2,128,2560]{2,1,0:T(8,128)(2,1)} %collective-permute-done.sibling), channel_id=1, source_target_pairs={{0,2},{1,7},{2,0},{3,5},{4,6},{5,3},{6,4},{7,1},{8,10},{9,15},{10,... | collective-permute-start | bytes 3932168 | tf_op jit(solution)/shard_map/ppermute | solution.py:374
  44.5 42.9 %copy-start.1 = (bf16[1,3,32,5120]{3,2,1,0:T(8,128)(2,1)S(1)}, bf16[1,3,32,5120]{3,2,1,0:T(8,128)(2,1)}, u32[]{:S(2)}) copy-start(bf16[1,3,32,5120]{3,2,1,0:T(8,128)(2,1)} %error.3) | copy-start | bytes 2949124
  44.5 42.9 %copy-start.3 = (bf16[128,5120]{1,0:T(8,128)(2,1)S(1)}, bf16[128,5120]{1,0:T(8,128)(2,1)}, u32[]{:S(2)}) copy-start(bf16[128,5120]{1,0:T(8,128)(2,1)} %x_away.1) | copy-start | bytes 3932164
  44.5 25.3 %all-to-all-start.2 = ((f32[16,8,128]{2,1,0:T(8,128)}), f32[16,8,128]{2,1,0:T(8,128)S(1)}, u32[]{:S(2)}, u32[]{:S(2)}) async-start(f32[16,8,128]{2,1,0:T(8,128)} %broadcast_in_dim.10), calls=%async_computation.2 | async-start | bytes 131072 | tf_op jit(solution)/shard_map/all_to_all | solution.py:318
  58.2 11.6 %collective-permute-start.1 = (bf16[96,1024]{1,0:T(8,128)(2,1)S(1)}, bf16[96,1024]{1,0:T(8,128)(2,1)S(1)}, u32[]{:S(2)}, u32[]{:S(2)}) collective-permute-start(bf16[96,1024]{1,0:T(8,128)(2,1)S(1)} %get-tuple-element.36), channel_id=1, source_target_pairs={{0,1},{1,0},{2,3},{3,2},{4,5},{5,4},{6,7},{7,6},{8,9},{9,8},{10,11... | collective-permute-start | bytes 589832 | tf_op jit(solution)/shard_map/ppermute | solution.py:322
  70.1 17.3 %collective-permute-start.3 = (bf16[192,512]{1,0:T(8,128)(2,1)S(1)}, bf16[192,512]{1,0:T(8,128)(2,1)S(1)}, u32[]{:S(2)}, u32[]{:S(2)}) collective-permute-start(bf16[192,512]{1,0:T(8,128)(2,1)S(1)} %pad_maximum_fusion.2), channel_id=1, source_target_pairs={{0,6},{1,3},{2,4},{3,1},{4,2},{5,7},{6,0},{7,5},{8,14},{9,11},{10,... | collective-permute-start | bytes 589832 | tf_op jit(solution)/shard_map/ppermute | solution.py:374
  72.7 14.7 %all-to-all-start.3 = ((f32[32,8,128]{2,1,0:T(8,128)}), f32[32,8,128]{2,1,0:T(8,128)S(1)}, u32[]{:S(2)}, u32[]{:S(2)}) async-start(f32[32,8,128]{2,1,0:T(8,128)} %broadcast_in_dim.11), calls=%async_computation.3 | async-start | bytes 262144 | tf_op jit(solution)/shard_map/all_to_all | solution.py:318
  87.3 5.7 %copy-start.13 = (bf16[192,512]{1,0:T(8,128)(2,1)}, bf16[192,512]{1,0:T(8,128)(2,1)S(1)}, u32[]{:S(2)}) copy-start(bf16[192,512]{1,0:T(8,128)(2,1)S(1)} %collective-permute-done.3.away) | copy-start | bytes 589828
  87.4 1.4 copy-start.4
  93.0 4.7 %collective-permute-start.5 = (f32[4,4,4,32,128]{4,3,2,1,0:T(8,128)S(1)}, f32[4,4,4,32,128]{4,3,2,1,0:T(8,128)S(1)}, u32[]{:S(2)}, u32[]{:S(2)}) collective-permute-start(f32[4,4,4,32,128]{4,3,2,1,0:T(8,128)S(1)} %get-tuple-element.43), channel_id=1, source_target_pairs={{0,1},{1,0},{2,3},{3,2},{4,5},{5,4},{6,7},{7,6},{8,9},{9,8},{10,11... | collective-permute-start | bytes 3145736 | tf_op jit(solution)/shard_map/ppermute | solution.py:322
  99.0 20.2 %all-to-all-start.4 = ((f32[16,4,32,128]{3,2,1,0:T(8,128)}), f32[16,4,32,128]{3,2,1,0:T(8,128)S(1)}, u32[]{:S(2)}, u32[]{:S(2)}) async-start(f32[16,4,32,128]{3,2,1,0:T(8,128)} %bitcast.30), calls=%async_computation.4 | async-start | bytes 2097152 | tf_op jit(solution)/shard_map/all_to_all | solution.py:420
  119.2 1.0 copy-start.5
  120.1 37.6 %collective-permute-start.7 = (f32[2,3,32,2560]{3,2,1,0:T(8,128)}, f32[2,3,32,2560]{3,2,1,0:T(8,128)S(1)}, u32[]{:S(2)}, u32[]{:S(2)}) collective-permute-start(f32[2,3,32,2560]{3,2,1,0:T(8,128)} %get-tuple-element.55), channel_id=1, source_target_pairs={{0,6},{1,3},{2,4},{3,1},{4,2},{5,7},{6,0},{7,5},{8,14},{9,11},{10,... | collective-permute-start | bytes 5898248 | tf_op jit(solution)/shard_map/ppermute | solution.py:374
  122.1 1.2 copy-start.6
  153.5 14.2 %all-to-all-start.7 = ((bf16[16,4,32,128]{3,2,1,0:T(8,128)(2,1)}), bf16[16,4,32,128]{3,2,1,0:T(8,128)(2,1)S(1)}, u32[]{:S(2)}, u32[]{:S(2)}) async-start(bf16[16,4,32,128]{3,2,1,0:T(8,128)(2,1)} %broadcast_in_dim.14), calls=%async_computation.7 | async-start | bytes 1048576 | tf_op jit(solution)/shard_map/all_to_all | solution.py:318
  157.8 19.2 %copy-start.9 = (f32[3,32,32]{2,1,0:T(8,128)S(1)}, f32[3,32,32]{2,1,0:T(8,128)}, u32[]{:S(2)}) copy-start(f32[3,32,32]{2,1,0:T(8,128)} %get-tuple-element.29.p_factor) | copy-start | bytes 36868
  160.0 17.0 %collective-permute-start.8 = (f32[3,32,2560]{2,1,0:T(8,128)}, f32[3,32,2560]{2,1,0:T(8,128)}, u32[]{:S(2)}, u32[]{:S(2)}) collective-permute-start(f32[3,32,2560]{2,1,0:T(8,128)} %fusion), channel_id=1, source_target_pairs={{0,1},{1,0},{2,3},{3,2},{4,5},{5,4},{6,7},{7,6},{8,9},{9,8},{10,11... | collective-permute-start | bytes 2949128 | tf_op jit(solution)/shard_map/ppermute | solution.py:322
  167.7 9.3 %collective-permute-start.6 = (bf16[4,16,32,128]{3,2,1,0:T(8,128)(2,1)S(1)}, bf16[4,16,32,128]{3,2,1,0:T(8,128)(2,1)S(1)}, u32[]{:S(2)}, u32[]{:S(2)}) collective-permute-start(bf16[4,16,32,128]{3,2,1,0:T(8,128)(2,1)S(1)} %bitcast.24), channel_id=1, source_target_pairs={{0,1},{1,0},{2,3},{3,2},{4,5},{5,4},{6,7},{7,6},{8,9},{9,8},{10,11... | collective-permute-start | bytes 1572872 | tf_op jit(solution)/shard_map/ppermute | solution.py:322
  177.0 1.2 copy-start.8

commit v6 on v5

--- a/solution.py
+++ b/solution.py
@@ -17,7 +17,7 @@
 BLOCKS = PIECE // 128
 TOKEN_STEPS = 2
 F32, BF16 = jnp.float32, jnp.bfloat16
-VMEM_BYTES = 48 * 1024 * 1024
+VMEM_BYTES = 24 * 1024 * 1024
 WIDE_VMEM_BYTES = 60 * 1024 * 1024
 PRECISE = lax.Precision.HIGHEST
 SMEM = pl.BlockSpec(memory_space=pltpu.SMEM)
@@ -102,7 +102,7 @@
             half_shape,
             half_shape,
         ],
-        compiler_params=params(),
+        compiler_params=params(WIDE_VMEM_BYTES),
         name="token_products",
     )(place, inputs, out_grad, error, q_start)
 
@@ -131,80 +131,107 @@
     )(shard, units, token_q, error_q)
 
 
-def right_kernel(
-    place, p_sum, units, x_near, x_away, o_near, o_away, e_near, e_away, near, away, token_p, error_p
-):
+def right_half(token_p, error_p, x_ref, o_ref, e_ref, out):
+    branch = jnp.dot(
+        token_p[: 2 * RANK], jnp.concatenate([x_ref[...]] * 3, axis=0), preferred_element_type=F32
+    )
+    down = jnp.dot(
+        token_p[2 * RANK :], jnp.concatenate([o_ref[...]] * 3, axis=0), preferred_element_type=F32
+    )
+    for m, product in enumerate((branch[:RANK], branch[RANK:], down)):
+        rows = slice(m * RANK, (m + 1) * RANK)
+        product = product + jnp.dot(
+            error_p[rows], jnp.concatenate([e_ref[0, m]] * 3, axis=0), preferred_element_type=F32
+        )
+        for block in range(BLOCKS):
+            unit = m * BLOCKS + block
+            out[0, unit // 4, unit % 4] = product[:, block * 128 : (block + 1) * 128]
+    out[0, NY - 1, 3] = jnp.zeros((RANK, 128), F32)
+
+
+def away_kernel(place, p_sum, units, x_ref, o_ref, e_ref, out, token_p, error_p):
     @pl.when(pl.program_id(0) == 0)
     def _():
-        parts = split3(p_sum[...])
+        columns = jnp.concatenate(
+            [
+                jnp.concatenate(
+                    [units[shard, m * ROWS : (m + 1) * ROWS] for shard in range(SHARDS)], axis=0
+                )
+                for m in range(3)
+            ],
+            axis=1,
+        )
+        total = jnp.zeros((128, 3 * OWN), F32)
+        for part in split3(p_sum[...].T)[::-1]:
+            total = total + jnp.dot(part, columns, preferred_element_type=F32)
         for m in range(3):
-            columns = jnp.concatenate(
-                [units[shard, m * ROWS : (m + 1) * ROWS] for shard in range(SHARDS)], axis=0
-            )
-            total = jnp.zeros((128, OWN), F32)
-            for part in parts[::-1]:
-                total = total + lax.dot_general(
-                    part, columns, ROWS_ON_ROWS, preferred_element_type=F32
-                )
-            token_p[m * RANK : (m + 1) * RANK] = jnp.concatenate(
-                split3(total[m * RANK : (m + 1) * RANK]), axis=1
+            rows = slice(m * RANK, (m + 1) * RANK)
+            token_p[rows] = jnp.concatenate(
+                split3(total[rows, m * OWN : (m + 1) * OWN]), axis=1
             )
         mine = p_sum[pl.ds(pl.multiple_of(place[1] * ROWS, ROWS), ROWS)]
-        error_p[...] = jnp.concatenate(split3(mine), axis=0)
-
-    for out, x_ref, o_ref, e_ref in ((near, x_near, o_near, e_near), (away, x_away, o_away, e_away)):
-        branch = jnp.dot(
-            token_p[: 2 * RANK], jnp.concatenate([x_ref[...]] * 3, axis=0), preferred_element_type=F32
-        )
-        down = jnp.dot(
-            token_p[2 * RANK :], jnp.concatenate([o_ref[...]] * 3, axis=0), preferred_element_type=F32
-        )
-        for m, product in enumerate((branch[:RANK], branch[RANK:], down)):
-            of_error = lax.dot_general(
-                error_p[...],
-                jnp.concatenate([e_ref[0, m]] * 3, axis=0),
-                ROWS_ON_ROWS,
-                preferred_element_type=F32,
-            )
-            product = product + of_error[m * RANK : (m + 1) * RANK]
-            for block in range(BLOCKS):
-                unit = m * BLOCKS + block
-                out[0, unit // 4, unit % 4] = product[:, block * 128 : (block + 1) * 128]
-        out[0, NY - 1, 3] = jnp.zeros((RANK, 128), F32)
-
-
-def right_product(place, p_sum, units, inputs, out_grad, error):
-    x_near = pl.BlockSpec((OWN, PIECE), lambda i, at: (0, at[0] * NX + i))
-    x_away = pl.BlockSpec((OWN, PIECE), lambda i, at: (0, (1 - at[0]) * NX + i))
-    e_near = pl.BlockSpec((1, 3, ROWS, PIECE), lambda i, at: (0, 0, 0, at[0] * NX + i))
-    e_away = pl.BlockSpec((1, 3, ROWS, PIECE), lambda i, at: (0, 0, 0, (1 - at[0]) * NX + i))
+        error_p[...] = jnp.concatenate([part.T for part in split3(mine)], axis=1)
+
+    right_half(token_p, error_p, x_ref, o_ref, e_ref, out)
+
+
+def near_kernel(place, token_p, error_p, x_ref, o_ref, e_ref, out):
+    right_half(token_p, error_p, x_ref, o_ref, e_ref, out)
+
+
+def right_specs(stays):
+    def column(i, at):
+        return (at[0] if stays else 1 - at[0]) * NX + i
+
+    x_spec = pl.BlockSpec((OWN, PIECE), lambda i, at: (0, column(i, at)))
+    e_spec = pl.BlockSpec((1, 3, ROWS, PIECE), lambda i, at: (0, 0, 0, column(i, at)))
     out_spec = pl.BlockSpec((1, NY, 4, RANK, 128), lambda i, at: (i, 0, 0, 0, 0))
-    out_shape = jax.ShapeDtypeStruct((NX, NY, 4, RANK, 128), F32)
-    return pl.pallas_call(
-        right_kernel,
+    token_spec = pl.BlockSpec((3 * RANK, 3 * OWN), lambda i, at: (0, 0))
+    error_spec = pl.BlockSpec((128, 3 * ROWS), lambda i, at: (0, 0))
+    return [x_spec, x_spec, e_spec], out_spec, [token_spec, error_spec]
+
+
+RIGHT_SHAPE = jax.ShapeDtypeStruct((NX, NY, 4, RANK, 128), F32)
+
+
+def right_away(place, p_sum, units, inputs, out_grad, error):
+    blocks, out_spec, left_specs = right_specs(False)
+    return pl.pallas_call(
+        away_kernel,
         grid_spec=pltpu.PrefetchScalarGridSpec(
             num_scalar_prefetch=1,
             grid=(NX,),
             in_specs=[
                 pl.BlockSpec((SHARDS * ROWS, 128), lambda i, at: (0, 0)),
                 pl.BlockSpec((SHARDS, 3 * ROWS, OWN), lambda i, at: (0, 0, 0)),
-                x_near,
-                x_away,
-                x_near,
-                x_away,
-                e_near,
-                e_away,
-            ],
-            out_specs=[out_spec, out_spec],
-            scratch_shapes=[
-                pltpu.VMEM((3 * RANK, 3 * OWN), BF16),
-                pltpu.VMEM((3 * ROWS, 128), BF16),
-            ],
+            ]
+            + blocks,
+            out_specs=[out_spec] + left_specs,
         ),
-        out_shape=[out_shape, out_shape],
-        compiler_params=params(),
-        name="right_product",
-    )(place, p_sum, units, inputs, inputs, out_grad, out_grad, error, error)
+        out_shape=[
+            RIGHT_SHAPE,
+            jax.ShapeDtypeStruct((3 * RANK, 3 * OWN), BF16),
+            jax.ShapeDtypeStruct((128, 3 * ROWS), BF16),
+        ],
+        compiler_params=params(),
+        name="right_away",
+    )(place, p_sum, units, inputs, out_grad, error)
+
+
+def right_near(place, token_p, error_p, inputs, out_grad, error):
+    blocks, out_spec, left_specs = right_specs(True)
+    return pl.pallas_call(
+        near_kernel,
+        grid_spec=pltpu.PrefetchScalarGridSpec(
+            num_scalar_prefetch=1,
+            grid=(NX,),
+            in_specs=left_specs + blocks,
+            out_specs=out_spec,
+        ),
+        out_shape=RIGHT_SHAPE,
+        compiler_params=params(),
+        name="right_near",
+    )(place, token_p, error_p, inputs, out_grad, error)
 
 
 def factor_kernel(place, p_sum, inverse, p_factor):
@@ -396,25 +423,28 @@
     token_q, error_q, keep, sent = token_products(
         place, inputs, out_grad, error_memory, q_start
     )
-    sibling = swap_core(sent)
 
     columns = jnp.concatenate([up_grad.T, gate_grad.T, hidden.T], axis=0)
     units = columns.reshape(3 * ROWS, SHARDS, OWN).transpose(1, 0, 2)
     units = lax.all_to_all(units, tensor, 0, 0)
     p_part = left_product(place[1:2], units, token_q, error_q)
+    p_part, late_sent = lax.optimization_barrier((p_part, sent))
+    sibling = swap_core(late_sent)
     p_rows = lax.all_to_all(p_part.reshape(SHARDS * NY, 8, 128), scatter, 0, 0).sum(0)
-    p_rows, late_keep, late_sibling, late_columns = lax.optimization_barrier(
-        (p_rows, keep, sibling, columns)
-    )
+    copies = jnp.broadcast_to(p_rows[None], (NZ,) + p_rows.shape)
+    copies, late_keep, late_sibling, late_columns = lax.optimization_barrier(
+        (copies, keep, sibling, columns)
+    )
+    pair, pair_sibling = swap_chip(late_keep, 0), swap_chip(late_sibling, 0)
     columns_beside = swap_core(late_columns)
-    pair, pair_sibling = swap_chip(late_keep, 0), swap_chip(late_sibling, 0)
-    p_rows = spread(p_rows, "z", NZ).sum(0)
+    p_rows = lax.all_to_all(copies, "z", 0, 0).sum(0)
     p_rows, columns_beside, pair = lax.optimization_barrier((p_rows, columns_beside, pair))
     u_near, u_away = pair_columns(columns, columns_beside)
     p_sum = spread(p_rows, scatter, SHARDS * NY).reshape(SHARDS * ROWS, 128)
     p_sum, u_away, pair_sibling = lax.optimization_barrier((p_sum, u_away, pair_sibling))
 
-    near, away = right_product(place, p_sum, units, inputs, out_grad, error_memory)
+    away, token_p, error_p = right_away(place, p_sum, units, inputs, out_grad, error_memory)
+    near = right_near(place, token_p, error_p, inputs, out_grad, error_memory)
     w_core = (near + swap_core(away)).reshape(NX * NY, 4, RANK, 128)
     inverse, p_factor = factors(place, p_sum)
     received = lax.all_to_all(w_core, ("x", "y"), 0, 0)
@@ -422,8 +452,9 @@
     received, mine, beside, away_sums, inverse = lax.optimization_barrier(
         (received, mine, beside, away_sums, inverse)
     )
+    q_y = scaled_sum(place, received, inverse)
+    q_y, away_sums = lax.optimization_barrier((q_y, away_sums))
     far = swap_chip(away_sums, 1)
-    q_y = scaled_sum(place, received, inverse)
     q_z = lax.all_to_all(q_y.reshape(NZ, 8, 128), "z", 0, 0).sum(0)
     q_part = (q_z / (NY * NZ)).astype(BF16)
 

time: 182 us -> 176 us (0.967)
  blocking collectives: 48 us -> 40.2 us
  starting transfers between devices: 67.7 us -> 72.1 us
  local copies, waits for them, and re-layouts: 10.9 us -> 7.19 us
  waiting for transfers between devices: 27.6 us -> 25.4 us
    all_to_all x0 -> x2, starting transfers between devices: none -> 23.3 us  [the longest x1 13.2 us: per_device(): p_rows = lax.all_to_all(copies, 'z', 0, 0).sum(0)]
    all_to_all x3 -> x2, starting transfers between devices: 25.2 us -> 12 us  [spread(): return lax.all_to_all(copies, axis, 0, 0)]
    all_to_all x0 -> x2, waiting for transfers between devices: none -> 9.49 us  [the longest x1 9.49 us: per_device(): p_rows = lax.all_to_all(copies, 'z', 0, 0).sum(0)]
    all_to_all x3 -> x2, waiting for transfers between devices: 17.1 us -> 7.57 us  [spread(): return lax.all_to_all(copies, axis, 0, 0)]
    all_to_all x1 -> x0, blocking collectives: 8.29 us -> none  [per_device(): units = lax.all_to_all(units, tensor, 0, 0)]
    ppermute x5, starting transfers between devices: 28.6 us -> 22.7 us  [swap_core(): return lax.ppermute(value, 'c', [(0, 1), (1, 0)])]
    unnamed x28 -> x24, local copies, waits for them, and re-layouts: 8.53 us -> 4.16 us
    ppermute x5, waiting for transfers between devices: 3.79 us -> 1.58 us  [swap_core(): return lax.ppermute(value, 'c', [(0, 1), (1, 0)])]
  transfers between devices with their start and end apart: 13 -> 14, of which waited for: 5 -> 5; matrix products, arithmetic and copies ran while one was open for 3% -> 3% of each run, Pallas kernels for 6% -> 9%
where the time goes in v6:
time: 176 us; the launch traced here: 175 us
  starting transfers between devices  72.1 us (41%)
  blocking collectives  40.2 us (23%)
  waiting for transfers between devices  25.4 us (14%)
  Pallas kernels  23.2 us (13%)
  local copies, waits for them, and re-layouts  7.19 us (4%)
  other arithmetic  5.97 us (3%)
    ppermute x5, starting transfers between devices, swap_core(): return lax.ppermute(value, 'c', [(0, 1), (1, 0)])  22.7 us
    all_to_all x1, blocking collectives, spread(): return lax.all_to_all(copies, axis, 0, 0)  14.4 us
    all_to_all x1, blocking collectives, per_device(): q_z = lax.all_to_all(q_y.reshape(NZ, 8, 128), 'z', 0, 0).sum(0)  14.2 us
    all_to_all x1, starting transfers between devices, per_device(): p_rows = lax.all_to_all(copies, 'z', 0, 0).sum(0)  13.2 us
    all_to_all x2, starting transfers between devices, spread(): return lax.all_to_all(copies, axis, 0, 0)  12 us
    all_to_all x1, blocking collectives, per_device(): lax.all_to_all(p_part.reshape(SHARDS * NY, 8, 128), scatter, 0, 0).sum(0)  11.6 us
    ppermute x4, starting transfers between devices, swap_chip(): return lax.ppermute(value, ('x', 'c'), perm)  10.5 us
    all_to_all x1, starting transfers between devices, per_device(): units = lax.all_to_all(units, tensor, 0, 0)  10.2 us
  transfers between devices with their start and end apart: 14, of which 5 were waited for; matrix products, arithmetic and copies ran while one was open for 3% of the time, Pallas kernels for 9%

profile of v6, /device:TPU:1, one launch (start us, length us, event | category | flops | bytes accessed | tf_op | source)
XLA Modules:
  0.0 175.0 jit_solution(11086373281143105469)
XLA Ops:
  0.6 0.9 pad_maximum_fusion.1
  1.6 0.7 copy.14
  2.3 10.2 %all-to-all-start = ((bf16[8,96,128]{2,1,0:T(8,128)(2,1)}), bf16[8,96,128]{2,1,0:T(8,128)(2,1)S(1)}, u32[]{:S(2)}, u32[]{:S(2)}) async-start(bf16[8,96,128]{2,1,0:T(8,128)(2,1)} %bitcast.23), calls=%async_computation | async-start | bytes 393216 | tf_op jit(solution)/shard_map/all_to_all | solution.py:429
  12.5 0.7 pad_add_fusion.place
  13.1 5.2 %token_products.1 = (f32[128,128]{1,0:T(8,128)}, f32[32,128]{1,0:T(8,128)}, bf16[2,128,2560]{2,1,0:T(8,128)(2,1)}, bf16[2,128,2560]{2,1,0:T(8,128)(2,1)}) custom-call(s32[3]{0:T(128)} %pad_add_fusion.place, bf16[128,5120]{1,0:T(8,128)(2,1)} %x_ref.3, bf16[128,5120]{1,0:T(8,128)(2,1)} %o_ref.3, bf16[1,3,32,5120]{3,2,1,0:T(8,128)(2,1)} %error.3, ...), custom_call_target="tpu_custom_call" | custom-call | tf_op jit(solution)/shard_map/token_products/pallas_call | solution.py:81
  18.4 0.0 all-to-all-done.units
  18.4 0.0 copy-start.4
  18.4 0.8 copy-done.4
  19.2 0.7 copy-done.7
  20.0 0.3 left_product.1
  20.3 2.8 %collective-permute-start = (bf16[2,128,2560]{2,1,0:T(8,128)(2,1)}, bf16[2,128,2560]{2,1,0:T(8,128)(2,1)}, u32[]{:S(2)}, u32[]{:S(2)}) collective-permute-start(bf16[2,128,2560]{2,1,0:T(8,128)(2,1)} %get-tuple-element.41), channel_id=1, source_target_pairs={{0,1},{1,0},{2,3},{3,2},{4,5},{5,4},{6,7},{7,6},{8,9},{9,8},{10,11... | collective-permute-start | bytes 3932168 | tf_op jit(solution)/shard_map/ppermute | solution.py:349
  23.1 11.6 %all_to_all.40 = f32[32,8,128]{2,1,0:T(8,128)S(1)} all-to-all(f32[32,8,128]{2,1,0:T(8,128)S(1)} %bitcast.28), channel_id=1, replica_groups=mesh['y'=4,'z'=16,'x'=4,'c'=2] {'x','c','y'}, dimensions={0} | all-to-all | bytes 262144 | tf_op jit(solution)/shard_map/all_to_all | solution.py:433
  34.7 0.0 collective-permute-done.sibling
  34.7 0.6 broadcast_in_dim.10
  35.4 3.0 %collective-permute-start.2 = (bf16[2,128,2560]{2,1,0:T(8,128)(2,1)}, bf16[2,128,2560]{2,1,0:T(8,128)(2,1)}, u32[]{:S(2)}, u32[]{:S(2)}) collective-permute-start(bf16[2,128,2560]{2,1,0:T(8,128)(2,1)} %get-tuple-element.44.own), channel_id=1, source_target_pairs={{0,2},{1,7},{2,0},{3,5},{4,6},{5,3},{6,4},{7,1},{8,10},{9,15},{10,... | collective-permute-start | bytes 3932168 | tf_op jit(solution)/shard_map/ppermute | solution.py:401
  38.3 3.7 %collective-permute-start.4 = (bf16[2,128,2560]{2,1,0:T(8,128)(2,1)}, bf16[2,128,2560]{2,1,0:T(8,128)(2,1)}, u32[]{:S(2)}, u32[]{:S(2)}) collective-permute-start(bf16[2,128,2560]{2,1,0:T(8,128)(2,1)} %collective-permute-done.sibling), channel_id=1, source_target_pairs={{0,2},{1,7},{2,0},{3,5},{4,6},{5,3},{6,4},{7,1},{8,10},{9,15},{10,... | collective-permute-start | bytes 3932168 | tf_op jit(solution)/shard_map/ppermute | solution.py:401
  42.0 13.2 %all-to-all-start.2 = ((f32[16,8,128]{2,1,0:T(8,128)}), f32[16,8,128]{2,1,0:T(8,128)S(1)}, u32[]{:S(2)}, u32[]{:S(2)}) async-start(f32[16,8,128]{2,1,0:T(8,128)} %broadcast_in_dim.10), calls=%async_computation.2 | async-start | bytes 131072 | tf_op jit(solution)/shard_map/all_to_all | solution.py:440
  55.2 2.0 %collective-permute-start.1 = (bf16[96,1024]{1,0:T(8,128)(2,1)S(1)}, bf16[96,1024]{1,0:T(8,128)(2,1)S(1)}, u32[]{:S(2)}, u32[]{:S(2)}) collective-permute-start(bf16[96,1024]{1,0:T(8,128)(2,1)S(1)} %get-tuple-element.43), channel_id=1, source_target_pairs={{0,1},{1,0},{2,3},{3,2},{4,5},{5,4},{6,7},{7,6},{8,9},{9,8},{10,11... | collective-permute-start | bytes 589832 | tf_op jit(solution)/shard_map/ppermute | solution.py:349
  57.3 9.5 %all-to-all-done.2 = f32[16,8,128]{2,1,0:T(8,128)S(1)} async-done(((f32[16,8,128]{2,1,0:T(8,128)}), f32[16,8,128]{2,1,0:T(8,128)S(1)}, u32[]{:S(2)}, u32[]{:S(2)}) %all-to-all-start.2) | async-done | bytes 65568 | tf_op jit(solution)/shard_map/all_to_all | solution.py:440
  66.8 0.0 collective-permute-done.1
  66.8 0.0 collective-permute-done.2.pair
  66.8 0.0 copy-done.8
  66.8 0.0 copy-done.9
  66.8 0.0 copy-done.10
  66.9 0.1 constant_dynamic-slice_fusion.3
  67.0 1.9 %collective-permute-start.3 = (bf16[192,512]{1,0:T(8,128)(2,1)S(1)}, bf16[192,512]{1,0:T(8,128)(2,1)S(1)}, u32[]{:S(2)}, u32[]{:S(2)}) collective-permute-start(bf16[192,512]{1,0:T(8,128)(2,1)S(1)} %pad_maximum_fusion.2), channel_id=1, source_target_pairs={{0,6},{1,3},{2,4},{3,1},{4,2},{5,7},{6,0},{7,5},{8,14},{9,11},{10,... | collective-permute-start | bytes 589832 | tf_op jit(solution)/shard_map/ppermute | solution.py:401
  69.0 0.7 broadcast_in_dim.11
  69.6 7.1 %all-to-all-start.3 = ((f32[32,8,128]{2,1,0:T(8,128)}), f32[32,8,128]{2,1,0:T(8,128)S(1)}, u32[]{:S(2)}, u32[]{:S(2)}) async-start(f32[32,8,128]{2,1,0:T(8,128)} %broadcast_in_dim.11), calls=%async_computation.3 | async-start | bytes 262144 | tf_op jit(solution)/shard_map/all_to_all | solution.py:345
  76.7 0.0 collective-permute-done.4.pair_sibling
  76.7 7.6 %all-to-all-done.3 = f32[32,8,128]{2,1,0:T(8,128)S(1)} async-done(((f32[32,8,128]{2,1,0:T(8,128)}), f32[32,8,128]{2,1,0:T(8,128)S(1)}, u32[]{:S(2)}, u32[]{:S(2)}) %all-to-all-start.3) | async-done | bytes 131104 | tf_op jit(solution)/shard_map/all_to_all | solution.py:345
  84.3 0.0 collective-permute-done.3.away
  84.3 0.0 copy-done
  84.3 0.0 copy-done.1
  84.3 0.0 copy-done.6
  84.3 0.0 copy-start.2
  84.4 1.4 copy-done.2
  85.7 2.6 %right_away.1 = (f32[4,4,4,32,128]{4,3,2,1,0:T(8,128)S(1)}, bf16[96,384]{1,0:T(8,128)(2,1)S(1)}, bf16[128,96]{1,0:T(8,128)(2,1)S(1)}) custom-call(s32[3]{0:T(128)S(1)} %copy-done.6, f32[256,128]{1,0:T(8,128)S(1)} %bitcast.26, bf16[8,96,128]{2,1,0:T(8,128)(2,1)S(1)} %all-to-all-done.units, bf16[128,5120]{1,0:T(8,128)(2,1)S(1)} %copy-done.1, ...), custom_call_target="tpu_custom_call" | custom-call | tf_op jit(solution)/shard_map/right_away/pallas_call | solution.py:199
  88.3 0.0 copy-done.11
  88.3 2.4 %collective-permute-start.5 = (f32[4,4,4,32,128]{4,3,2,1,0:T(8,128)S(1)}, f32[4,4,4,32,128]{4,3,2,1,0:T(8,128)S(1)}, u32[]{:S(2)}, u32[]{:S(2)}) collective-permute-start(f32[4,4,4,32,128]{4,3,2,1,0:T(8,128)S(1)} %get-tuple-element.51), channel_id=1, source_target_pairs={{0,1},{1,0},{2,3},{3,2},{4,5},{5,4},{6,7},{7,6},{8,9},{9,8},{10,11... | collective-permute-start | bytes 3145736 | tf_op jit(solution)/shard_map/ppermute | solution.py:349
  90.7 2.2 %right_near.1 = f32[4,4,4,32,128]{4,3,2,1,0:T(8,128)S(1)} custom-call(s32[3]{0:T(128)S(1)} %copy-done.6, bf16[96,384]{1,0:T(8,128)(2,1)S(1)} %get-tuple-element.49.token_p, bf16[128,96]{1,0:T(8,128)(2,1)S(1)} %get-tuple-element.50.error_p, bf16[128,5120]{1,0:T(8,128)(2,1)S(1)} %copy-done.1, bf16[128,5120]{1,0:T(8,128)(2,1)S(1)} %copy-done.2, ...), custom_call_target="tpu_custom_call" | custom-call | tf_op jit(solution)/shard_map/right_near/pallas_call | solution.py:223
  92.9 0.1 collective-permute-done.5
  93.0 1.3 add.64
  94.2 3.7 %all-to-all-start.4 = ((f32[16,4,32,128]{3,2,1,0:T(8,128)}), f32[16,4,32,128]{3,2,1,0:T(8,128)S(1)}, u32[]{:S(2)}, u32[]{:S(2)}) async-start(f32[16,4,32,128]{3,2,1,0:T(8,128)} %bitcast.30), calls=%async_computation.4 | async-start | bytes 2097152 | tf_op jit(solution)/shard_map/all_to_all | solution.py:450
  97.9 0.7 pad_maximum_fusion.3.near
  98.6 4.4 %factors.1 = (f32[3,32,32]{2,1,0:T(8,128)S(1)}, f32[3,32,32]{2,1,0:T(8,128)}) custom-call(s32[3]{0:T(128)S(1)} %copy-done.6, f32[256,128]{1,0:T(8,128)S(1)} %bitcast.27), custom_call_target="tpu_custom_call" | custom-call | tf_op jit(solution)/shard_map/factors/pallas_call | solution.py:272
  103.0 4.7 %gradients.1 = (f32[3,32,2560]{2,1,0:T(8,128)}, f32[3,32,2560]{2,1,0:T(8,128)}, f32[2,3,32,2560]{3,2,1,0:T(8,128)}) custom-call(bf16[192,512]{1,0:T(8,128)(2,1)} %pad_maximum_fusion.3.near, bf16[192,512]{1,0:T(8,128)(2,1)} %copy-done.11, bf16[2,128,2560]{2,1,0:T(8,128)(2,1)} %get-tuple-element.44.own, bf16[2,128,2560]{2,1,0:T(8,128)(2,1)} %collective-permute-done.sibling, ...), custom_call_target="tpu_custom_call" | custom-call | tf_op jit(solution)/shard_map/gradients/pallas_call | solution.py:328
  107.7 6.7 %all-to-all-done.4.received = f32[16,4,32,128]{3,2,1,0:T(8,128)S(1)} async-done(((f32[16,4,32,128]{3,2,1,0:T(8,128)}), f32[16,4,32,128]{3,2,1,0:T(8,128)S(1)}, u32[]{:S(2)}, u32[]{:S(2)}) %all-to-all-start.4) | async-done | bytes 1048608 | tf_op jit(solution)/shard_map/all_to_all | solution.py:450
  114.4 0.8 scaled_sum.1
  115.2 1.9 %collective-permute-start.7 = (f32[2,3,32,2560]{3,2,1,0:T(8,128)}, f32[2,3,32,2560]{3,2,1,0:T(8,128)S(1)}, u32[]{:S(2)}, u32[]{:S(2)}) collective-permute-start(f32[2,3,32,2560]{3,2,1,0:T(8,128)} %get-tuple-element.65), channel_id=1, source_target_pairs={{0,6},{1,3},{2,4},{3,1},{4,2},{5,7},{6,0},{7,5},{8,14},{9,11},{10,... | collective-permute-start | bytes 5898248 | tf_op jit(solution)/shard_map/ppermute | solution.py:401
  117.1 14.2 %all_to_all.41 = f32[16,8,128]{2,1,0:T(8,128)S(1)} all-to-all(f32[16,8,128]{2,1,0:T(8,128)S(1)} %bitcast.29), channel_id=1, replica_groups=mesh['y'=4,'z'=16,'x'=4,'c'=2] {'z'}, dimensions={0} | all-to-all | bytes 131072 | tf_op jit(solution)/shard_map/all_to_all | solution.py:458
  131.4 14.4 %all_to_all.42 = bf16[16,8,128]{2,1,0:T(8,128)(2,1)S(1)} all-to-all(bf16[16,8,128]{2,1,0:T(8,128)(2,1)S(1)} %broadcast_in_dim.12), channel_id=1, replica_groups=mesh['y'=4,'z'=16,'x'=4,'c'=2] {'z'}, dimensions={0} | all-to-all | bytes 65536 | tf_op jit(solution)/shard_map/all_to_all | solution.py:345
  145.8 0.9 broadcast_in_dim.14
  146.7 4.9 %all-to-all-start.7 = ((bf16[16,4,32,128]{3,2,1,0:T(8,128)(2,1)}), bf16[16,4,32,128]{3,2,1,0:T(8,128)(2,1)S(1)}, u32[]{:S(2)}, u32[]{:S(2)}) async-start(bf16[16,4,32,128]{3,2,1,0:T(8,128)(2,1)} %broadcast_in_dim.14), calls=%async_computation.7 | async-start | bytes 1048576 | tf_op jit(solution)/shard_map/all_to_all | solution.py:345
  151.6 0.0 copy-start.5
  151.6 0.0 collective-permute-done.7.far
  151.6 2.3 %fusion = f32[3,32,2560]{2,1,0:T(8,128)} fusion(f32[3,32,2560]{2,1,0:T(8,128)} %get-tuple-element.66, f32[2,3,32,2560]{3,2,1,0:T(8,128)S(1)} %collective-permute-done.7.far), kind=kLoop, calls=%fused_computation.1 | loop fusion | flops 245760 | bytes 2949120 | tf_op jit(solution)/shard_map/add | solution.py:464
  153.8 7.6 %collective-permute-start.8 = (f32[3,32,2560]{2,1,0:T(8,128)}, f32[3,32,2560]{2,1,0:T(8,128)}, u32[]{:S(2)}, u32[]{:S(2)}) collective-permute-start(f32[3,32,2560]{2,1,0:T(8,128)} %fusion), channel_id=1, source_target_pairs={{0,1},{1,0},{2,3},{3,2},{4,5},{5,4},{6,7},{7,6},{8,9},{9,8},{10,11... | collective-permute-start | bytes 2949128 | tf_op jit(solution)/shard_map/ppermute | solution.py:349
  161.5 0.0 all-to-all-done.7
  161.5 7.8 %collective-permute-start.6 = (bf16[4,16,32,128]{3,2,1,0:T(8,128)(2,1)S(1)}, bf16[4,16,32,128]{3,2,1,0:T(8,128)(2,1)S(1)}, u32[]{:S(2)}, u32[]{:S(2)}) collective-permute-start(bf16[4,16,32,128]{3,2,1,0:T(8,128)(2,1)S(1)} %bitcast.24), channel_id=1, source_target_pairs={{0,1},{1,0},{2,3},{3,2},{4,5},{5,4},{6,7},{7,6},{8,9},{9,8},{10,11... | collective-permute-start | bytes 1572872 | tf_op jit(solution)/shard_map/ppermute | solution.py:349
  169.3 1.5 collective-permute-done.6.q_far
  170.8 0.0 collective-permute-done.8.other
  170.8 0.0 copy-done.5
  170.8 1.2 copy-done.3
  172.0 3.0 %new_error.1 = (bf16[3,32,5120]{2,1,0:T(8,128)(2,1)}, bf16[1,3,32,5120]{3,2,1,0:T(8,128)(2,1)}) custom-call(s32[3]{0:T(128)S(1)} %copy-done.6, bf16[4,16,32,128]{3,2,1,0:T(8,128)(2,1)S(1)} %bitcast.25, bf16[4,16,32,128]{3,2,1,0:T(8,128)(2,1)S(1)} %collective-permute-done.6.q_far, f32[3,32,32]{2,1,0:T(8,128)S(1)} %copy-done.5, f32[3,32,2560]{2,1,0:T(8,128)S(1)} %copy-done.3, ...), custom_call_target="tpu_custom_call" | custom-call | tf_op jit(solution)/shard_map/new_error/pallas_call | solution.py:379
  (16 shorter events, 0.2 us)
Async XLA Ops:
  2.3 16.1 %all-to-all-start = ((bf16[8,96,128]{2,1,0:T(8,128)(2,1)}), bf16[8,96,128]{2,1,0:T(8,128)(2,1)S(1)}, u32[]{:S(2)}, u32[]{:S(2)}) async-start(bf16[8,96,128]{2,1,0:T(8,128)(2,1)} %bitcast.23), calls=%async_computation | async-start | bytes 393216 | tf_op jit(solution)/shard_map/all_to_all | solution.py:429
  13.1 53.7 %copy-start.8 = (bf16[1024,32]{0,1:T(8,128)(2,1)S(1)}, bf16[1024,32]{0,1:T(8,128)(2,1)}, u32[]{:S(2)}) copy-start(bf16[1024,32]{0,1:T(8,128)(2,1)} %param.9) | copy-start | bytes 196612
  13.1 53.7 %copy-start.9 = (bf16[1024,32]{0,1:T(8,128)(2,1)S(1)}, bf16[1024,32]{0,1:T(8,128)(2,1)}, u32[]{:S(2)}) copy-start(bf16[1024,32]{0,1:T(8,128)(2,1)} %param.11) | copy-start | bytes 196612
  13.1 53.7 %copy-start.10 = (bf16[1024,32]{0,1:T(8,128)(2,1)S(1)}, bf16[1024,32]{0,1:T(8,128)(2,1)}, u32[]{:S(2)}) copy-start(bf16[1024,32]{0,1:T(8,128)(2,1)} %param.10) | copy-start | bytes 196612
  18.4 0.8 copy-start.4
  19.2 0.7 copy-start.7
  20.3 14.5 %collective-permute-start = (bf16[2,128,2560]{2,1,0:T(8,128)(2,1)}, bf16[2,128,2560]{2,1,0:T(8,128)(2,1)}, u32[]{:S(2)}, u32[]{:S(2)}) collective-permute-start(bf16[2,128,2560]{2,1,0:T(8,128)(2,1)} %get-tuple-element.41), channel_id=1, source_target_pairs={{0,1},{1,0},{2,3},{3,2},{4,5},{5,4},{6,7},{7,6},{8,9},{9,8},{10,11... | collective-permute-start | bytes 3932168 | tf_op jit(solution)/shard_map/ppermute | solution.py:349
  35.4 48.9 %copy-start = (bf16[1,3,32,5120]{3,2,1,0:T(8,128)(2,1)S(1)}, bf16[1,3,32,5120]{3,2,1,0:T(8,128)(2,1)}, u32[]{:S(2)}) copy-start(bf16[1,3,32,5120]{3,2,1,0:T(8,128)(2,1)} %error.3) | copy-start | bytes 2949124
  35.4 48.9 %copy-start.1 = (bf16[128,5120]{1,0:T(8,128)(2,1)S(1)}, bf16[128,5120]{1,0:T(8,128)(2,1)}, u32[]{:S(2)}) copy-start(bf16[128,5120]{1,0:T(8,128)(2,1)} %x_ref.3) | copy-start | bytes 3932164
  35.4 49.0 %copy-start.6 = (s32[3]{0:T(128)S(1)}, s32[3]{0:T(128)}, u32[]{:S(2)}) copy-start(s32[3]{0:T(128)} %pad_add_fusion.place) | copy-start | bytes 40
  35.4 31.4 %collective-permute-start.2 = (bf16[2,128,2560]{2,1,0:T(8,128)(2,1)}, bf16[2,128,2560]{2,1,0:T(8,128)(2,1)}, u32[]{:S(2)}, u32[]{:S(2)}) collective-permute-start(bf16[2,128,2560]{2,1,0:T(8,128)(2,1)} %get-tuple-element.44.own), channel_id=1, source_target_pairs={{0,2},{1,7},{2,0},{3,5},{4,6},{5,3},{6,4},{7,1},{8,10},{9,15},{10,... | collective-permute-start | bytes 3932168 | tf_op jit(solution)/shard_map/ppermute | solution.py:401
  38.3 38.4 %collective-permute-start.4 = (bf16[2,128,2560]{2,1,0:T(8,128)(2,1)}, bf16[2,128,2560]{2,1,0:T(8,128)(2,1)}, u32[]{:S(2)}, u32[]{:S(2)}) collective-permute-start(bf16[2,128,2560]{2,1,0:T(8,128)(2,1)} %collective-permute-done.sibling), channel_id=1, source_target_pairs={{0,2},{1,7},{2,0},{3,5},{4,6},{5,3},{6,4},{7,1},{8,10},{9,15},{10,... | collective-permute-start | bytes 3932168 | tf_op jit(solution)/shard_map/ppermute | solution.py:401
  42.0 24.8 %all-to-all-start.2 = ((f32[16,8,128]{2,1,0:T(8,128)}), f32[16,8,128]{2,1,0:T(8,128)S(1)}, u32[]{:S(2)}, u32[]{:S(2)}) async-start(f32[16,8,128]{2,1,0:T(8,128)} %broadcast_in_dim.10), calls=%async_computation.2 | async-start | bytes 131072 | tf_op jit(solution)/shard_map/all_to_all | solution.py:440
  55.2 11.6 %collective-permute-start.1 = (bf16[96,1024]{1,0:T(8,128)(2,1)S(1)}, bf16[96,1024]{1,0:T(8,128)(2,1)S(1)}, u32[]{:S(2)}, u32[]{:S(2)}) collective-permute-start(bf16[96,1024]{1,0:T(8,128)(2,1)S(1)} %get-tuple-element.43), channel_id=1, source_target_pairs={{0,1},{1,0},{2,3},{3,2},{4,5},{5,4},{6,7},{7,6},{8,9},{9,8},{10,11... | collective-permute-start | bytes 589832 | tf_op jit(solution)/shard_map/ppermute | solution.py:349
  67.0 17.3 %collective-permute-start.3 = (bf16[192,512]{1,0:T(8,128)(2,1)S(1)}, bf16[192,512]{1,0:T(8,128)(2,1)S(1)}, u32[]{:S(2)}, u32[]{:S(2)}) collective-permute-start(bf16[192,512]{1,0:T(8,128)(2,1)S(1)} %pad_maximum_fusion.2), channel_id=1, source_target_pairs={{0,6},{1,3},{2,4},{3,1},{4,2},{5,7},{6,0},{7,5},{8,14},{9,11},{10,... | collective-permute-start | bytes 589832 | tf_op jit(solution)/shard_map/ppermute | solution.py:401
  69.6 14.7 %all-to-all-start.3 = ((f32[32,8,128]{2,1,0:T(8,128)}), f32[32,8,128]{2,1,0:T(8,128)S(1)}, u32[]{:S(2)}, u32[]{:S(2)}) async-start(f32[32,8,128]{2,1,0:T(8,128)} %broadcast_in_dim.11), calls=%async_computation.3 | async-start | bytes 262144 | tf_op jit(solution)/shard_map/all_to_all | solution.py:345
  84.3 4.0 %copy-start.11 = (bf16[192,512]{1,0:T(8,128)(2,1)}, bf16[192,512]{1,0:T(8,128)(2,1)S(1)}, u32[]{:S(2)}) copy-start(bf16[192,512]{1,0:T(8,128)(2,1)S(1)} %collective-permute-done.3.away) | copy-start | bytes 589828
  84.3 1.4 copy-start.2
  88.3 4.7 %collective-permute-start.5 = (f32[4,4,4,32,128]{4,3,2,1,0:T(8,128)S(1)}, f32[4,4,4,32,128]{4,3,2,1,0:T(8,128)S(1)}, u32[]{:S(2)}, u32[]{:S(2)}) collective-permute-start(f32[4,4,4,32,128]{4,3,2,1,0:T(8,128)S(1)} %get-tuple-element.51), channel_id=1, source_target_pairs={{0,1},{1,0},{2,3},{3,2},{4,5},{5,4},{6,7},{7,6},{8,9},{9,8},{10,11... | collective-permute-start | bytes 3145736 | tf_op jit(solution)/shard_map/ppermute | solution.py:349
  94.2 20.2 %all-to-all-start.4 = ((f32[16,4,32,128]{3,2,1,0:T(8,128)}), f32[16,4,32,128]{3,2,1,0:T(8,128)S(1)}, u32[]{:S(2)}, u32[]{:S(2)}) async-start(f32[16,4,32,128]{3,2,1,0:T(8,128)} %bitcast.30), calls=%async_computation.4 | async-start | bytes 2097152 | tf_op jit(solution)/shard_map/all_to_all | solution.py:450
  115.2 36.4 %collective-permute-start.7 = (f32[2,3,32,2560]{3,2,1,0:T(8,128)}, f32[2,3,32,2560]{3,2,1,0:T(8,128)S(1)}, u32[]{:S(2)}, u32[]{:S(2)}) collective-permute-start(f32[2,3,32,2560]{3,2,1,0:T(8,128)} %get-tuple-element.65), channel_id=1, source_target_pairs={{0,6},{1,3},{2,4},{3,1},{4,2},{5,7},{6,0},{7,5},{8,14},{9,11},{10,... | collective-permute-start | bytes 5898248 | tf_op jit(solution)/shard_map/ppermute | solution.py:401
  146.7 14.8 %all-to-all-start.7 = ((bf16[16,4,32,128]{3,2,1,0:T(8,128)(2,1)}), bf16[16,4,32,128]{3,2,1,0:T(8,128)(2,1)S(1)}, u32[]{:S(2)}, u32[]{:S(2)}) async-start(bf16[16,4,32,128]{3,2,1,0:T(8,128)(2,1)} %broadcast_in_dim.14), calls=%async_computation.7 | async-start | bytes 1048576 | tf_op jit(solution)/shard_map/all_to_all | solution.py:345
  151.6 19.2 %copy-start.5 = (f32[3,32,32]{2,1,0:T(8,128)S(1)}, f32[3,32,32]{2,1,0:T(8,128)}, u32[]{:S(2)}) copy-start(f32[3,32,32]{2,1,0:T(8,128)} %get-tuple-element.34.p_factor) | copy-start | bytes 36868
  153.8 17.0 %collective-permute-start.8 = (f32[3,32,2560]{2,1,0:T(8,128)}, f32[3,32,2560]{2,1,0:T(8,128)}, u32[]{:S(2)}, u32[]{:S(2)}) collective-permute-start(f32[3,32,2560]{2,1,0:T(8,128)} %fusion), channel_id=1, source_target_pairs={{0,1},{1,0},{2,3},{3,2},{4,5},{5,4},{6,7},{7,6},{8,9},{9,8},{10,11... | collective-permute-start | bytes 2949128 | tf_op jit(solution)/shard_map/ppermute | solution.py:349
  161.5 9.3 %collective-permute-start.6 = (bf16[4,16,32,128]{3,2,1,0:T(8,128)(2,1)S(1)}, bf16[4,16,32,128]{3,2,1,0:T(8,128)(2,1)S(1)}, u32[]{:S(2)}, u32[]{:S(2)}) collective-permute-start(bf16[4,16,32,128]{3,2,1,0:T(8,128)(2,1)S(1)} %bitcast.24), channel_id=1, source_target_pairs={{0,1},{1,0},{2,3},{3,2},{4,5},{5,4},{6,7},{7,6},{8,9},{9,8},{10,11... | collective-permute-start | bytes 1572872 | tf_op jit(solution)/shard_map/ppermute | solution.py:349
  170.8 1.2 copy-start.3

commit v7 on v6

--- a/solution.py
+++ b/solution.py
@@ -149,7 +149,7 @@
     out[0, NY - 1, 3] = jnp.zeros((RANK, 128), F32)
 
 
-def away_kernel(place, p_sum, units, x_ref, o_ref, e_ref, out, token_p, error_p):
+def away_kernel(core_ref, shard_ref, p_sum, units, x_ref, o_ref, e_ref, out, token_p, error_p):
     @pl.when(pl.program_id(0) == 0)
     def _():
         columns = jnp.concatenate(
@@ -169,7 +169,7 @@
             token_p[rows] = jnp.concatenate(
                 split3(total[rows, m * OWN : (m + 1) * OWN]), axis=1
             )
-        mine = p_sum[pl.ds(pl.multiple_of(place[1] * ROWS, ROWS), ROWS)]
+        mine = p_sum[pl.ds(pl.multiple_of(shard_ref[0] * ROWS, ROWS), ROWS)]
         error_p[...] = jnp.concatenate([part.T for part in split3(mine)], axis=1)
 
     right_half(token_p, error_p, x_ref, o_ref, e_ref, out)
@@ -183,27 +183,27 @@
     def column(i, at):
         return (at[0] if stays else 1 - at[0]) * NX + i
 
-    x_spec = pl.BlockSpec((OWN, PIECE), lambda i, at: (0, column(i, at)))
-    e_spec = pl.BlockSpec((1, 3, ROWS, PIECE), lambda i, at: (0, 0, 0, column(i, at)))
-    out_spec = pl.BlockSpec((1, NY, 4, RANK, 128), lambda i, at: (i, 0, 0, 0, 0))
-    token_spec = pl.BlockSpec((3 * RANK, 3 * OWN), lambda i, at: (0, 0))
-    error_spec = pl.BlockSpec((128, 3 * ROWS), lambda i, at: (0, 0))
+    x_spec = pl.BlockSpec((OWN, PIECE), lambda i, at, *rest: (0, column(i, at)))
+    e_spec = pl.BlockSpec((1, 3, ROWS, PIECE), lambda i, at, *rest: (0, 0, 0, column(i, at)))
+    out_spec = pl.BlockSpec((1, NY, 4, RANK, 128), lambda i, *at: (i, 0, 0, 0, 0))
+    token_spec = pl.BlockSpec((3 * RANK, 3 * OWN), lambda i, *at: (0, 0))
+    error_spec = pl.BlockSpec((128, 3 * ROWS), lambda i, *at: (0, 0))
     return [x_spec, x_spec, e_spec], out_spec, [token_spec, error_spec]
 
 
 RIGHT_SHAPE = jax.ShapeDtypeStruct((NX, NY, 4, RANK, 128), F32)
 
 
-def right_away(place, p_sum, units, inputs, out_grad, error):
+def right_away(core, shard, p_sum, units, inputs, out_grad, error):
     blocks, out_spec, left_specs = right_specs(False)
     return pl.pallas_call(
         away_kernel,
         grid_spec=pltpu.PrefetchScalarGridSpec(
-            num_scalar_prefetch=1,
+            num_scalar_prefetch=2,
             grid=(NX,),
             in_specs=[
-                pl.BlockSpec((SHARDS * ROWS, 128), lambda i, at: (0, 0)),
-                pl.BlockSpec((SHARDS, 3 * ROWS, OWN), lambda i, at: (0, 0, 0)),
+                pl.BlockSpec((SHARDS * ROWS, 128), lambda i, *at: (0, 0)),
+                pl.BlockSpec((SHARDS, 3 * ROWS, OWN), lambda i, *at: (0, 0, 0)),
             ]
             + blocks,
             out_specs=[out_spec] + left_specs,
@@ -215,10 +215,10 @@
         ],
         compiler_params=params(),
         name="right_away",
-    )(place, p_sum, units, inputs, out_grad, error)
-
-
-def right_near(place, token_p, error_p, inputs, out_grad, error):
+    )(core, shard, p_sum, units, inputs, out_grad, error)
+
+
+def right_near(core, token_p, error_p, inputs, out_grad, error):
     blocks, out_spec, left_specs = right_specs(True)
     return pl.pallas_call(
         near_kernel,
@@ -231,10 +231,10 @@
         out_shape=RIGHT_SHAPE,
         compiler_params=params(),
         name="right_near",
-    )(place, token_p, error_p, inputs, out_grad, error)
-
-
-def factor_kernel(place, p_sum, inverse, p_factor):
+    )(core, token_p, error_p, inputs, out_grad, error)
+
+
+def factor_kernel(shard_ref, p_sum, inverse, p_factor):
     lane = lax.broadcasted_iota(jnp.int32, (3, RANK, RANK), 2)
     row = lax.broadcasted_iota(jnp.int32, (3, RANK, RANK), 1)
     whole = p_sum[...]
@@ -256,7 +256,7 @@
     diagonal = jnp.sum(jnp.where(lane == row, left, 0.0), axis=2, keepdims=True)
     result = right / jnp.sqrt(diagonal)
     inverse[...] = result
-    mine = p_sum[pl.ds(pl.multiple_of(place[1] * ROWS, ROWS), ROWS)]
+    mine = p_sum[pl.ds(pl.multiple_of(shard_ref[0] * ROWS, ROWS), ROWS)]
     for m in range(3):
         p_factor[m] = lax.dot_general(
             columns_of(mine, m),
@@ -267,7 +267,7 @@
         )
 
 
-def factors(place, p_sum):
+def factors(shard, p_sum):
     shape = jax.ShapeDtypeStruct((3, RANK, RANK), F32)
     return pl.pallas_call(
         factor_kernel,
@@ -275,12 +275,12 @@
         out_shape=[shape, shape],
         compiler_params=params(),
         name="factors",
-    )(place, p_sum)
-
-
-def scale_kernel(place, received, inverse, q_part):
+    )(shard, p_sum)
+
+
+def scale_kernel(row_ref, received, inverse, q_part):
     for slot in range(4):
-        unit = place[2] * 4 + slot
+        unit = row_ref[0] * 4 + slot
         of_unit = jnp.where(
             unit < BLOCKS, inverse[0], jnp.where(unit < 2 * BLOCKS, inverse[1], inverse[2])
         )
@@ -290,14 +290,14 @@
         q_part[slot] = jnp.dot(of_unit, total, preferred_element_type=F32, precision=PRECISE)
 
 
-def scaled_sum(place, received, inverse):
+def scaled_sum(row, received, inverse):
     return pl.pallas_call(
         scale_kernel,
         in_specs=[SMEM] + [pl.BlockSpec(memory_space=pltpu.VMEM)] * 2,
         out_shape=jax.ShapeDtypeStruct((4, RANK, 128), F32),
         compiler_params=params(),
         name="scaled_sum",
-    )(place, received, inverse)
+    )(row, received, inverse)
 
 
 def gradient_kernel(near, away, own, sibling, pair, pair_sibling, mine, beside, far):
@@ -401,6 +401,19 @@
     return lax.ppermute(value, ("x", "c"), perm)
 
 
+def swap_across(value):
+    perm = []
+    for chip in range(NX):
+        for core in range(NC):
+            to = chip ^ 1 if core == 1 else 3 - chip
+            perm.append((chip * NC + core, to * NC + 1 - core))
+    return lax.ppermute(value, ("x", "c"), perm)
+
+
+def hidden_columns(up_grad, gate_grad, hidden):
+    return jnp.concatenate([up_grad.T, gate_grad.T, hidden.T], axis=0)
+
+
 def pair_columns(columns, beside):
     chip, core = lax.axis_index("x"), lax.axis_index("c")
     both = jnp.concatenate([columns, beside], axis=0)
@@ -418,41 +431,42 @@
 def per_device(inputs, out_grad, hidden, up_grad, gate_grad, error_memory, q_start):
     core, row = lax.axis_index("c"), lax.axis_index("y")
     shard = lax.axis_index("x") * NC + core
-    place = jnp.stack([core, shard, row]).astype(jnp.int32)
+    core, shard, row = (at.reshape(1).astype(jnp.int32) for at in (core, shard, row))
     tensor, scatter = ("x", "c"), ("x", "c", "y")
     token_q, error_q, keep, sent = token_products(
-        place, inputs, out_grad, error_memory, q_start
-    )
-
-    columns = jnp.concatenate([up_grad.T, gate_grad.T, hidden.T], axis=0)
-    units = columns.reshape(3 * ROWS, SHARDS, OWN).transpose(1, 0, 2)
+        core, inputs, out_grad, error_memory, q_start
+    )
+
+    units = hidden_columns(up_grad, gate_grad, hidden)
+    units = units.reshape(3 * ROWS, SHARDS, OWN).transpose(1, 0, 2)
     units = lax.all_to_all(units, tensor, 0, 0)
-    p_part = left_product(place[1:2], units, token_q, error_q)
-    p_part, late_sent = lax.optimization_barrier((p_part, sent))
-    sibling = swap_core(late_sent)
+    p_part = left_product(shard, units, token_q, error_q)
     p_rows = lax.all_to_all(p_part.reshape(SHARDS * NY, 8, 128), scatter, 0, 0).sum(0)
     copies = jnp.broadcast_to(p_rows[None], (NZ,) + p_rows.shape)
-    copies, late_keep, late_sibling, late_columns = lax.optimization_barrier(
-        (copies, keep, sibling, columns)
-    )
-    pair, pair_sibling = swap_chip(late_keep, 0), swap_chip(late_sibling, 0)
+    late = lax.optimization_barrier((copies, keep, sent, up_grad, gate_grad, hidden))
+    copies, late_keep, late_sent = late[:3]
+    late_columns = hidden_columns(*late[3:])
+    pair, pair_sibling = swap_chip(late_keep, 0), swap_across(late_sent)
     columns_beside = swap_core(late_columns)
     p_rows = lax.all_to_all(copies, "z", 0, 0).sum(0)
-    p_rows, columns_beside, pair = lax.optimization_barrier((p_rows, columns_beside, pair))
-    u_near, u_away = pair_columns(columns, columns_beside)
+    p_rows, columns_beside = lax.optimization_barrier((p_rows, columns_beside))
+    u_near, u_away = pair_columns(late_columns, columns_beside)
     p_sum = spread(p_rows, scatter, SHARDS * NY).reshape(SHARDS * ROWS, 128)
-    p_sum, u_away, pair_sibling = lax.optimization_barrier((p_sum, u_away, pair_sibling))
-
-    away, token_p, error_p = right_away(place, p_sum, units, inputs, out_grad, error_memory)
-    near = right_near(place, token_p, error_p, inputs, out_grad, error_memory)
+    p_sum, u_away, pair, pair_sibling, late_sent = lax.optimization_barrier(
+        (p_sum, u_away, pair, pair_sibling, late_sent)
+    )
+    sibling = swap_core(late_sent)
+
+    away, token_p, error_p = right_away(core, shard, p_sum, units, inputs, out_grad, error_memory)
+    near = right_near(core, token_p, error_p, inputs, out_grad, error_memory)
     w_core = (near + swap_core(away)).reshape(NX * NY, 4, RANK, 128)
-    inverse, p_factor = factors(place, p_sum)
+    inverse, p_factor = factors(shard, p_sum)
     received = lax.all_to_all(w_core, ("x", "y"), 0, 0)
     mine, beside, away_sums = gradients(u_near, u_away, (keep, sibling, pair, pair_sibling))
     received, mine, beside, away_sums, inverse = lax.optimization_barrier(
         (received, mine, beside, away_sums, inverse)
     )
-    q_y = scaled_sum(place, received, inverse)
+    q_y = scaled_sum(row, received, inverse)
     q_y, away_sums = lax.optimization_barrier((q_y, away_sums))
     far = swap_chip(away_sums, 1)
     q_z = lax.all_to_all(q_y.reshape(NZ, 8, 128), "z", 0, 0).sum(0)
@@ -463,7 +477,7 @@
 
     other = swap_core(beside + far[1])
     q_factor, error_next = new_error(
-        place, q_near, swap_core(q_near), p_factor, mine, far, other, error_memory
+        core, q_near, swap_core(q_near), p_factor, mine, far, other, error_memory
     )
     return (error_next, p_factor, q_factor)
 

time: 176 us -> 172 us (0.977)
  blocking collectives: 40.2 us -> 55.7 us
  starting transfers between devices: 72.1 us -> 63.2 us
  waiting for transfers between devices: 25.4 us -> 19.1 us
  Pallas kernels: 23.2 us -> 20.2 us
    all_to_all x1 -> x2, blocking collectives: 14.4 us -> 28.5 us  [spread(): return lax.all_to_all(copies, axis, 0, 0)]
    all_to_all x2 -> x1, waiting for transfers between devices: 7.57 us -> 0.01 us  [spread(): return lax.all_to_all(copies, axis, 0, 0)]
    all_to_all x2 -> x1, starting transfers between devices: 12 us -> 5.04 us  [spread(): return lax.all_to_all(copies, axis, 0, 0)]
    ppermute x4 -> x3, starting transfers between devices: 10.5 us -> 6.98 us  [swap_chip(): return lax.ppermute(value, ('x', 'c'), perm)]
    ppermute x0 -> x1, starting transfers between devices: none -> 2.57 us  [swap_across(): return lax.ppermute(value, ('x', 'c'), perm)]
    unnamed x24 -> x22, local copies, waits for them, and re-layouts: 4.16 us -> 4.16 us
  transfers between devices with their start and end apart: 14 -> 13, of which waited for: 5 -> 4; matrix products, arithmetic and copies ran while one was open for 3% -> 3% of each run, Pallas kernels for 9% -> 9%
where the time goes in v7:
time: 172 us; the launch traced here: 171 us
  starting transfers between devices  63.2 us (37%)
  blocking collectives  55.7 us (32%)
  Pallas kernels  20.2 us (12%)
  waiting for transfers between devices  19.1 us (11%)
  other arithmetic  5.98 us (3%)
  local copies, waits for them, and re-layouts  5.85 us (3%)
    all_to_all x2, blocking collectives, spread(): return lax.all_to_all(copies, axis, 0, 0)  28.5 us
    ppermute x5, starting transfers between devices, swap_core(): return lax.ppermute(value, 'c', [(0, 1), (1, 0)])  21.9 us
    all_to_all x1, blocking collectives, per_device(): q_z = lax.all_to_all(q_y.reshape(NZ, 8, 128), 'z', 0, 0).sum(0)  15.9 us
    all_to_all x1, starting transfers between devices, per_device(): p_rows = lax.all_to_all(copies, 'z', 0, 0).sum(0)  12.8 us
    all_to_all x1, blocking collectives, per_device(): lax.all_to_all(p_part.reshape(SHARDS * NY, 8, 128), scatter, 0, 0).sum(0)  11.3 us
    all_to_all x1, starting transfers between devices, per_device(): units = lax.all_to_all(units, tensor, 0, 0)  10.2 us
    all_to_all x1, waiting for transfers between devices, per_device(): p_rows = lax.all_to_all(copies, 'z', 0, 0).sum(0)  9.56 us
    ppermute x3, starting transfers between devices, swap_chip(): return lax.ppermute(value, ('x', 'c'), perm)  6.98 us
  transfers between devices with their start and end apart: 13, of which 4 were waited for; matrix products, arithmetic and copies ran while one was open for 3% of the time, Pallas kernels for 9%

profile of v7, /device:TPU:1, one launch (start us, length us, event | category | flops | bytes accessed | tf_op | source)
XLA Modules:
  0.0 171.0 jit_solution(7761423951671850799)
XLA Ops:
  0.6 1.6 bitcast_bitcast_fusion
  2.2 10.2 %all-to-all-start = ((bf16[8,96,128]{2,1,0:T(8,128)(2,1)}), bf16[8,96,128]{2,1,0:T(8,128)(2,1)S(1)}, u32[]{:S(2)}, u32[]{:S(2)}) async-start(bf16[8,96,128]{2,1,0:T(8,128)(2,1)} %bitcast_bitcast_fusion), calls=%async_computation | async-start | bytes 393216 | tf_op jit(solution)/shard_map/all_to_all | solution.py:442
  12.4 0.0 copy-start.7
  12.4 0.0 copy-start.8
  12.4 0.0 copy-start.9
  12.4 4.5 %token_products.1 = (f32[128,128]{1,0:T(8,128)}, f32[32,128]{1,0:T(8,128)}, bf16[2,128,2560]{2,1,0:T(8,128)(2,1)}, bf16[2,128,2560]{2,1,0:T(8,128)(2,1)}) custom-call(s32[1]{0:T(128)} %bitcast.place.core_ref, bf16[128,5120]{1,0:T(8,128)(2,1)} %x_ref.3, bf16[128,5120]{1,0:T(8,128)(2,1)} %o_ref.3, bf16[1,3,32,5120]{3,2,1,0:T(8,128)(2,1)} %error.3, ...), custom_call_target="tpu_custom_call" | custom-call | tf_op jit(solution)/shard_map/token_products/pallas_call | solution.py:81
  16.9 1.4 all-to-all-done.units
  18.3 0.8 copy-done.4
  19.2 0.0 copy-start.6
  19.2 0.7 copy-done.6
  19.9 0.3 left_product.1
  20.2 11.3 %all_to_all.40 = f32[32,8,128]{2,1,0:T(8,128)S(1)} all-to-all(f32[32,8,128]{2,1,0:T(8,128)S(1)} %bitcast.30), channel_id=1, replica_groups=mesh['y'=4,'z'=16,'x'=4,'c'=2] {'x','c','y'}, dimensions={0} | all-to-all | bytes 262144 | tf_op jit(solution)/shard_map/all_to_all | solution.py:444
  31.5 0.6 broadcast_in_dim.10
  32.1 2.6 %collective-permute-start.3 = (bf16[2,128,2560]{2,1,0:T(8,128)(2,1)}, bf16[2,128,2560]{2,1,0:T(8,128)(2,1)}, u32[]{:S(2)}, u32[]{:S(2)}) collective-permute-start(bf16[2,128,2560]{2,1,0:T(8,128)(2,1)} %get-tuple-element.54), channel_id=1, source_target_pairs={{0,7},{1,2},{2,5},{3,0},{4,3},{5,6},{6,1},{7,4},{8,15},{9,10},{10,... | collective-permute-start | bytes 3932168 | tf_op jit(solution)/shard_map/ppermute | solution.py:410
  34.7 2.9 %collective-permute-start.2 = (bf16[2,128,2560]{2,1,0:T(8,128)(2,1)}, bf16[2,128,2560]{2,1,0:T(8,128)(2,1)}, u32[]{:S(2)}, u32[]{:S(2)}) collective-permute-start(bf16[2,128,2560]{2,1,0:T(8,128)(2,1)} %get-tuple-element.47.own), channel_id=1, source_target_pairs={{0,2},{1,7},{2,0},{3,5},{4,6},{5,3},{6,4},{7,1},{8,10},{9,15},{10,... | collective-permute-start | bytes 3932168 | tf_op jit(solution)/shard_map/ppermute | solution.py:401
  37.6 12.8 %all-to-all-start.2 = ((f32[16,8,128]{2,1,0:T(8,128)}), f32[16,8,128]{2,1,0:T(8,128)S(1)}, u32[]{:S(2)}, u32[]{:S(2)}) async-start(f32[16,8,128]{2,1,0:T(8,128)} %broadcast_in_dim.10), calls=%async_computation.2 | async-start | bytes 131072 | tf_op jit(solution)/shard_map/all_to_all | solution.py:451
  50.5 0.0 copy-done.7
  50.5 0.0 copy-done.8
  50.5 0.0 copy-done.9
  50.5 0.0 copy-start
  50.5 0.0 copy-start.1
  50.5 2.1 %collective-permute-start = (bf16[96,1024]{1,0:T(8,128)(2,1)S(1)}, bf16[96,1024]{1,0:T(8,128)(2,1)S(1)}, u32[]{:S(2)}, u32[]{:S(2)}) collective-permute-start(bf16[96,1024]{1,0:T(8,128)(2,1)S(1)} %pad_maximum_fusion.1), channel_id=1, source_target_pairs={{0,1},{1,0},{2,3},{3,2},{4,5},{5,4},{6,7},{7,6},{8,9},{9,8},{10,11... | collective-permute-start | bytes 589832 | tf_op jit(solution)/shard_map/ppermute | solution.py:349
  52.7 9.6 %all-to-all-done.2 = f32[16,8,128]{2,1,0:T(8,128)S(1)} async-done(((f32[16,8,128]{2,1,0:T(8,128)}), f32[16,8,128]{2,1,0:T(8,128)S(1)}, u32[]{:S(2)}, u32[]{:S(2)}) %all-to-all-start.2) | async-done | bytes 65568 | tf_op jit(solution)/shard_map/all_to_all | solution.py:451
  62.2 0.0 collective-permute-done
  62.3 0.1 constant_dynamic-slice_fusion.3
  62.5 2.2 %collective-permute-start.1 = (bf16[192,512]{1,0:T(8,128)(2,1)S(1)}, bf16[192,512]{1,0:T(8,128)(2,1)S(1)}, u32[]{:S(2)}, u32[]{:S(2)}) collective-permute-start(bf16[192,512]{1,0:T(8,128)(2,1)S(1)} %pad_maximum_fusion.2), channel_id=1, source_target_pairs={{0,6},{1,3},{2,4},{3,1},{4,2},{5,7},{6,0},{7,5},{8,14},{9,11},{10,... | collective-permute-start | bytes 589832 | tf_op jit(solution)/shard_map/ppermute | solution.py:401
  64.7 14.2 %all_to_all.41 = f32[32,8,128]{2,1,0:T(8,128)S(1)} all-to-all(f32[32,8,128]{2,1,0:T(8,128)S(1)} %broadcast_in_dim.11), channel_id=1, replica_groups=mesh['y'=4,'z'=16,'x'=4,'c'=2] {'x','c','y'}, dimensions={0} | all-to-all | bytes 262144 | tf_op jit(solution)/shard_map/all_to_all | solution.py:345
  78.9 0.0 collective-permute-done.1.away
  78.9 0.0 collective-permute-done.3.pair_sibling
  78.9 0.0 collective-permute-done.2.pair
  78.9 0.0 copy-done
  78.9 0.0 copy-done.1
  78.9 0.0 copy-start.2
  78.9 1.4 copy-done.2
  80.3 2.0 %right_away.1 = (f32[4,4,4,32,128]{4,3,2,1,0:T(8,128)S(1)}, bf16[96,384]{1,0:T(8,128)(2,1)S(1)}, bf16[128,96]{1,0:T(8,128)(2,1)S(1)}) custom-call(s32[1]{0:T(128)} %bitcast.place.core_ref, s32[1]{0:T(128)} %bitcast.2.shard_ref, f32[256,128]{1,0:T(8,128)S(1)} %bitcast.28, bf16[8,96,128]{2,1,0:T(8,128)(2,1)S(1)} %all-to-all-done.units, ...), custom_call_target="tpu_custom_call" | custom-call | tf_op jit(solution)/shard_map/right_away/pallas_call | solution.py:199
  82.3 0.0 copy-done.10
  82.3 2.4 %collective-permute-start.4 = (f32[4,4,4,32,128]{4,3,2,1,0:T(8,128)S(1)}, f32[4,4,4,32,128]{4,3,2,1,0:T(8,128)S(1)}, u32[]{:S(2)}, u32[]{:S(2)}) collective-permute-start(f32[4,4,4,32,128]{4,3,2,1,0:T(8,128)S(1)} %get-tuple-element.52), channel_id=1, source_target_pairs={{0,1},{1,0},{2,3},{3,2},{4,5},{5,4},{6,7},{7,6},{8,9},{9,8},{10,11... | collective-permute-start | bytes 3145736 | tf_op jit(solution)/shard_map/ppermute | solution.py:349
  84.7 1.9 %collective-permute-start.5 = (bf16[2,128,2560]{2,1,0:T(8,128)(2,1)}, bf16[2,128,2560]{2,1,0:T(8,128)(2,1)}, u32[]{:S(2)}, u32[]{:S(2)}) collective-permute-start(bf16[2,128,2560]{2,1,0:T(8,128)(2,1)} %get-tuple-element.54), channel_id=1, source_target_pairs={{0,1},{1,0},{2,3},{3,2},{4,5},{5,4},{6,7},{7,6},{8,9},{9,8},{10,11... | collective-permute-start | bytes 3932168 | tf_op jit(solution)/shard_map/ppermute | solution.py:349
  86.7 1.7 right_near.1
  88.3 0.0 collective-permute-done.4
  88.3 1.2 add.64
  89.6 3.7 %all-to-all-start.4 = ((f32[16,4,32,128]{3,2,1,0:T(8,128)}), f32[16,4,32,128]{3,2,1,0:T(8,128)S(1)}, u32[]{:S(2)}, u32[]{:S(2)}) async-start(f32[16,4,32,128]{3,2,1,0:T(8,128)} %bitcast.32), calls=%async_computation.4 | async-start | bytes 2097152 | tf_op jit(solution)/shard_map/all_to_all | solution.py:464
  93.3 0.7 pad_maximum_fusion.3.near
  94.0 3.9 %factors.1 = (f32[3,32,32]{2,1,0:T(8,128)S(1)}, f32[3,32,32]{2,1,0:T(8,128)}) custom-call(s32[1]{0:T(128)} %bitcast.2.shard_ref, f32[256,128]{1,0:T(8,128)S(1)} %bitcast.29), custom_call_target="tpu_custom_call" | custom-call | tf_op jit(solution)/shard_map/factors/pallas_call | solution.py:272
  97.8 0.0 collective-permute-done.5.sibling
  97.8 4.7 %gradients.1 = (f32[3,32,2560]{2,1,0:T(8,128)}, f32[3,32,2560]{2,1,0:T(8,128)}, f32[2,3,32,2560]{3,2,1,0:T(8,128)}) custom-call(bf16[192,512]{1,0:T(8,128)(2,1)} %pad_maximum_fusion.3.near, bf16[192,512]{1,0:T(8,128)(2,1)} %copy-done.10, bf16[2,128,2560]{2,1,0:T(8,128)(2,1)} %get-tuple-element.47.own, bf16[2,128,2560]{2,1,0:T(8,128)(2,1)} %collective-permute-done.5.sibling, ...), custom_call_target="tpu_custom_call" | custom-call | tf_op jit(solution)/shard_map/gradients/pallas_call | solution.py:328
  102.5 6.6 %all-to-all-done.4.received = f32[16,4,32,128]{3,2,1,0:T(8,128)S(1)} async-done(((f32[16,4,32,128]{3,2,1,0:T(8,128)}), f32[16,4,32,128]{3,2,1,0:T(8,128)S(1)}, u32[]{:S(2)}, u32[]{:S(2)}) %all-to-all-start.4) | async-done | bytes 1048608 | tf_op jit(solution)/shard_map/all_to_all | solution.py:464
  109.1 0.2 scaled_sum.1
  109.4 1.9 %collective-permute-start.7 = (f32[2,3,32,2560]{3,2,1,0:T(8,128)}, f32[2,3,32,2560]{3,2,1,0:T(8,128)S(1)}, u32[]{:S(2)}, u32[]{:S(2)}) collective-permute-start(f32[2,3,32,2560]{3,2,1,0:T(8,128)} %get-tuple-element.67), channel_id=1, source_target_pairs={{0,6},{1,3},{2,4},{3,1},{4,2},{5,7},{6,0},{7,5},{8,14},{9,11},{10,... | collective-permute-start | bytes 5898248 | tf_op jit(solution)/shard_map/ppermute | solution.py:401
  111.3 15.9 %all_to_all.42 = f32[16,8,128]{2,1,0:T(8,128)S(1)} all-to-all(f32[16,8,128]{2,1,0:T(8,128)S(1)} %bitcast.31), channel_id=1, replica_groups=mesh['y'=4,'z'=16,'x'=4,'c'=2] {'z'}, dimensions={0} | all-to-all | bytes 131072 | tf_op jit(solution)/shard_map/all_to_all | solution.py:472
  127.2 14.3 %all_to_all.43 = bf16[16,8,128]{2,1,0:T(8,128)(2,1)S(1)} all-to-all(bf16[16,8,128]{2,1,0:T(8,128)(2,1)S(1)} %broadcast_in_dim.12), channel_id=1, replica_groups=mesh['y'=4,'z'=16,'x'=4,'c'=2] {'z'}, dimensions={0} | all-to-all | bytes 65536 | tf_op jit(solution)/shard_map/all_to_all | solution.py:345
  141.5 0.9 broadcast_in_dim.14
  142.4 5.0 %all-to-all-start.7 = ((bf16[16,4,32,128]{3,2,1,0:T(8,128)(2,1)}), bf16[16,4,32,128]{3,2,1,0:T(8,128)(2,1)S(1)}, u32[]{:S(2)}, u32[]{:S(2)}) async-start(bf16[16,4,32,128]{3,2,1,0:T(8,128)(2,1)} %broadcast_in_dim.14), calls=%async_computation.7 | async-start | bytes 1048576 | tf_op jit(solution)/shard_map/all_to_all | solution.py:345
  147.5 0.0 copy-start.5
  147.5 0.0 collective-permute-done.7.far
  147.5 2.3 %fusion = f32[3,32,2560]{2,1,0:T(8,128)} fusion(f32[3,32,2560]{2,1,0:T(8,128)} %get-tuple-element.68, f32[2,3,32,2560]{3,2,1,0:T(8,128)S(1)} %collective-permute-done.7.far), kind=kLoop, calls=%fused_computation.1 | loop fusion | flops 245760 | bytes 2949120 | tf_op jit(solution)/shard_map/add | solution.py:478
  149.7 7.7 %collective-permute-start.8 = (f32[3,32,2560]{2,1,0:T(8,128)}, f32[3,32,2560]{2,1,0:T(8,128)}, u32[]{:S(2)}, u32[]{:S(2)}) collective-permute-start(f32[3,32,2560]{2,1,0:T(8,128)} %fusion), channel_id=1, source_target_pairs={{0,1},{1,0},{2,3},{3,2},{4,5},{5,4},{6,7},{7,6},{8,9},{9,8},{10,11... | collective-permute-start | bytes 2949128 | tf_op jit(solution)/shard_map/ppermute | solution.py:349
  157.5 0.0 all-to-all-done.7
  157.5 7.8 %collective-permute-start.6 = (bf16[4,16,32,128]{3,2,1,0:T(8,128)(2,1)S(1)}, bf16[4,16,32,128]{3,2,1,0:T(8,128)(2,1)S(1)}, u32[]{:S(2)}, u32[]{:S(2)}) collective-permute-start(bf16[4,16,32,128]{3,2,1,0:T(8,128)(2,1)S(1)} %bitcast.26), channel_id=1, source_target_pairs={{0,1},{1,0},{2,3},{3,2},{4,5},{5,4},{6,7},{7,6},{8,9},{9,8},{10,11... | collective-permute-start | bytes 1572872 | tf_op jit(solution)/shard_map/ppermute | solution.py:349
  165.3 1.5 collective-permute-done.6.q_far
  166.8 0.0 collective-permute-done.8.other
  166.8 0.0 copy-done.5
  166.8 1.2 copy-done.3
  168.0 3.0 %new_error.1 = (bf16[3,32,5120]{2,1,0:T(8,128)(2,1)}, bf16[1,3,32,5120]{3,2,1,0:T(8,128)(2,1)}) custom-call(s32[1]{0:T(128)} %bitcast.place.core_ref, bf16[4,16,32,128]{3,2,1,0:T(8,128)(2,1)S(1)} %bitcast.27, bf16[4,16,32,128]{3,2,1,0:T(8,128)(2,1)S(1)} %collective-permute-done.6.q_far, f32[3,32,32]{2,1,0:T(8,128)S(1)} %copy-done.5, ...), custom_call_target="tpu_custom_call" | custom-call | tf_op jit(solution)/shard_map/new_error/pallas_call | solution.py:379
  (12 shorter events, 0.2 us)
Async XLA Ops:
  2.2 16.1 %all-to-all-start = ((bf16[8,96,128]{2,1,0:T(8,128)(2,1)}), bf16[8,96,128]{2,1,0:T(8,128)(2,1)S(1)}, u32[]{:S(2)}, u32[]{:S(2)}) async-start(bf16[8,96,128]{2,1,0:T(8,128)(2,1)} %bitcast_bitcast_fusion), calls=%async_computation | async-start | bytes 393216 | tf_op jit(solution)/shard_map/all_to_all | solution.py:442
  12.4 38.0 %copy-start.7 = (bf16[1024,32]{0,1:T(8,128)(2,1)S(1)}, bf16[1024,32]{0,1:T(8,128)(2,1)}, u32[]{:S(2)}) copy-start(bf16[1024,32]{0,1:T(8,128)(2,1)} %param.9) | copy-start | bytes 196612
  12.4 38.1 %copy-start.8 = (bf16[1024,32]{0,1:T(8,128)(2,1)S(1)}, bf16[1024,32]{0,1:T(8,128)(2,1)}, u32[]{:S(2)}) copy-start(bf16[1024,32]{0,1:T(8,128)(2,1)} %param.11) | copy-start | bytes 196612
  12.4 38.1 %copy-start.9 = (bf16[1024,32]{0,1:T(8,128)(2,1)S(1)}, bf16[1024,32]{0,1:T(8,128)(2,1)}, u32[]{:S(2)}) copy-start(bf16[1024,32]{0,1:T(8,128)(2,1)} %param.10) | copy-start | bytes 196612
  18.3 0.8 copy-start.4
  19.2 0.7 copy-start.6
  32.1 46.8 %collective-permute-start.3 = (bf16[2,128,2560]{2,1,0:T(8,128)(2,1)}, bf16[2,128,2560]{2,1,0:T(8,128)(2,1)}, u32[]{:S(2)}, u32[]{:S(2)}) collective-permute-start(bf16[2,128,2560]{2,1,0:T(8,128)(2,1)} %get-tuple-element.54), channel_id=1, source_target_pairs={{0,7},{1,2},{2,5},{3,0},{4,3},{5,6},{6,1},{7,4},{8,15},{9,10},{10,... | collective-permute-start | bytes 3932168 | tf_op jit(solution)/shard_map/ppermute | solution.py:410
  34.7 44.2 %collective-permute-start.2 = (bf16[2,128,2560]{2,1,0:T(8,128)(2,1)}, bf16[2,128,2560]{2,1,0:T(8,128)(2,1)}, u32[]{:S(2)}, u32[]{:S(2)}) collective-permute-start(bf16[2,128,2560]{2,1,0:T(8,128)(2,1)} %get-tuple-element.47.own), channel_id=1, source_target_pairs={{0,2},{1,7},{2,0},{3,5},{4,6},{5,3},{6,4},{7,1},{8,10},{9,15},{10,... | collective-permute-start | bytes 3932168 | tf_op jit(solution)/shard_map/ppermute | solution.py:401
  37.6 24.6 %all-to-all-start.2 = ((f32[16,8,128]{2,1,0:T(8,128)}), f32[16,8,128]{2,1,0:T(8,128)S(1)}, u32[]{:S(2)}, u32[]{:S(2)}) async-start(f32[16,8,128]{2,1,0:T(8,128)} %broadcast_in_dim.10), calls=%async_computation.2 | async-start | bytes 131072 | tf_op jit(solution)/shard_map/all_to_all | solution.py:451
  50.5 28.4 %copy-start = (bf16[1,3,32,5120]{3,2,1,0:T(8,128)(2,1)S(1)}, bf16[1,3,32,5120]{3,2,1,0:T(8,128)(2,1)}, u32[]{:S(2)}) copy-start(bf16[1,3,32,5120]{3,2,1,0:T(8,128)(2,1)} %error.3) | copy-start | bytes 2949124
  50.5 28.4 %copy-start.1 = (bf16[128,5120]{1,0:T(8,128)(2,1)S(1)}, bf16[128,5120]{1,0:T(8,128)(2,1)}, u32[]{:S(2)}) copy-start(bf16[128,5120]{1,0:T(8,128)(2,1)} %x_ref.3) | copy-start | bytes 3932164
  50.5 11.7 %collective-permute-start = (bf16[96,1024]{1,0:T(8,128)(2,1)S(1)}, bf16[96,1024]{1,0:T(8,128)(2,1)S(1)}, u32[]{:S(2)}, u32[]{:S(2)}) collective-permute-start(bf16[96,1024]{1,0:T(8,128)(2,1)S(1)} %pad_maximum_fusion.1), channel_id=1, source_target_pairs={{0,1},{1,0},{2,3},{3,2},{4,5},{5,4},{6,7},{7,6},{8,9},{9,8},{10,11... | collective-permute-start | bytes 589832 | tf_op jit(solution)/shard_map/ppermute | solution.py:349
  62.5 16.4 %collective-permute-start.1 = (bf16[192,512]{1,0:T(8,128)(2,1)S(1)}, bf16[192,512]{1,0:T(8,128)(2,1)S(1)}, u32[]{:S(2)}, u32[]{:S(2)}) collective-permute-start(bf16[192,512]{1,0:T(8,128)(2,1)S(1)} %pad_maximum_fusion.2), channel_id=1, source_target_pairs={{0,6},{1,3},{2,4},{3,1},{4,2},{5,7},{6,0},{7,5},{8,14},{9,11},{10,... | collective-permute-start | bytes 589832 | tf_op jit(solution)/shard_map/ppermute | solution.py:401
  78.9 3.4 %copy-start.10 = (bf16[192,512]{1,0:T(8,128)(2,1)}, bf16[192,512]{1,0:T(8,128)(2,1)S(1)}, u32[]{:S(2)}) copy-start(bf16[192,512]{1,0:T(8,128)(2,1)S(1)} %collective-permute-done.1.away) | copy-start | bytes 589828
  78.9 1.4 copy-start.2
  82.3 6.0 %collective-permute-start.4 = (f32[4,4,4,32,128]{4,3,2,1,0:T(8,128)S(1)}, f32[4,4,4,32,128]{4,3,2,1,0:T(8,128)S(1)}, u32[]{:S(2)}, u32[]{:S(2)}) collective-permute-start(f32[4,4,4,32,128]{4,3,2,1,0:T(8,128)S(1)} %get-tuple-element.52), channel_id=1, source_target_pairs={{0,1},{1,0},{2,3},{3,2},{4,5},{5,4},{6,7},{7,6},{8,9},{9,8},{10,11... | collective-permute-start | bytes 3145736 | tf_op jit(solution)/shard_map/ppermute | solution.py:349
  84.7 13.1 %collective-permute-start.5 = (bf16[2,128,2560]{2,1,0:T(8,128)(2,1)}, bf16[2,128,2560]{2,1,0:T(8,128)(2,1)}, u32[]{:S(2)}, u32[]{:S(2)}) collective-permute-start(bf16[2,128,2560]{2,1,0:T(8,128)(2,1)} %get-tuple-element.54), channel_id=1, source_target_pairs={{0,1},{1,0},{2,3},{3,2},{4,5},{5,4},{6,7},{7,6},{8,9},{9,8},{10,11... | collective-permute-start | bytes 3932168 | tf_op jit(solution)/shard_map/ppermute | solution.py:349
  89.6 19.5 %all-to-all-start.4 = ((f32[16,4,32,128]{3,2,1,0:T(8,128)}), f32[16,4,32,128]{3,2,1,0:T(8,128)S(1)}, u32[]{:S(2)}, u32[]{:S(2)}) async-start(f32[16,4,32,128]{3,2,1,0:T(8,128)} %bitcast.32), calls=%async_computation.4 | async-start | bytes 2097152 | tf_op jit(solution)/shard_map/all_to_all | solution.py:464
  109.4 38.1 %collective-permute-start.7 = (f32[2,3,32,2560]{3,2,1,0:T(8,128)}, f32[2,3,32,2560]{3,2,1,0:T(8,128)S(1)}, u32[]{:S(2)}, u32[]{:S(2)}) collective-permute-start(f32[2,3,32,2560]{3,2,1,0:T(8,128)} %get-tuple-element.67), channel_id=1, source_target_pairs={{0,6},{1,3},{2,4},{3,1},{4,2},{5,7},{6,0},{7,5},{8,14},{9,11},{10,... | collective-permute-start | bytes 5898248 | tf_op jit(solution)/shard_map/ppermute | solution.py:401
  142.4 15.1 %all-to-all-start.7 = ((bf16[16,4,32,128]{3,2,1,0:T(8,128)(2,1)}), bf16[16,4,32,128]{3,2,1,0:T(8,128)(2,1)S(1)}, u32[]{:S(2)}, u32[]{:S(2)}) async-start(bf16[16,4,32,128]{3,2,1,0:T(8,128)(2,1)} %broadcast_in_dim.14), calls=%async_computation.7 | async-start | bytes 1048576 | tf_op jit(solution)/shard_map/all_to_all | solution.py:345
  147.5 19.3 %copy-start.5 = (f32[3,32,32]{2,1,0:T(8,128)S(1)}, f32[3,32,32]{2,1,0:T(8,128)}, u32[]{:S(2)}) copy-start(f32[3,32,32]{2,1,0:T(8,128)} %get-tuple-element.35.p_factor) | copy-start | bytes 36868
  149.7 17.1 %collective-permute-start.8 = (f32[3,32,2560]{2,1,0:T(8,128)}, f32[3,32,2560]{2,1,0:T(8,128)}, u32[]{:S(2)}, u32[]{:S(2)}) collective-permute-start(f32[3,32,2560]{2,1,0:T(8,128)} %fusion), channel_id=1, source_target_pairs={{0,1},{1,0},{2,3},{3,2},{4,5},{5,4},{6,7},{7,6},{8,9},{9,8},{10,11... | collective-permute-start | bytes 2949128 | tf_op jit(solution)/shard_map/ppermute | solution.py:349
  157.5 9.3 %collective-permute-start.6 = (bf16[4,16,32,128]{3,2,1,0:T(8,128)(2,1)S(1)}, bf16[4,16,32,128]{3,2,1,0:T(8,128)(2,1)S(1)}, u32[]{:S(2)}, u32[]{:S(2)}) collective-permute-start(bf16[4,16,32,128]{3,2,1,0:T(8,128)(2,1)S(1)} %bitcast.26), channel_id=1, source_target_pairs={{0,1},{1,0},{2,3},{3,2},{4,5},{5,4},{6,7},{7,6},{8,9},{9,8},{10,11... | collective-permute-start | bytes 1572872 | tf_op jit(solution)/shard_map/ppermute | solution.py:349
  166.8 1.2 copy-start.3

commit v8 on v7

--- a/solution.py
+++ b/solution.py
@@ -15,7 +15,7 @@
 HALF = D // NC
 PIECE = HALF // NX
 BLOCKS = PIECE // 128
-TOKEN_STEPS = 2
+TOKEN_STEPS = 4
 F32, BF16 = jnp.float32, jnp.bfloat16
 VMEM_BYTES = 24 * 1024 * 1024
 WIDE_VMEM_BYTES = 60 * 1024 * 1024

time: 172 us -> 173 us (level)
  no operation moved by 1% of the time
where the time goes in v8:
time: 173 us; the launch traced here: 172 us
  starting transfers between devices  63.5 us (37%)
  blocking collectives  56.1 us (32%)
  Pallas kernels  20.9 us (12%)
  waiting for transfers between devices  18.4 us (11%)
  other arithmetic  5.98 us (3%)
  local copies, waits for them, and re-layouts  5.85 us (3%)
    all_to_all x2, blocking collectives, spread(): return lax.all_to_all(copies, axis, 0, 0)  28.5 us
    ppermute x5, starting transfers between devices, swap_core(): return lax.ppermute(value, 'c', [(0, 1), (1, 0)])  21.9 us
    all_to_all x1, blocking collectives, per_device(): q_z = lax.all_to_all(q_y.reshape(NZ, 8, 128), 'z', 0, 0).sum(0)  15.9 us
    all_to_all x1, starting transfers between devices, per_device(): p_rows = lax.all_to_all(copies, 'z', 0, 0).sum(0)  13.2 us
    all_to_all x1, blocking collectives, per_device(): lax.all_to_all(p_part.reshape(SHARDS * NY, 8, 128), scatter, 0, 0).sum(0)  11.6 us
    all_to_all x1, starting transfers between devices, per_device(): units = lax.all_to_all(units, tensor, 0, 0)  10.2 us
    all_to_all x1, waiting for transfers between devices, per_device(): p_rows = lax.all_to_all(copies, 'z', 0, 0).sum(0)  9.56 us
    ppermute x3, starting transfers between devices, swap_chip(): return lax.ppermute(value, ('x', 'c'), perm)  6.98 us
  transfers between devices with their start and end apart: 13, of which 4 were waited for; matrix products, arithmetic and copies ran while one was open for 3% of the time, Pallas kernels for 9%

profile of v8, /device:TPU:1, one launch (start us, length us, event | category | flops | bytes accessed | tf_op | source)
XLA Modules:
  0.0 171.7 jit_solution(5502511107669422650)
XLA Ops:
  0.6 1.6 bitcast_bitcast_fusion
  2.2 10.2 %all-to-all-start = ((bf16[8,96,128]{2,1,0:T(8,128)(2,1)}), bf16[8,96,128]{2,1,0:T(8,128)(2,1)S(1)}, u32[]{:S(2)}, u32[]{:S(2)}) async-start(bf16[8,96,128]{2,1,0:T(8,128)(2,1)} %bitcast_bitcast_fusion), calls=%async_computation | async-start | bytes 393216 | tf_op jit(solution)/shard_map/all_to_all | solution.py:442
  12.4 0.0 copy-start.7
  12.4 0.0 copy-start.8
  12.4 0.0 copy-start.9
  12.4 5.2 %token_products.1 = (f32[128,128]{1,0:T(8,128)}, f32[32,128]{1,0:T(8,128)}, bf16[2,128,2560]{2,1,0:T(8,128)(2,1)}, bf16[2,128,2560]{2,1,0:T(8,128)(2,1)}) custom-call(s32[1]{0:T(128)} %bitcast.place.core_ref, bf16[128,5120]{1,0:T(8,128)(2,1)} %x_ref.3, bf16[128,5120]{1,0:T(8,128)(2,1)} %o_ref.3, bf16[1,3,32,5120]{3,2,1,0:T(8,128)(2,1)} %error.3, ...), custom_call_target="tpu_custom_call" | custom-call | tf_op jit(solution)/shard_map/token_products/pallas_call | solution.py:81
  17.6 0.7 all-to-all-done.units
  18.3 0.0 copy-start.4
  18.3 0.8 copy-done.4
  19.2 0.7 copy-done.6
  19.9 0.3 left_product.1
  20.2 11.6 %all_to_all.40 = f32[32,8,128]{2,1,0:T(8,128)S(1)} all-to-all(f32[32,8,128]{2,1,0:T(8,128)S(1)} %bitcast.30), channel_id=1, replica_groups=mesh['y'=4,'z'=16,'x'=4,'c'=2] {'x','c','y'}, dimensions={0} | all-to-all | bytes 262144 | tf_op jit(solution)/shard_map/all_to_all | solution.py:444
  31.9 0.6 broadcast_in_dim.10
  32.5 2.6 %collective-permute-start.3 = (bf16[2,128,2560]{2,1,0:T(8,128)(2,1)}, bf16[2,128,2560]{2,1,0:T(8,128)(2,1)}, u32[]{:S(2)}, u32[]{:S(2)}) collective-permute-start(bf16[2,128,2560]{2,1,0:T(8,128)(2,1)} %get-tuple-element.54), channel_id=1, source_target_pairs={{0,7},{1,2},{2,5},{3,0},{4,3},{5,6},{6,1},{7,4},{8,15},{9,10},{10,... | collective-permute-start | bytes 3932168 | tf_op jit(solution)/shard_map/ppermute | solution.py:410
  35.1 2.9 %collective-permute-start.2 = (bf16[2,128,2560]{2,1,0:T(8,128)(2,1)}, bf16[2,128,2560]{2,1,0:T(8,128)(2,1)}, u32[]{:S(2)}, u32[]{:S(2)}) collective-permute-start(bf16[2,128,2560]{2,1,0:T(8,128)(2,1)} %get-tuple-element.47.own), channel_id=1, source_target_pairs={{0,2},{1,7},{2,0},{3,5},{4,6},{5,3},{6,4},{7,1},{8,10},{9,15},{10,... | collective-permute-start | bytes 3932168 | tf_op jit(solution)/shard_map/ppermute | solution.py:401
  38.0 13.2 %all-to-all-start.2 = ((f32[16,8,128]{2,1,0:T(8,128)}), f32[16,8,128]{2,1,0:T(8,128)S(1)}, u32[]{:S(2)}, u32[]{:S(2)}) async-start(f32[16,8,128]{2,1,0:T(8,128)} %broadcast_in_dim.10), calls=%async_computation.2 | async-start | bytes 131072 | tf_op jit(solution)/shard_map/all_to_all | solution.py:451
  51.1 0.0 copy-done.7
  51.1 0.0 copy-done.8
  51.2 0.0 copy-done.9
  51.2 0.0 copy-start
  51.2 0.0 copy-start.1
  51.2 2.1 %collective-permute-start = (bf16[96,1024]{1,0:T(8,128)(2,1)S(1)}, bf16[96,1024]{1,0:T(8,128)(2,1)S(1)}, u32[]{:S(2)}, u32[]{:S(2)}) collective-permute-start(bf16[96,1024]{1,0:T(8,128)(2,1)S(1)} %pad_maximum_fusion.1), channel_id=1, source_target_pairs={{0,1},{1,0},{2,3},{3,2},{4,5},{5,4},{6,7},{7,6},{8,9},{9,8},{10,11... | collective-permute-start | bytes 589832 | tf_op jit(solution)/shard_map/ppermute | solution.py:349
  53.3 9.6 %all-to-all-done.2 = f32[16,8,128]{2,1,0:T(8,128)S(1)} async-done(((f32[16,8,128]{2,1,0:T(8,128)}), f32[16,8,128]{2,1,0:T(8,128)S(1)}, u32[]{:S(2)}, u32[]{:S(2)}) %all-to-all-start.2) | async-done | bytes 65568 | tf_op jit(solution)/shard_map/all_to_all | solution.py:451
  62.9 0.0 collective-permute-done
  63.0 0.1 constant_dynamic-slice_fusion.3
  63.1 2.2 %collective-permute-start.1 = (bf16[192,512]{1,0:T(8,128)(2,1)S(1)}, bf16[192,512]{1,0:T(8,128)(2,1)S(1)}, u32[]{:S(2)}, u32[]{:S(2)}) collective-permute-start(bf16[192,512]{1,0:T(8,128)(2,1)S(1)} %pad_maximum_fusion.2), channel_id=1, source_target_pairs={{0,6},{1,3},{2,4},{3,1},{4,2},{5,7},{6,0},{7,5},{8,14},{9,11},{10,... | collective-permute-start | bytes 589832 | tf_op jit(solution)/shard_map/ppermute | solution.py:401
  65.3 14.2 %all_to_all.41 = f32[32,8,128]{2,1,0:T(8,128)S(1)} all-to-all(f32[32,8,128]{2,1,0:T(8,128)S(1)} %broadcast_in_dim.11), channel_id=1, replica_groups=mesh['y'=4,'z'=16,'x'=4,'c'=2] {'x','c','y'}, dimensions={0} | all-to-all | bytes 262144 | tf_op jit(solution)/shard_map/all_to_all | solution.py:345
  79.6 0.0 collective-permute-done.1.away
  79.6 0.0 collective-permute-done.3.pair_sibling
  79.6 0.0 collective-permute-done.2.pair
  79.6 0.0 copy-done
  79.6 0.0 copy-done.1
  79.6 0.0 copy-start.2
  79.6 1.4 copy-done.2
  81.0 2.0 %right_away.1 = (f32[4,4,4,32,128]{4,3,2,1,0:T(8,128)S(1)}, bf16[96,384]{1,0:T(8,128)(2,1)S(1)}, bf16[128,96]{1,0:T(8,128)(2,1)S(1)}) custom-call(s32[1]{0:T(128)} %bitcast.place.core_ref, s32[1]{0:T(128)} %bitcast.2.shard_ref, f32[256,128]{1,0:T(8,128)S(1)} %bitcast.28, bf16[8,96,128]{2,1,0:T(8,128)(2,1)S(1)} %all-to-all-done.units, ...), custom_call_target="tpu_custom_call" | custom-call | tf_op jit(solution)/shard_map/right_away/pallas_call | solution.py:199
  83.0 0.0 copy-done.10
  83.0 2.4 %collective-permute-start.4 = (f32[4,4,4,32,128]{4,3,2,1,0:T(8,128)S(1)}, f32[4,4,4,32,128]{4,3,2,1,0:T(8,128)S(1)}, u32[]{:S(2)}, u32[]{:S(2)}) collective-permute-start(f32[4,4,4,32,128]{4,3,2,1,0:T(8,128)S(1)} %get-tuple-element.52), channel_id=1, source_target_pairs={{0,1},{1,0},{2,3},{3,2},{4,5},{5,4},{6,7},{7,6},{8,9},{9,8},{10,11... | collective-permute-start | bytes 3145736 | tf_op jit(solution)/shard_map/ppermute | solution.py:349
  85.4 1.9 %collective-permute-start.5 = (bf16[2,128,2560]{2,1,0:T(8,128)(2,1)}, bf16[2,128,2560]{2,1,0:T(8,128)(2,1)}, u32[]{:S(2)}, u32[]{:S(2)}) collective-permute-start(bf16[2,128,2560]{2,1,0:T(8,128)(2,1)} %get-tuple-element.54), channel_id=1, source_target_pairs={{0,1},{1,0},{2,3},{3,2},{4,5},{5,4},{6,7},{7,6},{8,9},{9,8},{10,11... | collective-permute-start | bytes 3932168 | tf_op jit(solution)/shard_map/ppermute | solution.py:349
  87.3 1.7 right_near.1
  89.0 0.0 collective-permute-done.4
  89.0 1.2 add.64
  90.3 3.7 %all-to-all-start.4 = ((f32[16,4,32,128]{3,2,1,0:T(8,128)}), f32[16,4,32,128]{3,2,1,0:T(8,128)S(1)}, u32[]{:S(2)}, u32[]{:S(2)}) async-start(f32[16,4,32,128]{3,2,1,0:T(8,128)} %bitcast.32), calls=%async_computation.4 | async-start | bytes 2097152 | tf_op jit(solution)/shard_map/all_to_all | solution.py:464
  93.9 0.7 pad_maximum_fusion.3.near
  94.6 3.9 %factors.1 = (f32[3,32,32]{2,1,0:T(8,128)S(1)}, f32[3,32,32]{2,1,0:T(8,128)}) custom-call(s32[1]{0:T(128)} %bitcast.2.shard_ref, f32[256,128]{1,0:T(8,128)S(1)} %bitcast.29), custom_call_target="tpu_custom_call" | custom-call | tf_op jit(solution)/shard_map/factors/pallas_call | solution.py:272
  98.5 0.0 collective-permute-done.5.sibling
  98.5 4.7 %gradients.1 = (f32[3,32,2560]{2,1,0:T(8,128)}, f32[3,32,2560]{2,1,0:T(8,128)}, f32[2,3,32,2560]{3,2,1,0:T(8,128)}) custom-call(bf16[192,512]{1,0:T(8,128)(2,1)} %pad_maximum_fusion.3.near, bf16[192,512]{1,0:T(8,128)(2,1)} %copy-done.10, bf16[2,128,2560]{2,1,0:T(8,128)(2,1)} %get-tuple-element.47.own, bf16[2,128,2560]{2,1,0:T(8,128)(2,1)} %collective-permute-done.5.sibling, ...), custom_call_target="tpu_custom_call" | custom-call | tf_op jit(solution)/shard_map/gradients/pallas_call | solution.py:328
  103.2 6.6 %all-to-all-done.4.received = f32[16,4,32,128]{3,2,1,0:T(8,128)S(1)} async-done(((f32[16,4,32,128]{3,2,1,0:T(8,128)}), f32[16,4,32,128]{3,2,1,0:T(8,128)S(1)}, u32[]{:S(2)}, u32[]{:S(2)}) %all-to-all-start.4) | async-done | bytes 1048608 | tf_op jit(solution)/shard_map/all_to_all | solution.py:464
  109.8 0.2 scaled_sum.1
  110.0 1.9 %collective-permute-start.7 = (f32[2,3,32,2560]{3,2,1,0:T(8,128)}, f32[2,3,32,2560]{3,2,1,0:T(8,128)S(1)}, u32[]{:S(2)}, u32[]{:S(2)}) collective-permute-start(f32[2,3,32,2560]{3,2,1,0:T(8,128)} %get-tuple-element.67), channel_id=1, source_target_pairs={{0,6},{1,3},{2,4},{3,1},{4,2},{5,7},{6,0},{7,5},{8,14},{9,11},{10,... | collective-permute-start | bytes 5898248 | tf_op jit(solution)/shard_map/ppermute | solution.py:401
  111.9 15.9 %all_to_all.42 = f32[16,8,128]{2,1,0:T(8,128)S(1)} all-to-all(f32[16,8,128]{2,1,0:T(8,128)S(1)} %bitcast.31), channel_id=1, replica_groups=mesh['y'=4,'z'=16,'x'=4,'c'=2] {'z'}, dimensions={0} | all-to-all | bytes 131072 | tf_op jit(solution)/shard_map/all_to_all | solution.py:472
  127.9 14.3 %all_to_all.43 = bf16[16,8,128]{2,1,0:T(8,128)(2,1)S(1)} all-to-all(bf16[16,8,128]{2,1,0:T(8,128)(2,1)S(1)} %broadcast_in_dim.12), channel_id=1, replica_groups=mesh['y'=4,'z'=16,'x'=4,'c'=2] {'z'}, dimensions={0} | all-to-all | bytes 65536 | tf_op jit(solution)/shard_map/all_to_all | solution.py:345
  142.2 0.9 broadcast_in_dim.14
  143.1 5.0 %all-to-all-start.7 = ((bf16[16,4,32,128]{3,2,1,0:T(8,128)(2,1)}), bf16[16,4,32,128]{3,2,1,0:T(8,128)(2,1)S(1)}, u32[]{:S(2)}, u32[]{:S(2)}) async-start(bf16[16,4,32,128]{3,2,1,0:T(8,128)(2,1)} %broadcast_in_dim.14), calls=%async_computation.7 | async-start | bytes 1048576 | tf_op jit(solution)/shard_map/all_to_all | solution.py:345
  148.1 0.0 copy-start.5
  148.1 0.0 collective-permute-done.7.far
  148.2 2.3 %fusion = f32[3,32,2560]{2,1,0:T(8,128)} fusion(f32[3,32,2560]{2,1,0:T(8,128)} %get-tuple-element.68, f32[2,3,32,2560]{3,2,1,0:T(8,128)S(1)} %collective-permute-done.7.far), kind=kLoop, calls=%fused_computation.1 | loop fusion | flops 245760 | bytes 2949120 | tf_op jit(solution)/shard_map/add | solution.py:478
  150.4 7.7 %collective-permute-start.8 = (f32[3,32,2560]{2,1,0:T(8,128)}, f32[3,32,2560]{2,1,0:T(8,128)}, u32[]{:S(2)}, u32[]{:S(2)}) collective-permute-start(f32[3,32,2560]{2,1,0:T(8,128)} %fusion), channel_id=1, source_target_pairs={{0,1},{1,0},{2,3},{3,2},{4,5},{5,4},{6,7},{7,6},{8,9},{9,8},{10,11... | collective-permute-start | bytes 2949128 | tf_op jit(solution)/shard_map/ppermute | solution.py:349
  158.1 0.0 all-to-all-done.7
  158.2 7.8 %collective-permute-start.6 = (bf16[4,16,32,128]{3,2,1,0:T(8,128)(2,1)S(1)}, bf16[4,16,32,128]{3,2,1,0:T(8,128)(2,1)S(1)}, u32[]{:S(2)}, u32[]{:S(2)}) collective-permute-start(bf16[4,16,32,128]{3,2,1,0:T(8,128)(2,1)S(1)} %bitcast.26), channel_id=1, source_target_pairs={{0,1},{1,0},{2,3},{3,2},{4,5},{5,4},{6,7},{7,6},{8,9},{9,8},{10,11... | collective-permute-start | bytes 1572872 | tf_op jit(solution)/shard_map/ppermute | solution.py:349
  166.0 1.5 collective-permute-done.6.q_far
  167.5 0.0 collective-permute-done.8.other
  167.5 0.0 copy-done.5
  167.5 1.2 copy-done.3
  168.7 3.0 %new_error.1 = (bf16[3,32,5120]{2,1,0:T(8,128)(2,1)}, bf16[1,3,32,5120]{3,2,1,0:T(8,128)(2,1)}) custom-call(s32[1]{0:T(128)} %bitcast.place.core_ref, bf16[4,16,32,128]{3,2,1,0:T(8,128)(2,1)S(1)} %bitcast.27, bf16[4,16,32,128]{3,2,1,0:T(8,128)(2,1)S(1)} %collective-permute-done.6.q_far, f32[3,32,32]{2,1,0:T(8,128)S(1)} %copy-done.5, ...), custom_call_target="tpu_custom_call" | custom-call | tf_op jit(solution)/shard_map/new_error/pallas_call | solution.py:379
  (12 shorter events, 0.2 us)
Async XLA Ops:
  2.2 16.1 %all-to-all-start = ((bf16[8,96,128]{2,1,0:T(8,128)(2,1)}), bf16[8,96,128]{2,1,0:T(8,128)(2,1)S(1)}, u32[]{:S(2)}, u32[]{:S(2)}) async-start(bf16[8,96,128]{2,1,0:T(8,128)(2,1)} %bitcast_bitcast_fusion), calls=%async_computation | async-start | bytes 393216 | tf_op jit(solution)/shard_map/all_to_all | solution.py:442
  12.4 38.7 %copy-start.7 = (bf16[1024,32]{0,1:T(8,128)(2,1)S(1)}, bf16[1024,32]{0,1:T(8,128)(2,1)}, u32[]{:S(2)}) copy-start(bf16[1024,32]{0,1:T(8,128)(2,1)} %param.9) | copy-start | bytes 196612
  12.4 38.7 %copy-start.8 = (bf16[1024,32]{0,1:T(8,128)(2,1)S(1)}, bf16[1024,32]{0,1:T(8,128)(2,1)}, u32[]{:S(2)}) copy-start(bf16[1024,32]{0,1:T(8,128)(2,1)} %param.11) | copy-start | bytes 196612
  12.4 38.7 %copy-start.9 = (bf16[1024,32]{0,1:T(8,128)(2,1)S(1)}, bf16[1024,32]{0,1:T(8,128)(2,1)}, u32[]{:S(2)}) copy-start(bf16[1024,32]{0,1:T(8,128)(2,1)} %param.10) | copy-start | bytes 196612
  18.3 0.8 copy-start.4
  19.2 0.7 copy-start.6
  32.5 47.1 %collective-permute-start.3 = (bf16[2,128,2560]{2,1,0:T(8,128)(2,1)}, bf16[2,128,2560]{2,1,0:T(8,128)(2,1)}, u32[]{:S(2)}, u32[]{:S(2)}) collective-permute-start(bf16[2,128,2560]{2,1,0:T(8,128)(2,1)} %get-tuple-element.54), channel_id=1, source_target_pairs={{0,7},{1,2},{2,5},{3,0},{4,3},{5,6},{6,1},{7,4},{8,15},{9,10},{10,... | collective-permute-start | bytes 3932168 | tf_op jit(solution)/shard_map/ppermute | solution.py:410
  35.1 44.5 %collective-permute-start.2 = (bf16[2,128,2560]{2,1,0:T(8,128)(2,1)}, bf16[2,128,2560]{2,1,0:T(8,128)(2,1)}, u32[]{:S(2)}, u32[]{:S(2)}) collective-permute-start(bf16[2,128,2560]{2,1,0:T(8,128)(2,1)} %get-tuple-element.47.own), channel_id=1, source_target_pairs={{0,2},{1,7},{2,0},{3,5},{4,6},{5,3},{6,4},{7,1},{8,10},{9,15},{10,... | collective-permute-start | bytes 3932168 | tf_op jit(solution)/shard_map/ppermute | solution.py:401
  38.0 24.9 %all-to-all-start.2 = ((f32[16,8,128]{2,1,0:T(8,128)}), f32[16,8,128]{2,1,0:T(8,128)S(1)}, u32[]{:S(2)}, u32[]{:S(2)}) async-start(f32[16,8,128]{2,1,0:T(8,128)} %broadcast_in_dim.10), calls=%async_computation.2 | async-start | bytes 131072 | tf_op jit(solution)/shard_map/all_to_all | solution.py:451
  51.2 28.4 %copy-start = (bf16[1,3,32,5120]{3,2,1,0:T(8,128)(2,1)S(1)}, bf16[1,3,32,5120]{3,2,1,0:T(8,128)(2,1)}, u32[]{:S(2)}) copy-start(bf16[1,3,32,5120]{3,2,1,0:T(8,128)(2,1)} %error.3) | copy-start | bytes 2949124
  51.2 28.4 %copy-start.1 = (bf16[128,5120]{1,0:T(8,128)(2,1)S(1)}, bf16[128,5120]{1,0:T(8,128)(2,1)}, u32[]{:S(2)}) copy-start(bf16[128,5120]{1,0:T(8,128)(2,1)} %x_ref.3) | copy-start | bytes 3932164
  51.2 11.7 %collective-permute-start = (bf16[96,1024]{1,0:T(8,128)(2,1)S(1)}, bf16[96,1024]{1,0:T(8,128)(2,1)S(1)}, u32[]{:S(2)}, u32[]{:S(2)}) collective-permute-start(bf16[96,1024]{1,0:T(8,128)(2,1)S(1)} %pad_maximum_fusion.1), channel_id=1, source_target_pairs={{0,1},{1,0},{2,3},{3,2},{4,5},{5,4},{6,7},{7,6},{8,9},{9,8},{10,11... | collective-permute-start | bytes 589832 | tf_op jit(solution)/shard_map/ppermute | solution.py:349
  63.1 16.4 %collective-permute-start.1 = (bf16[192,512]{1,0:T(8,128)(2,1)S(1)}, bf16[192,512]{1,0:T(8,128)(2,1)S(1)}, u32[]{:S(2)}, u32[]{:S(2)}) collective-permute-start(bf16[192,512]{1,0:T(8,128)(2,1)S(1)} %pad_maximum_fusion.2), channel_id=1, source_target_pairs={{0,6},{1,3},{2,4},{3,1},{4,2},{5,7},{6,0},{7,5},{8,14},{9,11},{10,... | collective-permute-start | bytes 589832 | tf_op jit(solution)/shard_map/ppermute | solution.py:401
  79.6 3.4 %copy-start.10 = (bf16[192,512]{1,0:T(8,128)(2,1)}, bf16[192,512]{1,0:T(8,128)(2,1)S(1)}, u32[]{:S(2)}) copy-start(bf16[192,512]{1,0:T(8,128)(2,1)S(1)} %collective-permute-done.1.away) | copy-start | bytes 589828
  79.6 1.4 copy-start.2
  83.0 6.0 %collective-permute-start.4 = (f32[4,4,4,32,128]{4,3,2,1,0:T(8,128)S(1)}, f32[4,4,4,32,128]{4,3,2,1,0:T(8,128)S(1)}, u32[]{:S(2)}, u32[]{:S(2)}) collective-permute-start(f32[4,4,4,32,128]{4,3,2,1,0:T(8,128)S(1)} %get-tuple-element.52), channel_id=1, source_target_pairs={{0,1},{1,0},{2,3},{3,2},{4,5},{5,4},{6,7},{7,6},{8,9},{9,8},{10,11... | collective-permute-start | bytes 3145736 | tf_op jit(solution)/shard_map/ppermute | solution.py:349
  85.4 13.1 %collective-permute-start.5 = (bf16[2,128,2560]{2,1,0:T(8,128)(2,1)}, bf16[2,128,2560]{2,1,0:T(8,128)(2,1)}, u32[]{:S(2)}, u32[]{:S(2)}) collective-permute-start(bf16[2,128,2560]{2,1,0:T(8,128)(2,1)} %get-tuple-element.54), channel_id=1, source_target_pairs={{0,1},{1,0},{2,3},{3,2},{4,5},{5,4},{6,7},{7,6},{8,9},{9,8},{10,11... | collective-permute-start | bytes 3932168 | tf_op jit(solution)/shard_map/ppermute | solution.py:349
  90.3 19.5 %all-to-all-start.4 = ((f32[16,4,32,128]{3,2,1,0:T(8,128)}), f32[16,4,32,128]{3,2,1,0:T(8,128)S(1)}, u32[]{:S(2)}, u32[]{:S(2)}) async-start(f32[16,4,32,128]{3,2,1,0:T(8,128)} %bitcast.32), calls=%async_computation.4 | async-start | bytes 2097152 | tf_op jit(solution)/shard_map/all_to_all | solution.py:464
  110.0 38.1 %collective-permute-start.7 = (f32[2,3,32,2560]{3,2,1,0:T(8,128)}, f32[2,3,32,2560]{3,2,1,0:T(8,128)S(1)}, u32[]{:S(2)}, u32[]{:S(2)}) collective-permute-start(f32[2,3,32,2560]{3,2,1,0:T(8,128)} %get-tuple-element.67), channel_id=1, source_target_pairs={{0,6},{1,3},{2,4},{3,1},{4,2},{5,7},{6,0},{7,5},{8,14},{9,11},{10,... | collective-permute-start | bytes 5898248 | tf_op jit(solution)/shard_map/ppermute | solution.py:401
  143.1 15.1 %all-to-all-start.7 = ((bf16[16,4,32,128]{3,2,1,0:T(8,128)(2,1)}), bf16[16,4,32,128]{3,2,1,0:T(8,128)(2,1)S(1)}, u32[]{:S(2)}, u32[]{:S(2)}) async-start(bf16[16,4,32,128]{3,2,1,0:T(8,128)(2,1)} %broadcast_in_dim.14), calls=%async_computation.7 | async-start | bytes 1048576 | tf_op jit(solution)/shard_map/all_to_all | solution.py:345
  148.1 19.4 %copy-start.5 = (f32[3,32,32]{2,1,0:T(8,128)S(1)}, f32[3,32,32]{2,1,0:T(8,128)}, u32[]{:S(2)}) copy-start(f32[3,32,32]{2,1,0:T(8,128)} %get-tuple-element.35.p_factor) | copy-start | bytes 36868
  150.4 17.1 %collective-permute-start.8 = (f32[3,32,2560]{2,1,0:T(8,128)}, f32[3,32,2560]{2,1,0:T(8,128)}, u32[]{:S(2)}, u32[]{:S(2)}) collective-permute-start(f32[3,32,2560]{2,1,0:T(8,128)} %fusion), channel_id=1, source_target_pairs={{0,1},{1,0},{2,3},{3,2},{4,5},{5,4},{6,7},{7,6},{8,9},{9,8},{10,11... | collective-permute-start | bytes 2949128 | tf_op jit(solution)/shard_map/ppermute | solution.py:349
  158.2 9.3 %collective-permute-start.6 = (bf16[4,16,32,128]{3,2,1,0:T(8,128)(2,1)S(1)}, bf16[4,16,32,128]{3,2,1,0:T(8,128)(2,1)S(1)}, u32[]{:S(2)}, u32[]{:S(2)}) collective-permute-start(bf16[4,16,32,128]{3,2,1,0:T(8,128)(2,1)S(1)} %bitcast.26), channel_id=1, source_target_pairs={{0,1},{1,0},{2,3},{3,2},{4,5},{5,4},{6,7},{7,6},{8,9},{9,8},{10,11... | collective-permute-start | bytes 1572872 | tf_op jit(solution)/shard_map/ppermute | solution.py:349
  167.5 1.2 copy-start.3
